TPU v7x, 512 devices: a whole 4x8x8 slice. The times are simulated.
512 devices in a mesh: fsdp: 32 (over y_lo, z), expert: 16 (over x, y_hi, core).
Axes of the slice: x: 4, y: 8 (y_hi: 2, y_lo: 4; y = y_hi * 4 + y_lo), z: 8, core: 2. Of those that a mesh axis runs over, the one named last changes fastest.
Arguments:
- tokens: bfloat16 [4096, 1792], P('expert', 'fsdp'), may hold values from -6 to 6
- modulation: float32 [4, 3, 1792], replicated, may hold values from -4 to 4
- routes: int32 [4096, 2], P('expert'), may hold values from 0 to 15, all different within a row
- route_weights: float32 [4096, 2], P('expert'), may hold values from 0.2 to 1
- w_first: bfloat16 [16, 1792, 7168], P('expert', None, 'fsdp'), may hold values from -0.125 to 0.125
- w_second: bfloat16 [16, 7168, 1792], P('expert', 'fsdp'), may hold values from -0.0625 to 0.0625
- head: bfloat16 [16, 1792], P(None, 'fsdp'), may hold values from -0.125 to 0.125
- targets: float32 [4096, 16], P('expert'), may hold values from -6 to 6
- ref_err: float32 [4], replicated, may hold values from 1.5 to 4
- pair_ids: int32 [4], replicated, may hold values from 0 to 3, each once
- timesteps: int32 [2], replicated, may hold values from 0 to 999
Outputs:
- grad_tokens: bfloat16 [4096, 1792], P('expert', 'fsdp')
- loss: float32 [], replicated
Inputs may be any that keep to these rules, and one draw needn't show every extreme that they name: `routes`: each row names 2 different experts. `pair_ids`: each image once.
All inputs are finite; a program needn't handle non-finite values.
Results may differ from a plain program's by a relative error of at most 0.03.
Values may be sent and summed in bfloat16 or wider, within the bound.
No kernel may reach another device: no remote copies, remote signals or barrier semaphores. Data moves between devices by JAX's collectives and lax.ppermute only.
A program may use at most 64 MiB of HBM per device.

v0:
```python
import math

import jax
import jax.numpy as jnp
from jax import lax
from jax.sharding import PartitionSpec as P

D = 1792
TOPK = 2
C_OUT = 16
SAMPLES = 4


norm_eps = 1e-06
dpo_beta = 2.0


def gelu_tanh(values):
    return jax.nn.gelu(values, approximate=True)


def gelu_backward(pre_act, upstream):
    return jax.vjp(gelu_tanh, pre_act)[1](upstream)[0]


def dpo_terms(sample_err, ref_err, pair_ids, timesteps):
    count = sample_err.shape[0]
    sample_ids = jnp.arange(count, dtype=jnp.int32)
    winners = pair_ids[0::2]
    losers = pair_ids[1::2]
    win_sel = (winners[:, None] == sample_ids[None, :]).astype(jnp.float32)
    lose_sel = (losers[:, None] == sample_ids[None, :]).astype(jnp.float32)
    excess = sample_err - ref_err
    margin = jnp.sum(win_sel * excess[None, :], axis=1) - jnp.sum(
        lose_sel * excess[None, :], axis=1
    )
    fraction = timesteps.astype(jnp.float32) / 1000.0
    keep_level = jnp.cos((fraction + 0.008) / 1.008 * (math.pi / 2.0)) ** 2
    strength = dpo_beta * keep_level
    inside = -strength * margin
    loss = jnp.mean(jax.nn.softplus(-inside))
    slope = -jax.nn.sigmoid(-inside) / inside.shape[0]
    coef = jnp.sum(
        win_sel * (-slope * strength)[:, None] + lose_sel * (slope * strength)[:, None], axis=0
    )
    return (loss, coef)


def local_slots(routes, num_experts):
    flat_routes = routes.reshape(-1)
    expert_ids = jnp.arange(num_experts, dtype=jnp.int32)
    hits = (flat_routes[:, None] == expert_ids[None, :]).astype(jnp.int32)
    earlier = jnp.cumsum(hits, axis=0) - hits
    return jnp.sum(earlier * hits, axis=1).reshape(routes.shape)


def local(
    tokens,
    modulation,
    routes,
    route_weights,
    w_first,
    w_second,
    head,
    targets,
    ref_err,
    pair_ids,
    timesteps,
):
    highest = lax.Precision.HIGHEST
    contract_rows = (((0,), (0,)), ((), ()))
    contract_last = (((1,), (1,)), ((), ()))
    tok_rows, feat_dev = tokens.shape
    group_count = lax.axis_size("expert")
    num_experts = group_count * w_first.shape[0]
    capacity = TOPK * tok_rows // num_experts
    slot_total = group_count * capacity
    tokens_all = tok_rows * group_count
    tok_sample = tokens_all // SAMPLES
    feat_start = lax.axis_index("fsdp") * feat_dev
    row_ids = lax.axis_index("expert") * tok_rows + jnp.arange(tok_rows, dtype=jnp.int32)
    sample_sel = (
        (row_ids // tok_sample)[:, None] == jnp.arange(SAMPLES, dtype=jnp.int32)[None, :]
    ).astype(jnp.float32)
    mod_local = lax.dynamic_slice_in_dim(modulation, feat_start, feat_dev, 2)
    row_mod = jnp.einsum("ts,scd->tcd", sample_sel, mod_local, precision=highest)
    shift_rows = row_mod[:, 0]
    scale_rows = row_mod[:, 1]
    gate_rows = row_mod[:, 2]
    tok_float = tokens.astype(jnp.float32)
    slots = local_slots(routes, num_experts)
    kept = slots < capacity
    dest = routes * capacity + slots
    slot_ids = jnp.arange(num_experts * capacity, dtype=jnp.int32)
    place = ((dest[:, :, None] == slot_ids[None, None, :]) & kept[:, :, None]).astype(jnp.float32)
    pick = jnp.sum(place, axis=1)
    weighted = jnp.sum(place * route_weights[:, :, None], axis=1)
    w_in_local = w_first[0]
    w_out_local = w_second[0]
    row_squares = lax.psum(jnp.sum(tok_float * tok_float, axis=1), "fsdp")
    rms_scale = lax.rsqrt(row_squares / D + norm_eps)
    normed = (tok_float * rms_scale[:, None] * (1.0 + scale_rows) + shift_rows).astype(jnp.bfloat16)
    outgoing = lax.dot_general(
        pick.astype(jnp.bfloat16), normed, contract_rows, preferred_element_type=jnp.float32
    ).astype(jnp.bfloat16)
    arrived = lax.all_to_all(
        outgoing.reshape(num_experts, capacity, feat_dev),
        "expert",
        split_axis=0,
        concat_axis=0,
        tiled=True,
    )
    pre_act = jnp.dot(
        lax.all_gather(arrived.reshape(slot_total, feat_dev), "fsdp", axis=1, tiled=True),
        w_in_local,
        preferred_element_type=jnp.float32,
    )
    activation = gelu_tanh(pre_act).astype(jnp.bfloat16)
    partial_out = jnp.dot(activation, w_out_local, preferred_element_type=jnp.float32)
    partial_out = partial_out.reshape(group_count, capacity, partial_out.shape[1])
    summed = lax.psum_scatter(
        partial_out.astype(jnp.bfloat16), "fsdp", scatter_dimension=2, tiled=True
    )
    returned = lax.all_to_all(summed, "expert", split_axis=0, concat_axis=0, tiled=True)
    moe_out = jnp.dot(
        weighted,
        returned.reshape(num_experts * capacity, feat_dev).astype(jnp.float32),
        precision=highest,
    )
    block_out = (tok_float + gate_rows * moe_out).astype(jnp.bfloat16)
    pred_part = lax.dot_general(block_out, head, contract_last, preferred_element_type=jnp.float32)
    prediction = lax.psum(pred_part, "fsdp")
    residue = prediction - targets
    token_err = jnp.sum(residue * residue, axis=1)
    err_part = jnp.sum(sample_sel * token_err[:, None], axis=0) / (tok_sample * C_OUT)
    sample_err = lax.psum(err_part, "expert")
    loss, coef = dpo_terms(sample_err, ref_err, pair_ids, timesteps)
    row_coef = jnp.sum(sample_sel * coef[None, :], axis=1)
    grad_pred = tokens_all * C_OUT * row_coef[:, None] * 2.0 * residue / (tok_sample * C_OUT)
    grad_block = jnp.dot(grad_pred, head.astype(jnp.float32), precision=highest)
    grad_moe = gate_rows * grad_block
    grad_out = lax.dot_general(weighted, grad_moe, contract_rows, precision=highest).astype(
        jnp.bfloat16
    )
    grad_arrived = lax.all_to_all(
        grad_out.reshape(num_experts, capacity, feat_dev),
        "expert",
        split_axis=0,
        concat_axis=0,
        tiled=True,
    )
    grad_act = lax.dot_general(
        lax.all_gather(grad_arrived.reshape(slot_total, feat_dev), "fsdp", axis=1, tiled=True),
        w_out_local,
        contract_last,
        preferred_element_type=jnp.float32,
    )
    grad_pre = gelu_backward(pre_act, grad_act).astype(jnp.bfloat16)
    grad_part = lax.dot_general(
        grad_pre, w_in_local, contract_last, preferred_element_type=jnp.float32
    )
    grad_part = grad_part.reshape(group_count, capacity, grad_part.shape[1])
    grad_summed = lax.psum_scatter(
        grad_part.astype(jnp.bfloat16), "fsdp", scatter_dimension=2, tiled=True
    )
    grad_home = lax.all_to_all(grad_summed, "expert", split_axis=0, concat_axis=0, tiled=True)
    grad_normed = jnp.dot(
        pick,
        grad_home.reshape(num_experts * capacity, feat_dev).astype(jnp.float32),
        precision=highest,
    )
    scaled_grad = grad_normed * (1.0 + scale_rows)
    normed_base = tok_float * rms_scale[:, None]
    row_dot = lax.psum(jnp.sum(scaled_grad * normed_base, axis=1), "fsdp")
    grad_norm = rms_scale[:, None] * (scaled_grad - normed_base * (row_dot / D)[:, None])
    grad_tokens = (grad_block + grad_norm).astype(jnp.bfloat16)
    return (grad_tokens, loss)


def solution(mesh):
    in_specs = (
        P("expert", "fsdp"),
        P(),
        P("expert", None),
        P("expert", None),
        P("expert", None, "fsdp"),
        P("expert", "fsdp", None),
        P(None, "fsdp"),
        P("expert", None),
        P(),
        P(),
        P(),
    )
    out_specs = (P("expert", "fsdp"), P())
    return jax.shard_map(local, mesh=mesh, in_specs=in_specs, out_specs=out_specs, check_vma=False)
```

profile of v0, /device:TPU:1, one launch (start us, length us, event | category | flops | bytes accessed | tf_op | source)
XLA Modules:
  0.0 1091.4 jit_solution(2711835638781519814)
XLA Ops:
  7.2 0.9 copy.53
  8.4 1.2 reduce-window.6
  10.9 0.8 fusion.29
  11.6 73.2 %psum.28 = f32[256]{0:T(256)S(1)} all-reduce(f32[256]{0:T(256)S(1)} %fusion.29), channel_id=1, replica_groups=mesh['fsdp'=32,'expert'=16] {'fsdp'}, use_global_device_ids=true, to_apply=%region_6.7 | all-reduce | flops 256 | bytes 2048 | tf_op jit(solution)/shard_map/psum | solution.py:100
  84.8 1.9 convert_reduce_fusion
  86.8 1.1 fusion.44
  89.0 31.1 %all_to_all.20 = bf16[16,2,896]{2,1,0:T(2,128)(2,1)S(1)} all-to-all(bf16[16,2,896]{2,1,0:T(2,128)(2,1)S(1)} %reshape.103), channel_id=1, replica_groups=mesh['fsdp'=32,'expert'=16] {'expert'}, dimensions={0} | all-to-all | bytes 114688 | tf_op jit(solution)/shard_map/all_to_all | solution.py:106
  120.3 0.7 copy.59
  121.1 123.5 %all-gather.3.cloned.1.call-done = bf16[512,1792]{0,1:T(8,128)(2,1)} async-done(((bf16[512,56]{0,1:T(8,128)(2,1)}), bf16[512,1792]{0,1:T(8,128)(2,1)}) %all-gather.3.cloned.1.call-update) | async-done | bytes 1835024 | tf_op jit(solution)/shard_map/all_gather | solution.py:114
  244.7 2.9 multiply_convert_fusion
  247.7 1.8 convolution_convert_fusion.1
  249.4 7.6 copy.64
  257.0 10.7 reshape.98
  267.8 156.1 %reduce-scatter.7.cloned.1.call-done = bf16[56,512]{1,0:T(8,128)(2,1)} async-done(((bf16[1792,512]{1,0:T(8,128)(2,1)}), bf16[56,512]{1,0:T(8,128)(2,1)}) %reduce-scatter.7.cloned.1.call-update) | async-done | bytes 57360
  423.9 1.0 reshape.99
  425.2 0.8 reshape.105
  426.0 30.9 %all-to-all-start.1 = ((bf16[16,2,896]{2,1,0:T(2,128)(2,1)}), bf16[16,2,896]{2,1,0:T(2,128)(2,1)S(1)}, u32[]{:S(2)}, u32[]{:S(2)}) async-start(bf16[16,2,896]{2,1,0:T(2,128)(2,1)} %reshape.105), calls=%async_computation.1 | async-start | bytes 114688 | tf_op jit(solution)/shard_map/all_to_all | solution.py:124
  457.0 9.6 all-to-all-done.1
  467.4 121.2 %psum.29 = f32[256,16]{0,1:T(8,128)S(1)} all-reduce(f32[256,16]{0,1:T(8,128)S(1)} %fusion.53), channel_id=1, replica_groups=mesh['fsdp'=32,'expert'=16] {'fsdp'}, use_global_device_ids=true, to_apply=%region_8.9 | all-reduce | flops 4096 | bytes 32768 | tf_op jit(solution)/shard_map/psum | solution.py:132
  588.9 70.6 %psum.30 = f32[4]{0:T(128)S(1)} all-reduce(f32[4]{0:T(128)S(1)} %broadcast_multiply_fusion.2), channel_id=1, replica_groups=mesh['fsdp'=32,'expert'=16] {'expert'}, use_global_device_ids=true, to_apply=%region_11.12 | all-reduce | flops 4 | bytes 32 | tf_op jit(solution)/shard_map/psum | solution.py:136
  661.6 12.8 %all_to_all.21 = bf16[16,2,896]{2,1,0:T(2,128)(2,1)S(1)} all-to-all(bf16[16,2,896]{2,1,0:T(2,128)(2,1)S(1)} %reshape.107), channel_id=1, replica_groups=mesh['fsdp'=32,'expert'=16] {'expert'}, dimensions={0} | all-to-all | bytes 114688 | tf_op jit(solution)/shard_map/all_to_all | solution.py:145
  675.7 123.3 %all-gather.5.cloned.1.call-done = bf16[512,1792]{0,1:T(8,128)(2,1)} async-done(((bf16[512,56]{0,1:T(8,128)(2,1)}), bf16[512,1792]{0,1:T(8,128)(2,1)}) %all-gather.5.cloned.1.call-update) | async-done | bytes 1835024 | tf_op jit(solution)/shard_map/all_gather | solution.py:153
  799.0 2.3 fusion.15
  802.1 7.6 copy.66
  809.7 10.7 reshape.100
  820.4 156.3 %reduce-scatter.9.cloned.1.call-done = bf16[56,512]{1,0:T(8,128)(2,1)} async-done(((bf16[1792,512]{1,0:T(8,128)(2,1)}), bf16[56,512]{1,0:T(8,128)(2,1)}) %reduce-scatter.9.cloned.1.call-update) | async-done | bytes 57360
  976.7 1.0 reshape.101
  978.0 0.8 reshape.109
  978.8 30.8 %all-to-all-start.3 = ((bf16[16,2,896]{2,1,0:T(2,128)(2,1)}), bf16[16,2,896]{2,1,0:T(2,128)(2,1)S(1)}, u32[]{:S(2)}, u32[]{:S(2)}) async-start(bf16[16,2,896]{2,1,0:T(2,128)(2,1)} %reshape.109), calls=%async_computation.3 | async-start | bytes 114688 | tf_op jit(solution)/shard_map/all_to_all | solution.py:166
  1010.2 9.1 all-to-all-done.3
  1019.5 1.2 fusion.24
  1020.8 62.4 %psum.31 = f32[256]{0:T(256)S(1)} all-reduce(f32[256]{0:T(256)S(1)} %get-tuple-element.15), channel_id=1, replica_groups=mesh['fsdp'=32,'expert'=16] {'fsdp'}, use_global_device_ids=true, to_apply=%region_18.19 | all-reduce | flops 256 | bytes 2048 | tf_op jit(solution)/shard_map/psum | solution.py:174
  (77 shorter events, 9.8 us)
Async XLA Ops:
  7.2 237.5 %copy-start = (bf16[1,1792,224]{1,2,0:T(8,128)(2,1)S(1)}, bf16[1,1792,224]{1,2,0:T(8,128)(2,1)}, u32[]{:S(2)}) copy-start(bf16[1,1792,224]{1,2,0:T(8,128)(2,1)} %param.15) | copy-start | bytes 2408452
  7.2 81.3 %copy-start.5 = (bf16[256,56]{0,1:T(8,128)(2,1)S(1)}, bf16[256,56]{0,1:T(8,128)(2,1)}, u32[]{:S(2)}) copy-start(bf16[256,56]{0,1:T(8,128)(2,1)} %param.11) | copy-start | bytes 86020
  7.2 237.5 %all-gather.3.cloned.1.call-start = ((), (), s32[]{:S(2)}) async-start(), calls=%async_computation.6 | async-start | bytes 1892352 | tf_op jit(solution)/shard_map/all_gather | solution.py:114
  87.8 0.7 copy-start.2
  121.1 302.8 %reduce-scatter.7.cloned.1.call-start = ((), (), s32[]{:S(2)}) async-start(), calls=%async_computation.8 | async-start | bytes 1892352
  267.7 189.3 %copy-start.9 = (s32[4]{0:T(128)S(1)}, s32[4]{0:T(128)}, u32[]{:S(2)}) copy-start(s32[4]{0:T(128)} %param.20) | copy-start | bytes 52
  267.7 199.2 %copy-start.1 = (f32[256,512]{1,0:T(8,128)S(1)}, f32[256,512]{1,0:T(8,128)}, u32[]{:S(2)}) copy-start(f32[256,512]{1,0:T(8,128)} %get-tuple-element.3) | copy-start | bytes 1572868
  267.7 199.2 %copy-start.3 = (f32[256,3,56]{0,2,1:T(8,128)S(1)}, f32[256,3,56]{0,2,1:T(8,128)}, u32[]{:S(2)}) copy-start(f32[256,3,56]{0,2,1:T(8,128)} %copy-done.2) | copy-start | bytes 516100
  267.7 199.6 %copy-start.7 = (bf16[16,56]{1,0:T(8,128)(2,1)S(1)}, bf16[16,56]{1,0:T(8,128)(2,1)}, u32[]{:S(2)}) copy-start(bf16[16,56]{1,0:T(8,128)(2,1)} %param.17) | copy-start | bytes 5380
  267.7 321.0 %copy-start.6 = (f32[256,16]{0,1:T(8,128)S(1)}, f32[256,16]{0,1:T(8,128)}, u32[]{:S(2)}) copy-start(f32[256,16]{0,1:T(8,128)} %param.18) | copy-start | bytes 49156
  267.7 391.8 %copy-start.10 = (f32[4]{0:T(128)S(1)}, f32[4]{0:T(128)}, u32[]{:S(2)}) copy-start(f32[4]{0:T(128)} %param.19) | copy-start | bytes 52
  267.7 392.0 %copy-start.8 = (s32[2]{0:T(128)S(1)}, s32[2]{0:T(128)}, u32[]{:S(2)}) copy-start(s32[2]{0:T(128)} %param.21) | copy-start | bytes 28
  267.7 531.3 %copy-start.4 = (bf16[1,224,1792]{2,1,0:T(8,128)(2,1)S(1)}, bf16[1,224,1792]{2,1,0:T(8,128)(2,1)}, u32[]{:S(2)}) copy-start(bf16[1,224,1792]{2,1,0:T(8,128)(2,1)} %param.16) | copy-start | bytes 2408452
  426.0 40.6 %all-to-all-start.1 = ((bf16[16,2,896]{2,1,0:T(2,128)(2,1)}), bf16[16,2,896]{2,1,0:T(2,128)(2,1)S(1)}, u32[]{:S(2)}, u32[]{:S(2)}) async-start(bf16[16,2,896]{2,1,0:T(2,128)(2,1)} %reshape.105), calls=%async_computation.1 | async-start | bytes 114688 | tf_op jit(solution)/shard_map/all_to_all | solution.py:124
  456.9 342.1 %all-gather.5.cloned.1.call-start = ((), (), s32[]{:S(2)}) async-start(), calls=%async_computation.7 | async-start | bytes 1892352 | tf_op jit(solution)/shard_map/all_gather | solution.py:153
  675.4 301.2 %reduce-scatter.9.cloned.1.call-start = ((), (), s32[]{:S(2)}) async-start(), calls=%async_computation.9 | async-start | bytes 1892352
  978.8 40.5 %all-to-all-start.3 = ((bf16[16,2,896]{2,1,0:T(2,128)(2,1)}), bf16[16,2,896]{2,1,0:T(2,128)(2,1)S(1)}, u32[]{:S(2)}, u32[]{:S(2)}) async-start(bf16[16,2,896]{2,1,0:T(2,128)(2,1)} %reshape.109), calls=%async_computation.3 | async-start | bytes 114688 | tf_op jit(solution)/shard_map/all_to_all | solution.py:166
Sparse Core Ops, SparseCore 0:
  121.2 123.3 all-gather.2
  267.9 155.9 reduce-scatter.6
  675.6 123.4 all-gather.4
  820.5 156.1 reduce-scatter.8
where the time goes:
time: 1100 us; the launch traced here: 1090 us
  waiting for transfers between devices  578 us (53%)
  blocking collectives  371 us (34%)
  starting transfers between devices  62 us (6%)
  local copies, waits for them, and re-layouts  46.4 us (4%)
  between operations  15.8 us (1%)
  matrix products  11.3 us (1%)
    unnamed x6, waiting for transfers between devices  313 us
    all_gather x1, waiting for transfers between devices, local(): lax.all_gather(arrived.reshape(slot_total, feat_dev), 'fsdp', axis=1, til...  124 us
    all_gather x1, waiting for transfers between devices, local(): lax.all_gather(grad_arrived.reshape(slot_total, feat_dev), 'fsdp', axis=1...  123 us
    psum x1, blocking collectives, local(): prediction = lax.psum(pred_part, 'fsdp')  121 us
    psum x1, blocking collectives, local(): row_squares = lax.psum(jnp.sum(tok_float * tok_float, axis=1), 'fsdp')  73.2 us
    psum x1, blocking collectives, local(): sample_err = lax.psum(err_part, 'expert')  70.6 us
    psum x1, blocking collectives, local(): row_dot = lax.psum(jnp.sum(scaled_grad * normed_base, axis=1), 'fsdp')  62.4 us
    unnamed x39, local copies, waits for them, and re-layouts  43.6 us
  transfers between devices with their start and end apart: 6, of which 6 were waited for; matrix products, arithmetic and copies ran while one was open for 0% of the time, Pallas kernels for 0%

commit v1 on v0

v1 whole, which is shorter than its diff:
```python
import math

import jax
import jax.numpy as jnp
from jax import lax
from jax.sharding import PartitionSpec as P

D = 1792
TOPK = 2
C_OUT = 16
SAMPLES = 4
LANES = 128


norm_eps = 1e-06
dpo_beta = 2.0
bf16 = jnp.bfloat16
f32 = jnp.float32
highest = lax.Precision.HIGHEST
contract_first = (((0,), (0,)), ((), ()))
contract_last = (((1,), (1,)), ((), ()))


def gelu_tanh(values):
    return jax.nn.gelu(values, approximate=True)


def dpo_terms(sample_err, ref_err, pair_ids, timesteps):
    count = sample_err.shape[0]
    sample_ids = jnp.arange(count, dtype=jnp.int32)
    winners = pair_ids[0::2]
    losers = pair_ids[1::2]
    win_sel = (winners[:, None] == sample_ids[None, :]).astype(f32)
    lose_sel = (losers[:, None] == sample_ids[None, :]).astype(f32)
    excess = sample_err - ref_err
    margin = jnp.sum(win_sel * excess[None, :], axis=1) - jnp.sum(
        lose_sel * excess[None, :], axis=1
    )
    fraction = timesteps.astype(f32) / 1000.0
    keep_level = jnp.cos((fraction + 0.008) / 1.008 * (math.pi / 2.0)) ** 2
    strength = dpo_beta * keep_level
    inside = -strength * margin
    loss = jnp.mean(jax.nn.softplus(-inside))
    slope = -jax.nn.sigmoid(-inside) / inside.shape[0]
    coef = jnp.sum(
        win_sel * (-slope * strength)[:, None] + lose_sel * (slope * strength)[:, None], axis=0
    )
    return (loss, coef)


def local_slots(routes, num_experts):
    flat_routes = routes.reshape(-1)
    expert_ids = jnp.arange(num_experts, dtype=jnp.int32)
    hits = (flat_routes[:, None] == expert_ids[None, :]).astype(jnp.int32)
    earlier = jnp.cumsum(hits, axis=0) - hits
    return jnp.sum(earlier * hits, axis=1).reshape(routes.shape)


def high_low(values):
    high = lax.reduce_precision(values, exponent_bits=8, mantissa_bits=7)
    return high.astype(bf16), (values - high).astype(bf16)


def swap(chunks, axis):
    return lax.all_to_all(chunks, axis, split_axis=0, concat_axis=0, tiled=True)


def local(
    tokens,
    modulation,
    routes,
    route_weights,
    w_first,
    w_second,
    head,
    targets,
    ref_err,
    pair_ids,
    timesteps,
):
    tok_rows, feat_dev = tokens.shape
    groups = lax.axis_size("expert")
    shards = lax.axis_size("fsdp")
    capacity = TOPK * tok_rows // groups
    slot_total = groups * capacity
    tokens_all = tok_rows * groups
    tok_sample = tokens_all // SAMPLES
    my_sample = lax.axis_index("expert") * tok_rows // tok_sample
    w_in = w_first[0]
    w_out = w_second[0]
    shift, scale, gate = modulation[:, 0], modulation[:, 1], modulation[:, 2]

    with jax.named_scope("routing"):
        slots = local_slots(routes, groups)
        kept = slots < capacity
        dest = routes * capacity + slots
        slot_ids = jnp.arange(slot_total, dtype=jnp.int32)
        place = (dest[:, :, None] == slot_ids[None, None, :]) & kept[:, :, None]
        pick = jnp.any(place, axis=1).astype(bf16)
        weighted = jnp.sum(jnp.where(place, route_weights[:, :, None], 0.0), axis=1)

    with jax.named_scope("dispatch"):
        outgoing = lax.dot_general(
            pick, tokens, contract_first, preferred_element_type=f32
        ).astype(bf16)
        arrived = swap(outgoing.reshape(groups, capacity, feat_dev), "expert")
        arrived = arrived.reshape(SAMPLES, LANES, feat_dev).transpose(0, 2, 1)
        head_rows = jnp.pad(head, ((0, 0), (0, LANES - feat_dev)))
        parcel = jnp.concatenate([arrived.reshape(SAMPLES * feat_dev, LANES), head_rows], axis=0)
        gathered = swap(jnp.broadcast_to(parcel[None], (shards,) + parcel.shape), "fsdp")

    with jax.named_scope("projection"):
        body = SAMPLES * feat_dev
        head_all = gathered[:, body : body + C_OUT, :feat_dev].transpose(1, 0, 2).reshape(C_OUT, D)
        gated_head = (gate[:, None, :] * head_all[None].astype(f32)).reshape(SAMPLES * C_OUT, D)
        gated_pair = jnp.concatenate(high_low(gated_head), axis=0)
        proj = lax.dot_general(gated_pair, w_out, contract_last, preferred_element_type=f32)
        proj = proj[: SAMPLES * C_OUT] + proj[SAMPLES * C_OUT :]
        proj = proj.reshape(SAMPLES, C_OUT, -1)
        shift_pair = jnp.concatenate(high_low(shift), axis=0)
        shift_proj = jnp.dot(shift_pair, w_in, preferred_element_type=f32)
        shift_proj = shift_proj[:SAMPLES] + shift_proj[SAMPLES:]

    with jax.named_scope("first_layer"):
        normed, rms = [], []
        for s in range(SAMPLES):
            rows = gathered[:, s * feat_dev : (s + 1) * feat_dev].reshape(D, LANES).astype(f32)
            rms_s = lax.rsqrt(jnp.sum(rows * rows, axis=0) / D + norm_eps)
            rms.append(rms_s)
            normed.append(
                (rows * rms_s[None, :] * (1.0 + scale[s])[:, None] + shift[s][:, None]).astype(bf16)
            )
        normed = jnp.concatenate(normed, axis=1)
        rms = jnp.concatenate(rms)
        pre = lax.dot_general(w_in, normed, contract_first, preferred_element_type=f32)
        act, gelu_grad = jax.vjp(gelu_tanh, pre)
        act = act.astype(bf16)

    with jax.named_scope("predict"):
        parts = []
        for s in range(SAMPLES):
            proj_pair = jnp.concatenate(high_low(proj[s]), axis=0)
            part = jnp.dot(
                proj_pair, act[:, s * LANES : (s + 1) * LANES], preferred_element_type=f32
            )
            parts.append(part[:C_OUT] + part[C_OUT:])
        parts = jnp.concatenate(parts, axis=1)
        parts = parts.reshape(C_OUT, groups, capacity).transpose(1, 0, 2)
        returned = swap(parts.reshape(groups, C_OUT * capacity // LANES, LANES), "expert")
        returned = returned.reshape(groups, C_OUT, capacity).transpose(1, 0, 2)
        returned = returned.reshape(C_OUT, slot_total)
        pred = lax.dot_general(returned, weighted, contract_last, precision=highest)
        pred = pred + lax.dot_general(head, tokens, contract_last, preferred_element_type=f32)
        pred = jnp.sum(swap(jnp.broadcast_to(pred[None], (shards,) + pred.shape), "fsdp"), axis=0)
        residue = pred - targets.T
        group_err = jnp.sum(residue * residue)

    with jax.named_scope("residue"):
        weighted_residue = jnp.dot(residue, weighted, precision=highest)
        weighted_residue = weighted_residue.reshape(C_OUT, groups, capacity).transpose(1, 0, 2)
        parcel = jnp.concatenate(
            [
                weighted_residue.reshape(groups, C_OUT * capacity),
                jnp.broadcast_to(group_err, (groups, LANES)),
            ],
            axis=1,
        )
        parcel = swap(parcel.reshape(groups, -1, LANES), "expert").reshape(groups, -1)
        sample_err = jnp.sum(parcel[:, C_OUT * capacity].reshape(SAMPLES, -1), axis=1)
        upstream = parcel[:, : C_OUT * capacity].reshape(groups, C_OUT, capacity)
        upstream = upstream.transpose(1, 0, 2).reshape(C_OUT, slot_total)

    with jax.named_scope("backward"):
        grad_act = []
        for s in range(SAMPLES):
            grad_act.append(
                lax.dot_general(
                    proj[s],
                    upstream[:, s * LANES : (s + 1) * LANES],
                    contract_first,
                    precision=highest,
                )
            )
        grad_pre = gelu_grad(jnp.concatenate(grad_act, axis=1))[0]
        shift_cols = jnp.repeat(shift_proj.T, LANES, axis=1)
        row_dot = jnp.sum(grad_pre * (pre - shift_cols), axis=0)
        inner_high, inner_low = high_low((rms * rms * row_dot / D).reshape(SAMPLES, LANES))
        grad_in = jnp.dot(w_in, grad_pre.astype(bf16), preferred_element_type=f32)
        grad_in = (grad_in * rms[None, :]).astype(bf16)
        grad_in = grad_in.reshape(shards, feat_dev, SAMPLES, LANES).transpose(0, 2, 1, 3)
        parcel = jnp.concatenate(
            [
                grad_in.reshape(shards, SAMPLES * feat_dev, LANES),
                jnp.broadcast_to(inner_high[None], (shards, SAMPLES, LANES)),
                jnp.broadcast_to(inner_low[None], (shards, SAMPLES, LANES)),
            ],
            axis=1,
        )
        summed = jnp.sum(swap(parcel, "fsdp").astype(f32), axis=0)
        inner = summed[body : body + SAMPLES] + summed[body + SAMPLES : body + 2 * SAMPLES]
        inner_high, inner_low = high_low(inner)
        home = jnp.concatenate(
            [
                summed[:body].reshape(SAMPLES, feat_dev, LANES).astype(bf16),
                inner_high[:, None, :],
                inner_low[:, None, :],
            ],
            axis=1,
        )
        home = home.reshape(SAMPLES, feat_dev + 2, groups // SAMPLES, capacity)
        home = home.transpose(0, 2, 3, 1).reshape(groups, capacity, feat_dev + 2)
        home = swap(home, "expert").reshape(slot_total, feat_dev + 2)
        back = jnp.dot(pick, home, preferred_element_type=f32)

    with jax.named_scope("finish"):
        loss, coef = dpo_terms(
            sample_err / (tok_sample * C_OUT), ref_err, pair_ids, timesteps
        )
        feat_start = lax.axis_index("fsdp") * feat_dev
        my_scale = lax.dynamic_slice(scale, (my_sample, feat_start), (1, feat_dev))
        my_coef = lax.dynamic_slice(coef, (my_sample,), (1,))[0]
        my_coef = my_coef * (tokens_all * C_OUT * 2.0 / (tok_sample * C_OUT))
        grad_block = lax.dot_general(
            residue, head.astype(f32), contract_first, precision=highest
        )
        inner = back[:, feat_dev] + back[:, feat_dev + 1]
        grad_tokens = my_coef * (
            grad_block
            + back[:, :feat_dev] * (1.0 + my_scale)
            - tokens.astype(f32) * inner[:, None]
        )
    return (grad_tokens.astype(bf16), loss)


def solution(mesh):
    in_specs = (
        P("expert", "fsdp"),
        P(),
        P("expert", None),
        P("expert", None),
        P("expert", None, "fsdp"),
        P("expert", "fsdp", None),
        P(None, "fsdp"),
        P("expert", None),
        P(),
        P(),
        P(),
    )
    out_specs = (P("expert", "fsdp"), P())
    return jax.shard_map(local, mesh=mesh, in_specs=in_specs, out_specs=out_specs, check_vma=False)
```

time: 1100 us -> 253 us (0.23)
  waiting for transfers between devices: 578 us -> 140 us
  blocking collectives: 371 us -> 20.6 us
  local copies, waits for them, and re-layouts: 46.4 us -> 17.4 us
  starting transfers between devices: 62 us -> 46.3 us
  between operations: 15.8 us -> 3.68 us
    psum x4 -> x0, blocking collectives: 327 us -> none  [the longest x1 121 us: local(): prediction = lax.psum(pred_part, 'fsdp')]
    unnamed x6 -> x0, waiting for transfers between devices: 313 us -> none
    all_gather x2 -> x0, waiting for transfers between devices: 247 us -> none  [the longest x1 124 us: local(): lax.all_gather(arrived.reshape(slot_total, feat_dev), 'fsdp', axis=1, til...]
    all_to_all x2 -> x6, waiting for transfers between devices: 18.6 us -> 140 us  [swap(): return lax.all_to_all(chunks, axis, split_axis=0, concat_axis=0, tiled=True)]
    unnamed x39 -> x36, local copies, waits for them, and re-layouts: 43.6 us -> 2.49 us
    all_to_all x2 -> x1, blocking collectives: 43.9 us -> 20.6 us  [swap(): return lax.all_to_all(chunks, axis, split_axis=0, concat_axis=0, tiled=True)]
    all_to_all x2 -> x6, starting transfers between devices: 61.7 us -> 46.3 us  [swap(): return lax.all_to_all(chunks, axis, split_axis=0, concat_axis=0, tiled=True)]
  transfers between devices with their start and end apart: 6 -> 6, of which waited for: 6 -> 6; matrix products, arithmetic and copies ran while one was open for 0% -> 1% of each run, Pallas kernels for 0% -> 0%
where the time goes in v1:
time: 253 us; the launch traced here: 251 us
  waiting for transfers between devices  140 us (55%)
  starting transfers between devices  46.3 us (18%)
  blocking collectives  20.6 us (8%)
  local copies, waits for them, and re-layouts  17.4 us (7%)
  matrix products  12.2 us (5%)
  other arithmetic  10.5 us (4%)
  between operations  3.68 us (1%)
    all_to_all x6, waiting for transfers between devices, swap(): return lax.all_to_all(chunks, axis, split_axis=0, concat_axis=0, tiled=True)  140 us
    all_to_all x6, starting transfers between devices, swap(): return lax.all_to_all(chunks, axis, split_axis=0, concat_axis=0, tiled=True)  46.3 us
    all_to_all x1, blocking collectives, swap(): return lax.all_to_all(chunks, axis, split_axis=0, concat_axis=0, tiled=True)  20.6 us
  transfers between devices with their start and end apart: 6, of which 6 were waited for; matrix products, arithmetic and copies ran while one was open for 1% of the time, Pallas kernels for 0%

profile of v1, /device:TPU:1, one launch (start us, length us, event | category | flops | bytes accessed | tf_op | source)
XLA Modules:
  0.0 251.2 jit_solution(17325489793640781008)
XLA Ops:
  0.7 0.9 copy.158
  1.9 1.2 reduce-window.6
  3.6 0.7 multiply_add_fusion
  4.5 0.9 convolution_convert_fusion
  5.8 20.6 %all_to_all.35 = bf16[16,2,896]{2,1,0:T(2,128)(2,1)S(1)} all-to-all(bf16[16,2,896]{2,1,0:T(2,128)(2,1)S(1)} %reshape.280), channel_id=1, replica_groups=mesh['fsdp'=32,'expert'=16] {'expert'}, dimensions={0} | all-to-all | bytes 114688 | tf_op jit(solution)/shard_map/dispatch/all_to_all | solution.py:65
  26.8 1.5 broadcast_in_dim.22
  28.3 10.9 %all-to-all-start.1 = ((bf16[32,240,128]{2,1,0:T(8,128)(2,1)}), bf16[32,240,128]{2,1,0:T(8,128)(2,1)S(1)}, u32[]{:S(2)}, u32[]{:S(2)}) async-start(bf16[32,240,128]{2,1,0:T(8,128)(2,1)} %broadcast_in_dim.22), calls=%async_computation.1 | async-start | bytes 3932160 | tf_op jit(solution)/shard_map/dispatch/all_to_all | solution.py:65
  39.4 50.5 %all-to-all-done.1 = bf16[32,240,128]{2,1,0:T(8,128)(2,1)S(1)} async-done(((bf16[32,240,128]{2,1,0:T(8,128)(2,1)}), bf16[32,240,128]{2,1,0:T(8,128)(2,1)S(1)}, u32[]{:S(2)}, u32[]{:S(2)}) %all-to-all-start.1) | async-done | bytes 1966112 | tf_op jit(solution)/shard_map/dispatch/all_to_all | solution.py:65
  90.7 1.6 fusion.33
  92.6 1.4 fusion.25
  94.0 1.4 fusion.19
  95.4 1.4 multiply_convert_fusion.1
  97.6 0.7 reshape.251
  98.3 9.4 %all-to-all-start.2 = ((f32[16,4,128]{2,1,0:T(4,128)}), f32[16,4,128]{2,1,0:T(4,128)S(1)}, u32[]{:S(2)}, u32[]{:S(2)}) async-start(f32[16,4,128]{2,1,0:T(4,128)} %reshape.251), calls=%async_computation.2 | async-start | bytes 65536 | tf_op jit(solution)/shard_map/predict/all_to_all | solution.py:65
  107.9 9.4 %all-to-all-done.2 = f32[16,4,128]{2,1,0:T(4,128)S(1)} async-done(((f32[16,4,128]{2,1,0:T(4,128)}), f32[16,4,128]{2,1,0:T(4,128)S(1)}, u32[]{:S(2)}, u32[]{:S(2)}) %all-to-all-start.2) | async-done | bytes 32800 | tf_op jit(solution)/shard_map/predict/all_to_all | solution.py:65
  118.3 0.9 broadcast_in_dim.25
  119.1 7.9 %all-to-all-start.3 = ((f32[32,16,256]{2,1,0:T(8,128)}), f32[32,16,256]{2,1,0:T(8,128)S(1)}, u32[]{:S(2)}, u32[]{:S(2)}) async-start(f32[32,16,256]{2,1,0:T(8,128)} %broadcast_in_dim.25), calls=%async_computation.3 | async-start | bytes 1048576 | tf_op jit(solution)/shard_map/predict/all_to_all | solution.py:65
  127.7 14.3 %all-to-all-done.3 = f32[32,16,256]{2,1,0:T(8,128)S(1)} async-done(((f32[32,16,256]{2,1,0:T(8,128)}), f32[32,16,256]{2,1,0:T(8,128)S(1)}, u32[]{:S(2)}, u32[]{:S(2)}) %all-to-all-start.3) | async-done | bytes 524320 | tf_op jit(solution)/shard_map/predict/all_to_all | solution.py:65
  142.7 1.1 convolution_bitcast_fusion
  145.2 5.8 %all-to-all-start.4 = ((f32[16,5,128]{2,1,0:T(8,128)}), f32[16,5,128]{2,1,0:T(8,128)S(1)}, u32[]{:S(2)}, u32[]{:S(2)}) async-start(f32[16,5,128]{2,1,0:T(8,128)} %reshape.255), calls=%async_computation.4 | async-start | bytes 131072 | tf_op jit(solution)/shard_map/residue/all_to_all | solution.py:65
  151.1 9.8 %all-to-all-done.4 = f32[16,5,128]{2,1,0:T(8,128)S(1)} async-done(((f32[16,5,128]{2,1,0:T(8,128)}), f32[16,5,128]{2,1,0:T(8,128)S(1)}, u32[]{:S(2)}, u32[]{:S(2)}) %all-to-all-start.4) | async-done | bytes 40992 | tf_op jit(solution)/shard_map/residue/all_to_all | solution.py:65
  162.6 3.2 %fusion = bf16[1792,512]{0,1:T(8,128)(2,1)} fusion(f32[512]{0:T(512)S(1)} %pad_maximum_fusion.3, bf16[1,1792,224]{1,2,0:T(8,128)(2,1)S(1)} %copy-done, f32[224,512]{1,0:T(8,128)} %get-tuple-element.44, f32[224,128]{1,0:T(8,128)S(1)} %fusion.83, f32[224,128]{1,0:T(8,128)S(1)} %fusion.85, f32[224,128]{1,0:T(8,128)S(1)} %fusion.87, f32[224,128]{1,0:T(8,128)S(1)} %fusion.89), kind=kOutput, calls=%fused_computation.2 | convolution fusion | flops 415514624 | bytes 3557376 | tf_op jit(solution)/shard_map/backward/dot_general | solution.py:188
  165.8 2.8 %copy.172 = bf16[1792,512]{1,0:T(8,128)(2,1)S(1)} copy(bf16[1792,512]{0,1:T(8,128)(2,1)} %fusion) | data formatting | bytes 3670016 | tf_op jit(solution)/shard_map/backward/convert_element_type | solution.py:189
  168.6 1.5 reshape.259
  170.1 1.8 copy.173
  172.7 1.4 pad_maximum_fusion
  174.1 5.3 %all-to-all-start.5 = ((bf16[32,232,128]{2,1,0:T(8,128)(2,1)}), bf16[32,232,128]{2,1,0:T(8,128)(2,1)S(1)}, u32[]{:S(2)}, u32[]{:S(2)}) async-start(bf16[32,232,128]{2,1,0:T(8,128)(2,1)} %pad_maximum_fusion), calls=%async_computation.5 | async-start | bytes 3801088 | tf_op jit(solution)/shard_map/backward/all_to_all | solution.py:65
  181.0 48.8 %all-to-all-done.5 = bf16[32,232,128]{2,1,0:T(8,128)(2,1)S(1)} async-done(((bf16[32,232,128]{2,1,0:T(8,128)(2,1)}), bf16[32,232,128]{2,1,0:T(8,128)(2,1)S(1)}, u32[]{:S(2)}, u32[]{:S(2)}) %all-to-all-start.5) | async-done | bytes 1900576 | tf_op jit(solution)/shard_map/backward/all_to_all | solution.py:65
  231.2 0.8 reshape.282
  232.0 7.0 %all-to-all-start.6 = ((bf16[16,2,928]{2,1,0:T(2,128)(2,1)}), bf16[16,2,928]{2,1,0:T(2,128)(2,1)S(1)}, u32[]{:S(2)}, u32[]{:S(2)}) async-start(bf16[16,2,928]{2,1,0:T(2,128)(2,1)} %reshape.282), calls=%async_computation.6 | async-start | bytes 131072 | tf_op jit(solution)/shard_map/backward/all_to_all | solution.py:65
  241.0 7.8 %all-to-all-done.6 = bf16[16,2,928]{2,1,0:T(2,128)(2,1)S(1)} async-done(((bf16[16,2,928]{2,1,0:T(2,128)(2,1)}), bf16[16,2,928]{2,1,0:T(2,128)(2,1)S(1)}, u32[]{:S(2)}, u32[]{:S(2)}) %all-to-all-start.6) | async-done | bytes 59424 | tf_op jit(solution)/shard_map/backward/all_to_all | solution.py:65
  249.2 0.8 fusion.14
  (130 shorter events, 14.2 us)
Async XLA Ops:
  0.6 94.8 %copy-start = (bf16[1,1792,224]{1,2,0:T(8,128)(2,1)S(1)}, bf16[1,1792,224]{1,2,0:T(8,128)(2,1)}, u32[]{:S(2)}) copy-start(bf16[1,1792,224]{1,2,0:T(8,128)(2,1)} %param.15) | copy-start | bytes 2408452
  0.6 26.1 %copy-start.5 = (bf16[16,56]{1,0:T(8,128)(2,1)S(1)}, bf16[16,56]{1,0:T(8,128)(2,1)}, u32[]{:S(2)}) copy-start(bf16[16,56]{1,0:T(8,128)(2,1)} %param.17) | copy-start | bytes 5380
  28.3 10.9 %copy-start.2 = (f32[4,3,1792]{2,0,1:T(4,128)S(1)}, f32[4,3,1792]{2,0,1:T(4,128)}, u32[]{:S(2)}) copy-start(f32[4,3,1792]{2,0,1:T(4,128)} %param.12) | copy-start | bytes 258052
  28.3 61.6 %all-to-all-start.1 = ((bf16[32,240,128]{2,1,0:T(8,128)(2,1)}), bf16[32,240,128]{2,1,0:T(8,128)(2,1)S(1)}, u32[]{:S(2)}, u32[]{:S(2)}) async-start(bf16[32,240,128]{2,1,0:T(8,128)(2,1)} %broadcast_in_dim.22), calls=%async_computation.1 | async-start | bytes 3932160 | tf_op jit(solution)/shard_map/dispatch/all_to_all | solution.py:65
  90.3 3.7 %copy-start.6 = (f32[128]{0:T(128)}, f32[128]{0:T(128)S(1)}, u32[]{:S(2)}) copy-start(f32[128]{0:T(128)S(1)} %add_rsqrt_fusion) | copy-start | bytes 1540
  90.3 3.7 %copy-start.8 = (f32[128]{0:T(128)}, f32[128]{0:T(128)S(1)}, u32[]{:S(2)}) copy-start(f32[128]{0:T(128)S(1)} %add_rsqrt_fusion.1) | copy-start | bytes 1540
  95.4 12.2 %copy-start.11 = (f32[256,2]{0,1:T(2,128)S(1)}, f32[256,2]{0,1:T(2,128)}, u32[]{:S(2)}) copy-start(f32[256,2]{0,1:T(2,128)} %param.14) | copy-start | bytes 6148
  96.8 21.3 %copy-start.4 = (bf16[256,56]{0,1:T(8,128)(2,1)S(1)}, bf16[256,56]{0,1:T(8,128)(2,1)}, u32[]{:S(2)}) copy-start(bf16[256,56]{0,1:T(8,128)(2,1)} %param.11) | copy-start | bytes 86020
  98.3 19.1 %all-to-all-start.2 = ((f32[16,4,128]{2,1,0:T(4,128)}), f32[16,4,128]{2,1,0:T(4,128)S(1)}, u32[]{:S(2)}, u32[]{:S(2)}) async-start(f32[16,4,128]{2,1,0:T(4,128)} %reshape.251), calls=%async_computation.2 | async-start | bytes 65536 | tf_op jit(solution)/shard_map/predict/all_to_all | solution.py:65
  119.1 22.9 %copy-start.3 = (f32[256,16]{0,1:T(8,128)S(1)}, f32[256,16]{0,1:T(8,128)}, u32[]{:S(2)}) copy-start(f32[256,16]{0,1:T(8,128)} %param.18) | copy-start | bytes 49156
  119.1 22.9 %all-to-all-start.3 = ((f32[32,16,256]{2,1,0:T(8,128)}), f32[32,16,256]{2,1,0:T(8,128)S(1)}, u32[]{:S(2)}, u32[]{:S(2)}) async-start(f32[32,16,256]{2,1,0:T(8,128)} %broadcast_in_dim.25), calls=%async_computation.3 | async-start | bytes 1048576 | tf_op jit(solution)/shard_map/predict/all_to_all | solution.py:65
  127.0 24.0 %copy-start.7 = (f32[128]{0:T(128)S(1)}, f32[128]{0:T(128)}, u32[]{:S(2)}) copy-start(f32[128]{0:T(128)} %copy-done.6) | copy-start | bytes 1540
  127.0 24.0 %copy-start.9 = (f32[128]{0:T(128)S(1)}, f32[128]{0:T(128)}, u32[]{:S(2)}) copy-start(f32[128]{0:T(128)} %copy-done.8) | copy-start | bytes 1540
  145.2 15.6 %all-to-all-start.4 = ((f32[16,5,128]{2,1,0:T(8,128)}), f32[16,5,128]{2,1,0:T(8,128)S(1)}, u32[]{:S(2)}, u32[]{:S(2)}) async-start(f32[16,5,128]{2,1,0:T(8,128)} %reshape.255), calls=%async_computation.4 | async-start | bytes 131072 | tf_op jit(solution)/shard_map/residue/all_to_all | solution.py:65
  170.1 2.1 copy-start.1
  170.1 2.5 copy-start.10
  174.1 5.4 %copy-start.13 = (s32[4]{0:T(128)S(1)}, s32[4]{0:T(128)}, u32[]{:S(2)}) copy-start(s32[4]{0:T(128)} %param.20) | copy-start | bytes 52
  174.1 6.0 %copy-start.14 = (f32[4]{0:T(128)S(1)}, f32[4]{0:T(128)}, u32[]{:S(2)}) copy-start(f32[4]{0:T(128)} %param.19) | copy-start | bytes 52
  174.1 6.2 %copy-start.12 = (s32[2]{0:T(128)S(1)}, s32[2]{0:T(128)}, u32[]{:S(2)}) copy-start(s32[2]{0:T(128)} %param.21) | copy-start | bytes 28
  174.1 55.7 %all-to-all-start.5 = ((bf16[32,232,128]{2,1,0:T(8,128)(2,1)}), bf16[32,232,128]{2,1,0:T(8,128)(2,1)S(1)}, u32[]{:S(2)}, u32[]{:S(2)}) async-start(bf16[32,232,128]{2,1,0:T(8,128)(2,1)} %pad_maximum_fusion), calls=%async_computation.5 | async-start | bytes 3801088 | tf_op jit(solution)/shard_map/backward/all_to_all | solution.py:65
  232.0 16.7 %all-to-all-start.6 = ((bf16[16,2,928]{2,1,0:T(2,128)(2,1)}), bf16[16,2,928]{2,1,0:T(2,128)(2,1)S(1)}, u32[]{:S(2)}, u32[]{:S(2)}) async-start(bf16[16,2,928]{2,1,0:T(2,128)(2,1)} %reshape.282), calls=%async_computation.6 | async-start | bytes 131072 | tf_op jit(solution)/shard_map/backward/all_to_all | solution.py:65

commit v2 on v1

v2 whole, which is shorter than its diff:
```python
import math

import jax
import jax.numpy as jnp
from jax import lax
from jax.sharding import Mesh, PartitionSpec as P

D = 1792
TOPK = 2
C_OUT = 16
SAMPLES = 4
LANES = 128
ATTRS = 64
FSDP = ("yh", "yl", "zh", "zl")


norm_eps = 1e-06
dpo_beta = 2.0
bf16 = jnp.bfloat16
f32 = jnp.float32
highest = lax.Precision.HIGHEST
contract_first = (((0,), (0,)), ((), ()))
contract_last = (((1,), (1,)), ((), ()))


def gelu_tanh(values):
    return jax.nn.gelu(values, approximate=True)


def dpo_terms(sample_err, ref_err, pair_ids, timesteps):
    count = sample_err.shape[0]
    sample_ids = jnp.arange(count, dtype=jnp.int32)
    winners = pair_ids[0::2]
    losers = pair_ids[1::2]
    win_sel = (winners[:, None] == sample_ids[None, :]).astype(f32)
    lose_sel = (losers[:, None] == sample_ids[None, :]).astype(f32)
    excess = sample_err - ref_err
    margin = jnp.sum(win_sel * excess[None, :], axis=1) - jnp.sum(
        lose_sel * excess[None, :], axis=1
    )
    fraction = timesteps.astype(f32) / 1000.0
    keep_level = jnp.cos((fraction + 0.008) / 1.008 * (math.pi / 2.0)) ** 2
    strength = dpo_beta * keep_level
    inside = -strength * margin
    loss = jnp.mean(jax.nn.softplus(-inside))
    slope = -jax.nn.sigmoid(-inside) / inside.shape[0]
    coef = jnp.sum(
        win_sel * (-slope * strength)[:, None] + lose_sel * (slope * strength)[:, None], axis=0
    )
    return (loss, coef)


def local_slots(routes, num_experts):
    flat_routes = routes.reshape(-1)
    expert_ids = jnp.arange(num_experts, dtype=jnp.int32)
    hits = (flat_routes[:, None] == expert_ids[None, :]).astype(jnp.int32)
    earlier = jnp.cumsum(hits, axis=0) - hits
    return jnp.sum(earlier * hits, axis=1).reshape(routes.shape)


def high_low(values):
    high = lax.reduce_precision(values, exponent_bits=8, mantissa_bits=7)
    return high.astype(bf16), (values - high).astype(bf16)


def swap(chunks, axis):
    return lax.all_to_all(chunks, axis, split_axis=0, concat_axis=0, tiled=True)


def copies(part, count):
    return jnp.broadcast_to(part[None], (count,) + part.shape)


def trade(part, axis):
    return lax.ppermute(part, axis, [(0, 1), (1, 0)])


def local(
    tokens,
    modulation,
    routes,
    route_weights,
    w_first,
    w_second,
    head,
    targets,
    ref_err,
    pair_ids,
    timesteps,
):
    tok_rows, feat_dev = tokens.shape
    groups = lax.axis_size("expert")
    shards = lax.axis_size(FSDP)
    capacity = TOPK * tok_rows // groups
    slot_total = groups * capacity
    tokens_all = tok_rows * groups
    tok_sample = tokens_all // SAMPLES
    block = tok_rows // shards
    my_shard = lax.axis_index(FSDP)
    my_sample = lax.axis_index("expert") * tok_rows // tok_sample
    quarter = lax.axis_index(("yl", "zl"))
    leader = (lax.axis_index(("yh", "zh")) == 0).astype(f32)
    sharers = lax.axis_size(("yh", "zh"))
    head_rows = C_OUT * feat_dev // LANES
    w_in = w_first[0]
    w_out = w_second[0]

    with jax.named_scope("weights"):
        half = D // 2
        w_y = trade(w_in, "yl")
        w_z = trade(w_in, "zl")
        w_d = jnp.concatenate([trade(w_z[:half], "yl"), trade(w_y[half:], "zl")], axis=0)
        weights = [w_in, w_y, w_z, w_d]

    with jax.named_scope("routing"):
        slots = local_slots(routes, groups)
        kept = slots < capacity
        dest = jnp.where(kept, routes * capacity + slots, -1)
        slot_ids = jnp.arange(slot_total, dtype=jnp.int32)
        place = (dest.T.reshape(-1)[:, None] == slot_ids[None, :]).astype(bf16)
        pick = place[:tok_rows] + place[tok_rows:]
        kept_w = jnp.where(kept, route_weights, 0.0)
        other_e = jnp.where(kept, routes, 0).astype(f32)
        other_s = jnp.where(kept, slots, 0).astype(f32)
        first = jnp.stack([jnp.ones((tok_rows,), f32), 1.0 - kept[:, 0].astype(f32)])
        target_parts = jnp.concatenate(high_low(targets.T), axis=0)
        rows = list(high_low(route_weights.T.reshape(-1)))
        rows += list(high_low(kept_w[:, ::-1].T.reshape(-1)))
        rows += [other_e[:, ::-1].T.reshape(-1), other_s[:, ::-1].T.reshape(-1), first.reshape(-1)]
        rows = jnp.stack([row.astype(bf16) for row in rows])
        table = jnp.concatenate(
            [
                jnp.concatenate([target_parts, target_parts], axis=1),
                rows,
                jnp.zeros((ATTRS - 2 * C_OUT - rows.shape[0], TOPK * tok_rows), bf16),
            ],
            axis=0,
        )
        share = ATTRS // shards
        mine = lax.dynamic_slice_in_dim(table, my_shard * share, share, 0)
        flat_tokens = tokens.T
        outgoing = jnp.concatenate(
            [jnp.concatenate([flat_tokens, flat_tokens], axis=1), mine], axis=0
        )

    with jax.named_scope("dispatch"):
        width = feat_dev + share
        outgoing = jnp.dot(outgoing, place, preferred_element_type=f32).astype(bf16)
        outgoing = outgoing.reshape(width, groups, capacity).transpose(1, 0, 2)
        arrived = swap(outgoing, "expert")
        arrived = arrived.reshape(SAMPLES, groups // SAMPLES, width, capacity)
        arrived = arrived.transpose(0, 2, 1, 3).reshape(1, 2, 1, 2, width, LANES)
        base = lax.dot_general(head, tokens, contract_last, preferred_element_type=f32)
        base = base.reshape(C_OUT, shards, block).transpose(1, 0, 2).reshape(shards, LANES)
        base_high, base_low = high_low(base)
        parcel = jnp.concatenate(
            [
                jnp.broadcast_to(arrived, (2, 2, 4, 2, width, LANES)).reshape(shards, width, LANES),
                copies(head.reshape(head_rows, LANES), shards),
                base_high[:, None],
                base_low[:, None],
                jnp.zeros((shards, -(width + head_rows + 2) % 8, LANES), bf16),
            ],
            axis=1,
        )
        gathered = swap(parcel, FSDP)

    with jax.named_scope("projection"):
        at = width + head_rows
        head_all = gathered[:, width:at].reshape(shards, C_OUT, feat_dev)
        head_all = head_all.transpose(1, 0, 2).reshape(C_OUT, D)
        base = jnp.sum(gathered[:, at : at + 2].astype(f32), axis=(0, 1)).reshape(C_OUT, block)
        gated_head = modulation[:, 2][:, None, :] * head_all[None].astype(f32)
        gated_pair = jnp.concatenate(high_low(gated_head.reshape(SAMPLES * C_OUT, D)), axis=0)
        proj = lax.dot_general(gated_pair, w_out, contract_last, preferred_element_type=f32)
        proj = proj[: SAMPLES * C_OUT] + proj[SAMPLES * C_OUT :]
        proj = proj.reshape(SAMPLES, C_OUT, -1)

        def projection_of(flip):
            return lax.dynamic_index_in_dim(proj, quarter ^ flip, 0, keepdims=False)

        opposite = [(i, 3 - i) for i in range(4)]
        proj = [
            projection_of(0),
            trade(projection_of(2), "yl"),
            trade(projection_of(1), "zl"),
            lax.ppermute(projection_of(3), ("yl", "zl"), opposite),
        ]

    with jax.named_scope("first_layer"):
        mod = lax.dynamic_index_in_dim(modulation, quarter, 0, keepdims=False)
        shift = mod[0][:, None]
        scale = 1.0 + mod[1][:, None]
        rows = gathered[:, :feat_dev].reshape(D, LANES)
        row_float = rows.astype(f32)
        rms = lax.rsqrt(jnp.sum(row_float * row_float, axis=0) / D + norm_eps)
        normed = (row_float * rms[None, :] * scale + shift).astype(bf16)
        attrs = gathered[:, feat_dev:width].reshape(ATTRS, LANES).astype(f32)
        target = attrs[:C_OUT] + attrs[C_OUT : 2 * C_OUT]
        own_w = attrs[32] + attrs[33]
        other_w = attrs[34] + attrs[35]
        first = attrs[38]
        base_rows = jnp.dot(head_all, rows, preferred_element_type=f32)
        act, gelu_grad = [], []
        for weight in weights:
            pre = lax.dot_general(weight, normed, contract_first, preferred_element_type=f32)
            values, backward = jax.vjp(gelu_tanh, pre)
            act.append(values.astype(bf16))
            gelu_grad.append(backward)

    with jax.named_scope("predict"):
        part = 0.0
        for proj_block, act_block in zip(proj, act):
            proj_pair = jnp.concatenate(high_low(proj_block), axis=0)
            part = part + jnp.dot(proj_pair, act_block, preferred_element_type=f32)
        part = part[:C_OUT] + part[C_OUT:]
        own = jnp.sum(swap(copies(part, sharers), ("yh", "zh")), axis=0)
        everyone = swap(copies(own.astype(bf16), groups), "expert")
        everyone = everyone.transpose(1, 0, 2).reshape(C_OUT, groups * LANES)
        lane = jnp.arange(LANES, dtype=jnp.int32)
        source = attrs[36] * LANES + attrs[37] + (lane // capacity * capacity).astype(f32)
        source = source.astype(jnp.int32)
        chosen = jnp.arange(groups * LANES, dtype=jnp.int32)[:, None] == source[None, :]
        partner = jnp.dot(everyone, chosen.astype(bf16), preferred_element_type=f32)
        residue = base_rows + own_w * own + other_w * partner - target
        kept_err = jnp.sum(first * residue * residue)

    with jax.named_scope("dropped"):
        lost = 1.0 - jnp.any(kept, axis=1).astype(f32)
        my_lost = lax.dynamic_slice_in_dim(lost, my_shard * block, block, 0)
        my_targets = lax.dynamic_slice_in_dim(targets, my_shard * block, block, 0)
        lost_residue = (base - my_targets.T) * my_lost[None, :]
        sample_ids = jnp.arange(LANES, dtype=jnp.int32)
        err_row = jnp.where(sample_ids == quarter, leader * kept_err, 0.0)
        err_row += jnp.where(sample_ids == my_sample, jnp.sum(lost_residue * lost_residue), 0.0)

    with jax.named_scope("backward"):
        upstream = own_w * residue
        grad_in = 0.0
        for weight, proj_block, backward in zip(weights, proj, gelu_grad):
            grad_act = lax.dot_general(proj_block, upstream, contract_first, precision=highest)
            grad_pre = backward(grad_act)[0].astype(bf16)
            grad_in = grad_in + jnp.dot(weight, grad_pre, preferred_element_type=f32)
        grad_in = grad_in * (rms[None, :] * scale)
        inner = jnp.sum(grad_in * row_float, axis=0) * rms * rms / D
        direct = jnp.concatenate(high_low(first * residue / sharers), axis=0)
        direct = lax.dot_general(
            jnp.concatenate([head_all, head_all], axis=0),
            direct,
            contract_first,
            preferred_element_type=f32,
        )
        grad_rows = (grad_in - row_float * inner[None, :] + direct).astype(bf16)
        tail = jnp.stack(high_low(lost_residue.reshape(LANES)) + high_low(err_row))
        tail = jnp.concatenate([tail, jnp.zeros((4, LANES), bf16)], axis=0)
        parcel = jnp.concatenate(
            [grad_rows.reshape(shards, feat_dev, LANES), copies(tail, shards)], axis=1
        )
        parcel = swap(parcel, FSDP)
        lost_residue = parcel[:, feat_dev].astype(f32) + parcel[:, feat_dev + 1].astype(f32)
        lost_residue = lost_residue.reshape(shards, C_OUT, block)
        lost_residue = lost_residue.transpose(1, 0, 2).reshape(C_OUT, tok_rows)
        err_row = jnp.sum(
            parcel[:, feat_dev + 2 : feat_dev + 4, :SAMPLES].astype(f32), axis=(0, 1)
        )
        home = parcel[:, :feat_dev].reshape(2, 2, 4, 2, feat_dev, LANES).astype(f32)
        home = jnp.sum(home, axis=(0, 2)).astype(bf16)
        home = home.reshape(SAMPLES, feat_dev, groups // SAMPLES, capacity)
        home = home.transpose(0, 2, 1, 3).reshape(groups, feat_dev, capacity)
        tail = jnp.concatenate(high_low(err_row) + (jnp.zeros((capacity - 8,), bf16),))
        home = jnp.concatenate([home, copies(tail[None], groups)], axis=1)
        home = swap(home, "expert")
        err_row = home[:, feat_dev, :SAMPLES].astype(f32) + home[:, feat_dev, 4:8].astype(f32)
        sample_err = jnp.sum(err_row, axis=0)
        back = home[:, :feat_dev].transpose(0, 2, 1).reshape(slot_total, feat_dev)
        back = jnp.dot(pick, back, preferred_element_type=f32)

    with jax.named_scope("finish"):
        loss, coef = dpo_terms(
            sample_err / (tok_sample * C_OUT), ref_err, pair_ids, timesteps
        )
        my_coef = lax.dynamic_slice(coef, (my_sample,), (1,))[0]
        my_coef = my_coef * (tokens_all * C_OUT * 2.0 / (tok_sample * C_OUT))
        direct = lax.dot_general(
            lost_residue, head.astype(f32), contract_first, precision=highest
        )
        grad_tokens = my_coef * (direct + back)
    return (grad_tokens.astype(bf16), loss)


def solution(mesh):
    mesh = Mesh(mesh.devices.reshape(2, 2, 4, 2, 16), FSDP + ("expert",))
    in_specs = (
        P("expert", FSDP),
        P(),
        P("expert", None),
        P("expert", None),
        P("expert", None, FSDP),
        P("expert", FSDP, None),
        P(None, FSDP),
        P("expert", None),
        P(),
        P(),
        P(),
    )
    out_specs = (P("expert", FSDP), P())
    return jax.shard_map(local, mesh=mesh, in_specs=in_specs, out_specs=out_specs, check_vma=False)
```

time: 253 us -> 191 us (0.75)
  waiting for transfers between devices: 140 us -> 66.7 us
  starting transfers between devices: 46.3 us -> 67.5 us
  blocking collectives: 20.6 us -> 0 us
  local copies, waits for them, and re-layouts: 17.4 us -> 26.8 us
    all_to_all x6, waiting for transfers between devices: 140 us -> 50.8 us  [swap(): return lax.all_to_all(chunks, axis, split_axis=0, concat_axis=0, tiled=True)]
    ppermute x0 -> x7, starting transfers between devices: none -> 22.8 us  [the longest x6 20.1 us: trade(): return lax.ppermute(part, axis, [(0, 1), (1, 0)])]
    all_to_all x1 -> x0, blocking collectives: 20.6 us -> none  [swap(): return lax.all_to_all(chunks, axis, split_axis=0, concat_axis=0, tiled=True)]
    ppermute x0 -> x7, waiting for transfers between devices: none -> 15.8 us  [the longest x6 15.8 us: trade(): return lax.ppermute(part, axis, [(0, 1), (1, 0)])]
    unnamed x36 -> x84, local copies, waits for them, and re-layouts: 2.49 us -> 13.3 us
    concatenate x5 -> x4, local copies, waits for them, and re-layouts: 1.25 us -> 5.64 us  [the longest x1 4.58 us: local(): jnp.concatenate([jnp.broadcast_to(arrived, (2, 2, 4, 2, width, LANES)).re...]
    reshape x11 -> x5, local copies, waits for them, and re-layouts: 3.51 us -> 0.63 us  [the longest x1 0.21 us: local(): head_all = gathered[:, width:at].reshape(shards, C_OUT, feat_dev)]
    dot_general x16 -> x22, matrix products: 10.5 us -> 13 us  [the longest x4 3.34 us: local(): lax.dot_general(weight, normed, contract_first, preferred_element_type=f32)]
  transfers between devices with their start and end apart: 6 -> 13, of which waited for: 6 -> 7; matrix products, arithmetic and copies ran while one was open for 1% -> 12% of each run, Pallas kernels for 0% -> 0%
where the time goes in v2:
time: 191 us; the launch traced here: 189 us
  starting transfers between devices  67.5 us (35%)
  waiting for transfers between devices  66.7 us (35%)
  local copies, waits for them, and re-layouts  26.8 us (14%)
  matrix products  13.6 us (7%)
  other arithmetic  9.64 us (5%)
  between operations  4.73 us (2%)
    all_to_all x6, waiting for transfers between devices, swap(): return lax.all_to_all(chunks, axis, split_axis=0, concat_axis=0, tiled=True)  50.8 us
    all_to_all x6, starting transfers between devices, swap(): return lax.all_to_all(chunks, axis, split_axis=0, concat_axis=0, tiled=True)  44.8 us
    ppermute x6, starting transfers between devices, trade(): return lax.ppermute(part, axis, [(0, 1), (1, 0)])  20.1 us
    ppermute x6, waiting for transfers between devices, trade(): return lax.ppermute(part, axis, [(0, 1), (1, 0)])  15.8 us
    unnamed x84, local copies, waits for them, and re-layouts  13.3 us
    concatenate x1, local copies, waits for them, and re-layouts, local(): jnp.concatenate([jnp.broadcast_to(arrived, (2, 2, 4, 2, width, LANES)).re...  4.58 us
  transfers between devices with their start and end apart: 13, of which 7 were waited for; matrix products, arithmetic and copies ran while one was open for 12% of the time, Pallas kernels for 0%

profile of v2, /device:TPU:1, one launch (start us, length us, event | category | flops | bytes accessed | tf_op | source)
XLA Modules:
  0.0 189.0 jit_solution(17188297072333891730)
XLA Ops:
  0.6 5.0 %collective-permute-start.3 = (bf16[1792,224]{0,1:T(8,128)(2,1)}, bf16[1792,224]{0,1:T(8,128)(2,1)S(1)}, u32[]{:S(2)}, u32[]{:S(2)}) collective-permute-start(bf16[1792,224]{0,1:T(8,128)(2,1)} %bitcast.181), channel_id=1, source_target_pairs={{0,16},{16,0},{1,17},{17,1},{2,18},{18,2},{3,19},{19,3},{4,20},{20... | collective-permute-start | bytes 2408456 | tf_op jit(solution)/shard_map/weights/ppermute | solution.py:75
  5.6 3.2 %collective-permute-start.1 = (bf16[1792,224]{0,1:T(8,128)(2,1)}, bf16[1792,224]{0,1:T(8,128)(2,1)S(1)}, u32[]{:S(2)}, u32[]{:S(2)}) collective-permute-start(bf16[1792,224]{0,1:T(8,128)(2,1)} %bitcast.182), channel_id=1, source_target_pairs={{0,128},{128,0},{1,129},{129,1},{2,130},{130,2},{3,131},{131,3},{4... | collective-permute-start | bytes 2408456 | tf_op jit(solution)/shard_map/weights/ppermute | solution.py:75
  10.5 1.2 reduce-window.6
  16.5 0.8 reshape.451
  17.3 10.0 %all-to-all-start = ((bf16[16,2,928]{2,1,0:T(2,128)(2,1)}), bf16[16,2,928]{2,1,0:T(2,128)(2,1)S(1)}, u32[]{:S(2)}, u32[]{:S(2)}) async-start(bf16[16,2,928]{2,1,0:T(2,128)(2,1)} %reshape.451), calls=%async_computation | async-start | bytes 131072 | tf_op jit(solution)/shard_map/dispatch/all_to_all | solution.py:67
  27.9 9.2 %all-to-all-done = bf16[16,2,928]{2,1,0:T(2,128)(2,1)S(1)} async-done(((bf16[16,2,928]{2,1,0:T(2,128)(2,1)}), bf16[16,2,928]{2,1,0:T(2,128)(2,1)S(1)}, u32[]{:S(2)}, u32[]{:S(2)}) %all-to-all-start) | async-done | bytes 59424 | tf_op jit(solution)/shard_map/dispatch/all_to_all | solution.py:67
  37.7 4.6 %concatenate.59 = bf16[32,72,128]{2,1,0:T(8,128)(2,1)} concatenate(bf16[32,58,128]{2,1,0:T(8,128)(2,1)S(1)} %bitcast.183, bf16[32,7,128]{2,1,0:T(8,128)(2,1)S(1)} %broadcast_in_dim.53, bf16[32,1,128]{2,1,0:T(2,128)(2,1)S(1)} %copy.180, bf16[32,1,128]{2,1,0:T(2,128)(2,1)S(1)} %copy.181, bf16[32,5,128]{2,1,0:T(8,128)(2,1)S(1)} %broadcast_in_dim.54), dimensions={1} | concatenate | bytes 1179648 | tf_op jit(solution)/shard_map/dispatch/concatenate | solution.py:156
  42.2 10.8 %all-to-all-start.1 = ((bf16[32,72,128]{2,1,0:T(8,128)(2,1)}), bf16[32,72,128]{2,1,0:T(8,128)(2,1)S(1)}, u32[]{:S(2)}, u32[]{:S(2)}) async-start(bf16[32,72,128]{2,1,0:T(8,128)(2,1)} %concatenate.59), calls=%async_computation.1 | async-start | bytes 1179648 | tf_op jit(solution)/shard_map/dispatch/all_to_all | solution.py:67
  53.5 3.1 %collective-permute-start.5 = (bf16[896,224]{0,1:T(8,128)(2,1)S(1)}, bf16[896,224]{0,1:T(8,128)(2,1)S(1)}, u32[]{:S(2)}, u32[]{:S(2)}) collective-permute-start(bf16[896,224]{0,1:T(8,128)(2,1)S(1)} %slice.157), channel_id=1, source_target_pairs={{0,128},{128,0},{1,129},{129,1},{2,130},{130,2},{3,131},{131,3},{4... | collective-permute-start | bytes 1204232 | tf_op jit(solution)/shard_map/weights/ppermute | solution.py:75
  56.7 3.1 %collective-permute-start.6 = (bf16[896,224]{0,1:T(8,128)(2,1)S(1)}, bf16[896,224]{0,1:T(8,128)(2,1)S(1)}, u32[]{:S(2)}, u32[]{:S(2)}) collective-permute-start(bf16[896,224]{0,1:T(8,128)(2,1)S(1)} %slice.158), channel_id=1, source_target_pairs={{0,16},{16,0},{1,17},{17,1},{2,18},{18,2},{3,19},{19,3},{4,20},{20... | collective-permute-start | bytes 1204232 | tf_op jit(solution)/shard_map/weights/ppermute | solution.py:75
  59.8 12.6 %collective-permute-done.5 = bf16[896,224]{0,1:T(8,128)(2,1)S(1)} collective-permute-done((bf16[896,224]{0,1:T(8,128)(2,1)S(1)}, bf16[896,224]{0,1:T(8,128)(2,1)S(1)}, u32[]{:S(2)}, u32[]{:S(2)}) %collective-permute-start.5) | collective-permute-done | bytes 401440 | tf_op jit(solution)/shard_map/weights/ppermute | solution.py:75
  73.2 3.3 %collective-permute-done.6 = bf16[896,224]{0,1:T(8,128)(2,1)S(1)} collective-permute-done((bf16[896,224]{0,1:T(8,128)(2,1)S(1)}, bf16[896,224]{0,1:T(8,128)(2,1)S(1)}, u32[]{:S(2)}, u32[]{:S(2)}) %collective-permute-start.6) | collective-permute-done | bytes 401440 | tf_op jit(solution)/shard_map/weights/ppermute | solution.py:75
  78.0 1.0 slice_convert_fusion
  79.0 1.5 copy.184
  81.8 2.8 %collective-permute-start = (f32[16,224]{1,0:T(8,128)S(1)}, f32[16,224]{1,0:T(8,128)S(1)}, u32[]{:S(2)}, u32[]{:S(2)}) collective-permute-start(f32[16,224]{1,0:T(8,128)S(1)} %get-tuple-element.25), channel_id=1, source_target_pairs={{0,128},{128,0},{1,129},{129,1},{2,130},{130,2},{3,131},{131,3},{4... | collective-permute-start | bytes 43016 | tf_op jit(solution)/shard_map/projection/ppermute | solution.py:75
  86.3 2.9 %collective-permute-start.2 = (f32[16,224]{1,0:T(8,128)S(1)}, f32[16,224]{1,0:T(8,128)S(1)}, u32[]{:S(2)}, u32[]{:S(2)}) collective-permute-start(f32[16,224]{1,0:T(8,128)S(1)} %get-tuple-element.24), channel_id=1, source_target_pairs={{0,16},{16,0},{1,17},{17,1},{2,18},{18,2},{3,19},{19,3},{4,20},{20... | collective-permute-start | bytes 43016 | tf_op jit(solution)/shard_map/projection/ppermute | solution.py:75
  89.2 2.6 %collective-permute-start.4 = (f32[16,224]{1,0:T(8,128)S(1)}, f32[16,224]{1,0:T(8,128)S(1)}, u32[]{:S(2)}, u32[]{:S(2)}) collective-permute-start(f32[16,224]{1,0:T(8,128)S(1)} %get-tuple-element.23), channel_id=1, source_target_pairs={{0,144},{16,128},{128,16},{144,0},{1,145},{17,129},{129,17},{145,1... | collective-permute-start | bytes 43016 | tf_op jit(solution)/shard_map/projection/ppermute | solution.py:187
  92.6 1.6 fusion.151
  96.0 1.0 convolution_bitcast_fusion.2
  101.0 7.4 %all-to-all-start.2 = ((f32[8,16,128]{2,1,0:T(8,128)}), f32[8,16,128]{2,1,0:T(8,128)S(1)}, u32[]{:S(2)}, u32[]{:S(2)}) async-start(f32[8,16,128]{2,1,0:T(8,128)} %broadcast_in_dim.102), calls=%async_computation.2 | async-start | bytes 131072 | tf_op jit(solution)/shard_map/predict/all_to_all | solution.py:67
  108.9 8.0 %all-to-all-done.2 = f32[8,16,128]{2,1,0:T(8,128)S(1)} async-done(((f32[8,16,128]{2,1,0:T(8,128)}), f32[8,16,128]{2,1,0:T(8,128)S(1)}, u32[]{:S(2)}, u32[]{:S(2)}) %all-to-all-start.2) | async-done | bytes 65568 | tf_op jit(solution)/shard_map/predict/all_to_all | solution.py:67
  117.6 6.3 %all-to-all-start.3 = ((bf16[16,16,128]{2,1,0:T(8,128)(2,1)}), bf16[16,16,128]{2,1,0:T(8,128)(2,1)S(1)}, u32[]{:S(2)}, u32[]{:S(2)}) async-start(bf16[16,16,128]{2,1,0:T(8,128)(2,1)} %broadcast_in_dim.103), calls=%async_computation.3 | async-start | bytes 131072 | tf_op jit(solution)/shard_map/predict/all_to_all | solution.py:67
  124.1 9.5 %all-to-all-done.3 = bf16[16,16,128]{2,1,0:T(8,128)(2,1)S(1)} async-done(((bf16[16,16,128]{2,1,0:T(8,128)(2,1)}), bf16[16,16,128]{2,1,0:T(8,128)(2,1)S(1)}, u32[]{:S(2)}, u32[]{:S(2)}) %all-to-all-start.3) | async-done | bytes 65568 | tf_op jit(solution)/shard_map/predict/all_to_all | solution.py:67
  133.6 1.6 reduce-precision_convert_fusion.7
  135.3 1.0 fusion.27
  137.5 1.5 fusion.152
  145.0 0.9 pad_maximum_fusion
  145.8 4.3 %all-to-all-start.4 = ((bf16[32,64,128]{2,1,0:T(8,128)(2,1)}), bf16[32,64,128]{2,1,0:T(8,128)(2,1)S(1)}, u32[]{:S(2)}, u32[]{:S(2)}) async-start(bf16[32,64,128]{2,1,0:T(8,128)(2,1)} %pad_maximum_fusion), calls=%async_computation.4 | async-start | bytes 1048576 | tf_op jit(solution)/shard_map/backward/all_to_all | solution.py:67
  150.5 14.7 %all-to-all-done.4 = bf16[32,64,128]{2,1,0:T(8,128)(2,1)S(1)} async-done(((bf16[32,64,128]{2,1,0:T(8,128)(2,1)}), bf16[32,64,128]{2,1,0:T(8,128)(2,1)S(1)}, u32[]{:S(2)}, u32[]{:S(2)}) %all-to-all-start.4) | async-done | bytes 524320 | tf_op jit(solution)/shard_map/backward/all_to_all | solution.py:67
  166.5 6.0 %all-to-all-start.5 = ((bf16[16,2,912]{2,1,0:T(2,128)(2,1)}), bf16[16,2,912]{2,1,0:T(2,128)(2,1)S(1)}, u32[]{:S(2)}, u32[]{:S(2)}) async-start(bf16[16,2,912]{2,1,0:T(2,128)(2,1)} %reshape.453), calls=%async_computation.5 | async-start | bytes 131072 | tf_op jit(solution)/shard_map/backward/all_to_all | solution.py:67
  172.8 9.5 %all-to-all-done.5 = bf16[16,2,912]{2,1,0:T(2,128)(2,1)S(1)} async-done(((bf16[16,2,912]{2,1,0:T(2,128)(2,1)}), bf16[16,2,912]{2,1,0:T(2,128)(2,1)S(1)}, u32[]{:S(2)}, u32[]{:S(2)}) %all-to-all-start.5) | async-done | bytes 58400 | tf_op jit(solution)/shard_map/backward/all_to_all | solution.py:67
  187.0 0.9 fusion.4
  (217 shorter events, 32.5 us)
Async XLA Ops:
  0.6 80.5 %copy-start = (bf16[1,224,1792]{2,1,0:T(8,128)(2,1)S(1)}, bf16[1,224,1792]{2,1,0:T(8,128)(2,1)}, u32[]{:S(2)}) copy-start(bf16[1,224,1792]{2,1,0:T(8,128)(2,1)} %param.16) | copy-start | bytes 2408452
  0.6 52.8 %collective-permute-start.3 = (bf16[1792,224]{0,1:T(8,128)(2,1)}, bf16[1792,224]{0,1:T(8,128)(2,1)S(1)}, u32[]{:S(2)}, u32[]{:S(2)}) collective-permute-start(bf16[1792,224]{0,1:T(8,128)(2,1)} %bitcast.181), channel_id=1, source_target_pairs={{0,16},{16,0},{1,17},{17,1},{2,18},{18,2},{3,19},{19,3},{4,20},{20... | collective-permute-start | bytes 2408456 | tf_op jit(solution)/shard_map/weights/ppermute | solution.py:75
  5.6 51.0 %collective-permute-start.1 = (bf16[1792,224]{0,1:T(8,128)(2,1)}, bf16[1792,224]{0,1:T(8,128)(2,1)S(1)}, u32[]{:S(2)}, u32[]{:S(2)}) collective-permute-start(bf16[1792,224]{0,1:T(8,128)(2,1)} %bitcast.182), channel_id=1, source_target_pairs={{0,128},{128,0},{1,129},{129,1},{2,130},{130,2},{3,131},{131,3},{4... | collective-permute-start | bytes 2408456 | tf_op jit(solution)/shard_map/weights/ppermute | solution.py:75
  17.3 10.0 %copy-start.11 = (bf16[16,56]{1,0:T(8,128)(2,1)S(1)}, bf16[16,56]{1,0:T(8,128)(2,1)}, u32[]{:S(2)}) copy-start(bf16[16,56]{1,0:T(8,128)(2,1)} %param.17) | copy-start | bytes 5380
  17.3 19.8 %all-to-all-start = ((bf16[16,2,928]{2,1,0:T(2,128)(2,1)}), bf16[16,2,928]{2,1,0:T(2,128)(2,1)S(1)}, u32[]{:S(2)}, u32[]{:S(2)}) async-start(bf16[16,2,928]{2,1,0:T(2,128)(2,1)} %reshape.451), calls=%async_computation | async-start | bytes 131072 | tf_op jit(solution)/shard_map/dispatch/all_to_all | solution.py:67
  42.2 10.9 %copy-start.14 = (f32[4,3,1792]{2,0,1:T(4,128)S(1)}, f32[4,3,1792]{2,0,1:T(4,128)}, u32[]{:S(2)}) copy-start(f32[4,3,1792]{2,0,1:T(4,128)} %param.12) | copy-start | bytes 258052
  42.2 35.1 %all-to-all-start.1 = ((bf16[32,72,128]{2,1,0:T(8,128)(2,1)}), bf16[32,72,128]{2,1,0:T(8,128)(2,1)S(1)}, u32[]{:S(2)}, u32[]{:S(2)}) async-start(bf16[32,72,128]{2,1,0:T(8,128)(2,1)} %concatenate.59), calls=%async_computation.1 | async-start | bytes 1179648 | tf_op jit(solution)/shard_map/dispatch/all_to_all | solution.py:67
  53.5 3.3 %copy-start.1 = (bf16[1792,224]{0,1:T(8,128)(2,1)}, bf16[1792,224]{0,1:T(8,128)(2,1)S(1)}, u32[]{:S(2)}) copy-start(bf16[1792,224]{0,1:T(8,128)(2,1)S(1)} %collective-permute-done.3) | copy-start | bytes 2408452
  53.5 18.9 %collective-permute-start.5 = (bf16[896,224]{0,1:T(8,128)(2,1)S(1)}, bf16[896,224]{0,1:T(8,128)(2,1)S(1)}, u32[]{:S(2)}, u32[]{:S(2)}) collective-permute-start(bf16[896,224]{0,1:T(8,128)(2,1)S(1)} %slice.157), channel_id=1, source_target_pairs={{0,128},{128,0},{1,129},{129,1},{2,130},{130,2},{3,131},{131,3},{4... | collective-permute-start | bytes 1204232 | tf_op jit(solution)/shard_map/weights/ppermute | solution.py:75
  56.7 16.6 %copy-start.4 = (bf16[1792,224]{0,1:T(8,128)(2,1)}, bf16[1792,224]{0,1:T(8,128)(2,1)S(1)}, u32[]{:S(2)}) copy-start(bf16[1792,224]{0,1:T(8,128)(2,1)S(1)} %collective-permute-done.1) | copy-start | bytes 2408452
  56.7 19.8 %collective-permute-start.6 = (bf16[896,224]{0,1:T(8,128)(2,1)S(1)}, bf16[896,224]{0,1:T(8,128)(2,1)S(1)}, u32[]{:S(2)}, u32[]{:S(2)}) collective-permute-start(bf16[896,224]{0,1:T(8,128)(2,1)S(1)} %slice.158), channel_id=1, source_target_pairs={{0,16},{16,0},{1,17},{17,1},{2,18},{18,2},{3,19},{19,3},{4,20},{20... | collective-permute-start | bytes 1204232 | tf_op jit(solution)/shard_map/weights/ppermute | solution.py:75
  78.0 6.7 %copy-start.23 = (f32[128]{0:T(128)}, f32[128]{0:T(128)S(1)}, u32[]{:S(2)}) copy-start(f32[128]{0:T(128)S(1)} %add_rsqrt_fusion) | copy-start | bytes 1540
  81.8 16.0 %collective-permute-start = (f32[16,224]{1,0:T(8,128)S(1)}, f32[16,224]{1,0:T(8,128)S(1)}, u32[]{:S(2)}, u32[]{:S(2)}) collective-permute-start(f32[16,224]{1,0:T(8,128)S(1)} %get-tuple-element.25), channel_id=1, source_target_pairs={{0,128},{128,0},{1,129},{129,1},{2,130},{130,2},{3,131},{131,3},{4... | collective-permute-start | bytes 43016 | tf_op jit(solution)/shard_map/projection/ppermute | solution.py:75
  84.8 1.1 copy-start.7
  86.3 12.3 %collective-permute-start.2 = (f32[16,224]{1,0:T(8,128)S(1)}, f32[16,224]{1,0:T(8,128)S(1)}, u32[]{:S(2)}, u32[]{:S(2)}) collective-permute-start(f32[16,224]{1,0:T(8,128)S(1)} %get-tuple-element.24), channel_id=1, source_target_pairs={{0,16},{16,0},{1,17},{17,1},{2,18},{18,2},{3,19},{19,3},{4,20},{20... | collective-permute-start | bytes 43016 | tf_op jit(solution)/shard_map/projection/ppermute | solution.py:75
  89.2 10.3 %collective-permute-start.4 = (f32[16,224]{1,0:T(8,128)S(1)}, f32[16,224]{1,0:T(8,128)S(1)}, u32[]{:S(2)}, u32[]{:S(2)}) collective-permute-start(f32[16,224]{1,0:T(8,128)S(1)} %get-tuple-element.23), channel_id=1, source_target_pairs={{0,144},{16,128},{128,16},{144,0},{1,145},{17,129},{129,17},{145,1... | collective-permute-start | bytes 43016 | tf_op jit(solution)/shard_map/projection/ppermute | solution.py:187
  92.6 3.0 %copy-start.5 = (bf16[1792,224]{0,1:T(8,128)(2,1)S(1)}, bf16[1792,224]{0,1:T(8,128)(2,1)}, u32[]{:S(2)}) copy-start(bf16[1792,224]{0,1:T(8,128)(2,1)} %copy-done.4) | copy-start | bytes 2408452
  94.9 1.2 copy-start.2
  97.7 26.2 %copy-start.25 = (f32[128]{0:T(128)}, f32[128]{0:T(128)S(1)}, u32[]{:S(2)}) copy-start(f32[128]{0:T(128)S(1)} %get-tuple-element.31) | copy-start | bytes 1540
  98.5 0.9 copy-start.9
  101.0 16.0 %all-to-all-start.2 = ((f32[8,16,128]{2,1,0:T(8,128)}), f32[8,16,128]{2,1,0:T(8,128)S(1)}, u32[]{:S(2)}, u32[]{:S(2)}) async-start(f32[8,16,128]{2,1,0:T(8,128)} %broadcast_in_dim.102), calls=%async_computation.2 | async-start | bytes 131072 | tf_op jit(solution)/shard_map/predict/all_to_all | solution.py:67
  117.6 16.0 %all-to-all-start.3 = ((bf16[16,16,128]{2,1,0:T(8,128)(2,1)}), bf16[16,16,128]{2,1,0:T(8,128)(2,1)S(1)}, u32[]{:S(2)}, u32[]{:S(2)}) async-start(bf16[16,16,128]{2,1,0:T(8,128)(2,1)} %broadcast_in_dim.103), calls=%async_computation.3 | async-start | bytes 131072 | tf_op jit(solution)/shard_map/predict/all_to_all | solution.py:67
  124.1 12.2 %copy-start.8 = (bf16[1,1792,224]{1,2,0:T(8,128)(2,1)S(1)}, bf16[1,1792,224]{1,2,0:T(8,128)(2,1)}, u32[]{:S(2)}) copy-start(bf16[1,1792,224]{1,2,0:T(8,128)(2,1)} %param.15) | copy-start | bytes 2408452
  137.4 1.6 copy-start.10
  137.4 1.6 copy-start.18
  137.4 2.0 %copy-start.16 = (f32[16,224]{1,0:T(8,128)S(1)}, f32[16,224]{1,0:T(8,128)}, u32[]{:S(2)}) copy-start(f32[16,224]{1,0:T(8,128)} %copy-done.15) | copy-start | bytes 43012
  139.0 1.1 copy-start.6
  140.1 1.1 copy-start.3
  140.1 1.1 copy-start.24
  145.8 4.3 %copy-start.32 = (s32[4]{0:T(128)S(1)}, s32[4]{0:T(128)}, u32[]{:S(2)}) copy-start(s32[4]{0:T(128)} %param.20) | copy-start | bytes 52
  145.8 19.3 %all-to-all-start.4 = ((bf16[32,64,128]{2,1,0:T(8,128)(2,1)}), bf16[32,64,128]{2,1,0:T(8,128)(2,1)S(1)}, u32[]{:S(2)}, u32[]{:S(2)}) async-start(bf16[32,64,128]{2,1,0:T(8,128)(2,1)} %pad_maximum_fusion), calls=%async_computation.4 | async-start | bytes 1048576 | tf_op jit(solution)/shard_map/backward/all_to_all | solution.py:67
  166.5 15.8 %all-to-all-start.5 = ((bf16[16,2,912]{2,1,0:T(2,128)(2,1)}), bf16[16,2,912]{2,1,0:T(2,128)(2,1)S(1)}, u32[]{:S(2)}, u32[]{:S(2)}) async-start(bf16[16,2,912]{2,1,0:T(2,128)(2,1)} %reshape.453), calls=%async_computation.5 | async-start | bytes 131072 | tf_op jit(solution)/shard_map/backward/all_to_all | solution.py:67
  (16 other events, 10.6 us)

commit v3 on v0

v3 whole, which is shorter than its diff:
```python
import functools
import math

import jax
import jax.numpy as jnp
from jax import lax
from jax.experimental import pallas as pl
from jax.experimental.pallas import tpu as pltpu
from jax.sharding import Mesh, PartitionSpec as P

D = 1792
TOPK = 2
C_OUT = 16
SAMPLES = 4
LANES = 128
FEAT = 56
SHARDS = 32
GROUPS = 16
CAP = 32
TOK = 256
HID = 224
PACK = 64
ROWS = 72
FSDP = ("yh", "yl", "zh", "zl")
QUAD = ("yl", "zl")
SHARERS = ("yh", "zh")


norm_eps = 1e-06
dpo_beta = 2.0
bf16 = jnp.bfloat16
f32 = jnp.float32
i32 = jnp.int32
highest = lax.Precision.HIGHEST
contract_last = (((1,), (1,)), ((), ()))
contract_first = (((0,), (0,)), ((), ()))


def dot(a, b, **kw):
    return jnp.dot(a, b, preferred_element_type=f32, **kw)


def dot_nt(a, b, **kw):
    return lax.dot_general(a, b, contract_last, preferred_element_type=f32, **kw)


def iota(shape, axis):
    return lax.broadcasted_iota(i32, shape, axis)


def high_low(values):
    high = values.astype(bf16).astype(f32)
    return high, values - high


def whole(weight):
    if isinstance(weight, tuple):
        return jnp.concatenate([part[...] for part in weight], axis=0)
    return weight[...]


def lane_blocks(tiles):
    block = iota(tiles[0].shape, 1) // CAP
    out = []
    for b in range(4):
        total = None
        for j in range(4):
            moved = tiles[j] if j == b else pltpu.roll(tiles[j], (CAP * (j - b)) % LANES, axis=1)
            total = moved if total is None else jnp.where(block == j, moved, total)
        out.append(total)
    return out


def routing_kernel(
    place_ref, tokens_ref, routes_ref, weights_ref, targets_ref, head_ref,
    sent_ref, pick_ref, base_ref, facts_ref,
):
    shard = place_ref[0]
    tokens = tokens_ref[...]
    expert = iota((GROUPS, TOK), 0)
    hits = [(routes_ref[k : k + 1, :] == expert).astype(f32) for k in range(TOPK)]
    below = (iota((TOK, TOK), 0) < iota((TOK, TOK), 1)).astype(bf16)
    earlier = dot((hits[0] + hits[1]).astype(bf16), below)
    slots = [jnp.sum(earlier * hit, axis=0, keepdims=True) for hit in hits]
    kept = [(slot < CAP).astype(f32) for slot in slots]
    lane = iota((GROUPS * CAP, TOK), 0)
    places = []
    for k in range(TOPK):
        dest = jnp.where(
            kept[k] > 0.5, routes_ref[k : k + 1, :] * CAP + slots[k].astype(i32), -1
        )
        places.append((lane == dest).astype(f32))
    pick_ref[...] = (places[0] + places[1]).astype(bf16)
    pick_ref.start()

    target_high, target_low = high_low(targets_ref[...])
    row = iota((PACK, LANES), 0)
    column = iota((PACK, LANES), 1)
    pick_fact = (row >= FEAT) & (row < FEAT + 2) & (column == 2 * shard + row - FEAT)
    pick_fact = pick_fact.astype(bf16)
    body = jnp.concatenate([tokens.astype(f32), jnp.zeros((PACK - FEAT, TOK), f32)], axis=0)
    packed = None
    for k in range(TOPK):
        other = 1 - k
        own = high_low(weights_ref[k : k + 1, :])
        partner = high_low(weights_ref[other : other + 1, :] * kept[other])
        first = jnp.ones((1, TOK), f32) if k == 0 else 1.0 - kept[0]
        facts = [
            own[0], own[1], partner[0], partner[1],
            routes_ref[other : other + 1, :].astype(f32) * kept[other],
            slots[other] * kept[other],
            first,
        ]
        line = iota((8, TOK), 0)
        table = jnp.zeros((8, TOK), f32)
        for place, fact in enumerate(facts):
            table = jnp.where(line == place, fact, table)
        table = jnp.concatenate(
            [target_high, target_low, table, jnp.zeros((LANES - 40, TOK), f32)], axis=0
        )
        features = body + dot(pick_fact, table.astype(bf16))
        part = dot_nt(features.astype(bf16), places[k].astype(bf16))
        packed = part if packed is None else packed + part
    for tile in range(4):
        pieces = [
            packed[16 * j : 16 * j + 16, tile * LANES : (tile + 1) * LANES] for j in range(4)
        ]
        for b, piece in enumerate(lane_blocks(pieces)):
            sent_ref[4 * tile + b] = piece.astype(bf16)

    base = dot(head_ref[...], tokens)
    lost = (1.0 - kept[0]) * (1.0 - kept[1])
    lost = jnp.broadcast_to(lost, (C_OUT, TOK))
    stack = jnp.concatenate([base, targets_ref[...], lost], axis=0).T
    stack = jnp.concatenate([stack, jnp.zeros((TOK, LANES - 3 * C_OUT), f32)], axis=1)
    group = iota((SHARDS, LANES), 1) // C_OUT
    for place in range(3):
        total = jnp.zeros((SHARDS, LANES), f32)
        for j in range(8):
            piece = stack[SHARDS * j : SHARDS * (j + 1)]
            shift = (C_OUT * (j - place)) % LANES
            piece = pltpu.roll(piece, shift, axis=1) if shift else piece
            total = jnp.where(group == j, piece, total)
        if place == 0:
            base_ref[...] = total
        else:
            facts_ref[place - 1] = total


def parcel_kernel(arrived_ref, base_ref, head_ref, parcel_ref):
    base_high, base_low = high_low(base_ref[...])
    row = iota((8, LANES), 0)
    head = head_ref[...].astype(f32)
    for q in range(4):
        tiles = lane_blocks([arrived_ref[4 * q + b].astype(f32) for b in range(4)])
        body = jnp.concatenate([tiles[0], tiles[1], tiles[2], tiles[3][:8]], axis=0)
        last = tiles[3][8:]
        for high in range(8):
            f = (high // 4) * 16 + (q // 2) * 8 + (high % 4) * 2 + q % 2
            tail = jnp.where(row == 2, base_high[f : f + 1], last)
            tail = jnp.where(row == 3, base_low[f : f + 1], tail)
            parcel_ref[f] = jnp.concatenate([body, tail, head], axis=0).astype(bf16)


def head_kernel(gathered_ref, gate_ref, w_out_ref, proj_ref, head_ref):
    pieces = []
    for f in range(SHARDS):
        rows = gathered_ref[f, PACK:ROWS].astype(f32)
        for i in range(FEAT // 8):
            pieces.append(jnp.broadcast_to(rows[i : i + 1], (8, LANES)))
    spread = jnp.concatenate(pieces, axis=0)
    lane = iota((D, LANES), 1)
    spread = jnp.where(lane // C_OUT == iota((D, LANES), 0) % 8, spread, 0.0).astype(bf16)
    fold = iota((LANES, LANES), 0) % C_OUT == iota((LANES, LANES), 1) % C_OUT
    head = dot(spread, fold.astype(bf16))
    head_ref[...] = head.astype(bf16)
    head_ref.start()
    high, low = high_low(head * gate_ref[...])
    pair = jnp.where(lane < PACK, high, low).astype(bf16)
    proj = dot(w_out_ref[...], pair)
    proj = proj + pltpu.roll(proj, PACK, axis=1)
    proj = proj.T
    for s in range(SAMPLES):
        proj_ref[s] = proj[C_OUT * s : C_OUT * (s + 1)]


def first_kernel(
    gathered_ref, mod_ref, w0_ref, w1_ref, w2_ref, w3_ref, w4_ref, act_ref, slope_ref, rows_ref
):
    rows = jnp.concatenate([gathered_ref[f, :FEAT].astype(f32) for f in range(SHARDS)], axis=0).T
    rows_ref[...] = rows.astype(bf16)
    rows_ref.start()
    rms = lax.rsqrt(jnp.sum(rows * rows, axis=1, keepdims=True) / D + norm_eps)
    normed = (rows * rms) * (1.0 + mod_ref[1:2, :]) + mod_ref[0:1, :]
    normed = normed.astype(bf16)
    weights = [w0_ref, w1_ref, w2_ref, (w3_ref, w4_ref)]
    for b, weight in enumerate(weights):
        pre = dot_nt(normed, whole(weight))
        cubic = math.sqrt(2.0 / math.pi)
        square = pre * pre
        tanh = jnp.tanh(cubic * (pre + 0.044715 * square * pre))
        half = 0.5 * (1.0 + tanh)
        act_ref[b] = (pre * half).astype(bf16)
        slope_ref[b] = half + 0.5 * pre * (1.0 - tanh * tanh) * (
            cubic * (1.0 + 3.0 * 0.044715 * square)
        )


def predict_kernel(place_ref, act_ref, proj_ref, part_ref):
    quarter = place_ref[1]
    total = None
    for b in range(4):
        high, low = high_low(proj_ref[quarter ^ b])
        pair = jnp.concatenate([high, low], axis=0).astype(bf16)
        part = dot_nt(pair, act_ref[b])
        total = part if total is None else total + part
    total = total[:C_OUT] + total[C_OUT:]
    for other in range(8):
        part_ref[other] = total


def own_kernel(parts_ref, own_ref, shared_ref):
    own = jnp.sum(parts_ref[...], axis=0)
    own_ref[...] = own
    for e in range(GROUPS):
        shared_ref[e] = own.astype(bf16)


def base_kernel(gathered_ref, rows_ref, head_ref, base_ref, facts_ref):
    base = dot(rows_ref[...], head_ref[...]).T
    base_ref[...] = base[:C_OUT]
    tails = [gathered_ref[f, FEAT:PACK].astype(f32) for f in range(SHARDS)]
    facts = jnp.concatenate([tail[:2] for tail in tails], axis=0)
    facts_ref[:PACK] = facts
    facts_ref[PACK:] = functools.reduce(jnp.add, tails)


def backward_kernel(
    place_ref, shared_ref, own_ref, base_ref, facts_ref, block_ref, proj_ref, slope_ref,
    mod_ref, head_ref, rows_ref, w0_ref, w1_ref, w2_ref, w3_ref, w4_ref, parcel_ref,
):
    shard, quarter, leader, sample = place_ref[0], place_ref[1], place_ref[2], place_ref[3]
    facts = facts_ref[...]
    target = facts[:C_OUT] + facts[C_OUT : 2 * C_OUT]
    own_w = facts[32:33] + facts[33:34]
    other_w = facts[34:35] + facts[35:36]
    first = facts[38:39]
    lane = iota((1, LANES), 1)
    source = facts[36:37].astype(i32) * LANES + facts[37:38].astype(i32) + lane // CAP * CAP
    chosen = (iota((GROUPS * LANES, LANES), 0) == source).astype(f32).astype(bf16)
    everyone = jnp.concatenate([shared_ref[e] for e in range(GROUPS)], axis=1)
    partner = dot(everyone, chosen)
    residue = base_ref[...] + own_w * own_ref[...] + other_w * partner - target
    kept_err = jnp.sum(first * residue * residue, keepdims=True)

    lost_base = facts[PACK + 2 : PACK + 3] + facts[PACK + 3 : PACK + 4]
    lost = (lost_base - block_ref[0, pl.ds(shard, 1), :]) * block_ref[1, pl.ds(shard, 1), :]
    lost_err = jnp.sum(lost * lost, keepdims=True)
    err = jnp.where((lane == quarter) & (leader == 1), kept_err, 0.0)
    err = err + jnp.where(lane == sample, lost_err, 0.0)
    row = iota((8, LANES), 0)
    tail = jnp.zeros((8, LANES), f32)
    for place, values in enumerate(high_low(lost) + high_low(err)):
        tail = jnp.where(row == place, values, tail)

    upstream = (own_w * residue).T
    weights = [w0_ref, w1_ref, w2_ref, (w3_ref, w4_ref)]
    total = None
    for b, weight in enumerate(weights):
        grad = slope_ref[b] * dot(upstream, proj_ref[quarter ^ b], precision=highest)
        part = dot(grad.astype(bf16), whole(weight))
        total = part if total is None else total + part
    rows = rows_ref[...].astype(f32)
    rms = lax.rsqrt(jnp.sum(rows * rows, axis=1, keepdims=True) / D + norm_eps)
    total = total * (rms * (1.0 + mod_ref[1:2, :]))
    inner = jnp.sum(total * rows, axis=1, keepdims=True) * (rms * rms / D)
    high, low = high_low(first * residue * 0.125)
    direct = jnp.concatenate([high, low, jnp.zeros((LANES - 2 * C_OUT, LANES), f32)], axis=0)
    total = total - rows * inner + dot_nt(direct.T.astype(bf16), head_ref[...])
    total = total.T
    for f in range(SHARDS):
        parcel_ref[f] = jnp.concatenate(
            [total[FEAT * f : FEAT * (f + 1)], tail], axis=0
        ).astype(bf16)


def mid_kernel(parcel_ref, home_ref, lost_ref):
    lane = iota((1, LANES), 1)
    row = iota((8, LANES), 0)
    sums, tails = [], []
    for q in range(4):
        total = None
        for high in range(8):
            f = (high // 4) * 16 + (q // 2) * 8 + (high % 4) * 2 + q % 2
            part = parcel_ref[f].astype(f32)
            lost_ref[0, f : f + 1] = part[FEAT : FEAT + 1]
            lost_ref[1, f : f + 1] = part[FEAT + 1 : FEAT + 2]
            total = part if total is None else total + part
        sums.append(total[:FEAT])
        tails.append(total[FEAT:])
    tail = tails[0] + tails[1] + tails[2] + tails[3]
    err = jnp.where(lane < SAMPLES, tail[2:3] + tail[3:4], 0.0)
    err = err + pltpu.roll(err, CAP, axis=1)
    err = err + pltpu.roll(err, 2 * CAP, axis=1)
    high, low = high_low(err)
    tail = jnp.where(row == 0, high, 0.0) + jnp.where(row == 1, low, 0.0)
    for q in range(4):
        full = jnp.concatenate([sums[q], tail], axis=0)
        tiles = lane_blocks([full[16 * j : 16 * j + 16] for j in range(4)])
        for b in range(4):
            home_ref[4 * q + b] = tiles[b].astype(bf16)


def end_kernel(
    place_ref, levels_ref, home_ref, pick_ref, lost_ref, head_ref,
    grad_ref, loss_ref,
):
    sample = place_ref[3]
    pairs = [place_ref[4 + i] for i in range(SAMPLES)]
    columns = []
    for tile in range(4):
        tiles = lane_blocks([home_ref[4 * tile + b].astype(f32) for b in range(4)])
        columns.append(jnp.concatenate(tiles, axis=0))
    home = jnp.concatenate(columns, axis=1)
    back = dot(home.astype(bf16), pick_ref[...])
    err = functools.reduce(jnp.add, [column[FEAT : FEAT + 1] for column in columns])
    err = err + functools.reduce(jnp.add, [column[FEAT + 1 : FEAT + 2] for column in columns])
    err = jnp.broadcast_to(err, (8, LANES)) / (TOK * GROUPS // SAMPLES * C_OUT)
    lane = iota((8, LANES), 1) % CAP
    excess = []
    for s in range(SAMPLES):
        total = jnp.sum(jnp.where(lane == s, err, 0.0), axis=1, keepdims=True)
        excess.append(jnp.broadcast_to(total, (8, LANES)) - levels_ref[s])
    loss, coef = 0.0, 0.0
    for k in range(2):
        winner, loser = pairs[2 * k], pairs[2 * k + 1]
        margin = 0.0
        for s in range(SAMPLES):
            margin = margin + jnp.where(winner == s, excess[s], 0.0)
        for s in range(SAMPLES):
            margin = margin - jnp.where(loser == s, excess[s], 0.0)
        down = levels_ref[SAMPLES + k] * margin
        loss = loss + jnp.maximum(down, 0.0) + jnp.log1p(jnp.exp(-jnp.abs(down)))
        rate = levels_ref[SAMPLES + k] / (1.0 + jnp.exp(-down)) * 0.5
        coef = coef + jnp.where(winner == sample, rate, 0.0)
        coef = coef - jnp.where(loser == sample, rate, 0.0)
    loss_ref[...] = loss[0:1, 0:1] * 0.5
    lane = iota((SHARDS, LANES), 1) // C_OUT
    head_tile = jnp.concatenate([head_ref[...]] * 8, axis=0).astype(f32).T.astype(bf16)
    direct = 0.0
    for part in range(2):
        lost = [jnp.where(lane == j, lost_ref[part], 0.0) for j in range(8)]
        direct = direct + dot_nt(head_tile, jnp.concatenate(lost, axis=0).astype(bf16))
    coef = coef[0:1, 0:1] * (TOK * GROUPS * C_OUT * 2.0 / (TOK * GROUPS // SAMPLES * C_OUT))
    grad_ref[...] = (coef * (direct + back[:FEAT])).astype(bf16)


class Fetched:
    def __init__(self, source, held, semaphore):
        self.held = held
        self.copy = pltpu.make_async_copy(source, held, semaphore)
        self.copy.start()

    def wait(self):
        if self.copy is not None:
            self.copy.wait()
            self.copy = None

    def __getitem__(self, index):
        self.wait()
        return self.held[index]


class Stored:
    def __init__(self, target, held, semaphore):
        self.held = held
        self.copy = pltpu.make_async_copy(held, target, semaphore)
        self.started = False

    def __setitem__(self, index, values):
        self.held[index] = values

    def start(self):
        if not self.started:
            self.copy.start()
            self.started = True

    def wait(self):
        self.copy.wait()


def call(kernel, scalars, arrays, outs, fetch=(), store=(), flops=0):
    vmem = pl.BlockSpec(memory_space=pltpu.VMEM)
    smem = pl.BlockSpec(memory_space=pltpu.SMEM)
    hbm = pl.BlockSpec(memory_space=pltpu.HBM)
    size = sum(a.size * a.dtype.itemsize for a in arrays)
    out_shape = [
        pltpu.HBM(shape, dtype) if i in store else jax.ShapeDtypeStruct(shape, dtype)
        for i, (shape, dtype) in enumerate(outs)
    ]
    arrays = [
        pltpu.with_memory_space_constraint(a, pltpu.HBM) if i in fetch else a
        for i, a in enumerate(arrays)
    ]
    moved = [arrays[i] for i in fetch] + [out_shape[i] for i in store]
    scratch = [pltpu.VMEM(a.shape, a.dtype) for a in moved]
    if moved:
        scratch.append(pltpu.SemaphoreType.DMA((len(moved),)))

    def body(*refs):
        refs = list(refs)
        at_in = len(scalars)
        at_out = at_in + len(arrays)
        at_held = at_out + len(outs)
        fetched, stored = [], []
        for n, i in enumerate(fetch):
            fetched.append(Fetched(refs[at_in + i], refs[at_held + n], refs[-1].at[n]))
            refs[at_in + i] = fetched[-1]
        for n, i in enumerate(store, len(fetch)):
            stored.append(Stored(refs[at_out + i], refs[at_held + n], refs[-1].at[n]))
            refs[at_out + i] = stored[-1]
        kernel(*refs[:at_held])
        for item in stored:
            item.start()
        for item in fetched + stored:
            item.wait()

    return pl.pallas_call(
        body,
        out_shape=out_shape,
        in_specs=[smem] * len(scalars)
        + [hbm if i in fetch else vmem for i in range(len(arrays))],
        out_specs=[hbm if i in store else vmem for i in range(len(outs))],
        scratch_shapes=scratch,
        compiler_params=pltpu.CompilerParams(vmem_limit_bytes=24 * 1024 * 1024),
        cost_estimate=pl.CostEstimate(flops=flops, bytes_accessed=size, transcendentals=0),
    )(*scalars, *arrays)


def swap(chunks, axis):
    return lax.all_to_all(chunks, axis, split_axis=0, concat_axis=0, tiled=True)


def local(
    tokens,
    modulation,
    routes,
    route_weights,
    w_first,
    w_second,
    head,
    targets,
    ref_err,
    pair_ids,
    timesteps,
):
    shard = lax.axis_index(FSDP)
    quarter = lax.axis_index(QUAD)
    leader = (lax.axis_index(SHARERS) == 0).astype(i32)
    my_sample = lax.axis_index("expert") * SAMPLES // GROUPS
    place = jnp.concatenate([jnp.stack([shard, quarter, leader, my_sample]).astype(i32), pair_ids])
    fraction = timesteps.astype(f32) / 1000.0
    keep_level = jnp.cos((fraction + 0.008) / 1.008 * (math.pi / 2.0)) ** 2
    levels = jnp.concatenate([ref_err, dpo_beta * keep_level])
    w_in = w_first[0].T

    with jax.named_scope("weights"):
        swap_pair = [(0, 1), (1, 0)]
        w_z = lax.ppermute(w_in, "zl", swap_pair)
        w_y = lax.ppermute(w_in, "yl", swap_pair)

    with jax.named_scope("routing"):
        sent, pick, base, block = call(
            routing_kernel,
            [place],
            [tokens.T, routes.T, route_weights.T, targets.T, head],
            [
                ((GROUPS, 16, LANES), bf16),
                ((GROUPS * CAP, TOK), bf16),
                ((SHARDS, LANES), f32),
                ((2, SHARDS, LANES), f32),
            ],
            store=(1, 3),
        )
    with jax.named_scope("dispatch"):
        arrived = swap(sent, "expert")
        half = HID // 2
        weights = [w_in, w_z, w_y]
        weights.append(lax.ppermute(w_z[:half], "yl", swap_pair))
        weights.append(lax.ppermute(w_y[half:], "zl", swap_pair))
        head_flat = jnp.pad(head.T.reshape(FEAT // 8, LANES), ((0, 1), (0, 0)))
        (parcel,) = call(
            parcel_kernel, [], [arrived, base, head_flat], [((SHARDS, ROWS, LANES), bf16)]
        )
        gathered = swap(parcel, FSDP)

    with jax.named_scope("projection"):
        gate = jnp.tile(jnp.repeat(modulation[:, 2].T, C_OUT, axis=1), (1, 2))
        proj, head_all = call(
            head_kernel,
            [],
            [gathered, gate, w_second[0]],
            [((SAMPLES, C_OUT, HID), f32), ((D, LANES), bf16)],
            fetch=(2,),
            store=(0, 1),
        )
        proj = swap(proj, QUAD)

    with jax.named_scope("first_layer"):
        mod = lax.dynamic_index_in_dim(modulation, quarter, 0, keepdims=False)
        act, slope, rows = call(
            first_kernel,
            [],
            [gathered, mod] + weights,
            [((4, LANES, HID), bf16), ((4, LANES, HID), f32), ((LANES, D), bf16)],
            fetch=(2, 3, 4, 5, 6),
            store=(0, 1, 2),
            flops=8 * D * HID * LANES,
        )

    with jax.named_scope("predict"):
        (part,) = call(
            predict_kernel, [place], [act, proj], [((8, C_OUT, LANES), f32)], fetch=(0,)
        )
        parts = swap(part, SHARERS)
        own, shared = call(
            own_kernel, [], [parts], [((C_OUT, LANES), f32), ((GROUPS, C_OUT, LANES), bf16)],
            store=(0,),
        )
        base_rows, facts = call(
            base_kernel, [], [gathered, rows, head_all], [((C_OUT, LANES), f32), ((72, LANES), f32)],
            fetch=(1, 2),
            store=(0, 1),
        )
        shared = swap(shared, "expert")

    with jax.named_scope("backward"):
        (parcel,) = call(
            backward_kernel,
            [place],
            [shared, own, base_rows, facts, block, proj, slope, mod, head_all, rows]
            + weights,
            [((SHARDS, PACK, LANES), bf16)],
            fetch=tuple(range(1, 15)),
            flops=8 * D * HID * LANES,
        )
        parcel = swap(parcel, FSDP)
        home, lost = call(
            mid_kernel, [], [parcel], [((GROUPS, 16, LANES), bf16), ((2, SHARDS, LANES), f32)],
            store=(1,),
        )
        home = swap(home, "expert")

    with jax.named_scope("finish"):
        grad_tokens, loss = call(
            end_kernel,
            [place, levels],
            [home, pick, lost, head],
            [((FEAT, TOK), bf16), ((1, 1), f32)],
            fetch=(1, 2),
        )
    return (grad_tokens.T, loss.reshape(()))


def solution(mesh):
    mesh = Mesh(mesh.devices.reshape(2, 2, 4, 2, 16), FSDP + ("expert",))
    in_specs = (
        P("expert", FSDP),
        P(),
        P("expert", None),
        P("expert", None),
        P("expert", None, FSDP),
        P("expert", FSDP, None),
        P(None, FSDP),
        P("expert", None),
        P(),
        P(),
        P(),
    )
    out_specs = (P("expert", FSDP), P())
    return jax.shard_map(local, mesh=mesh, in_specs=in_specs, out_specs=out_specs, check_vma=False)
```

time: 1100 us -> 156 us (0.14)
  waiting for transfers between devices: 578 us -> 33 us
  blocking collectives: 371 us -> 33.3 us
  local copies, waits for them, and re-layouts: 46.4 us -> 5.21 us
  Pallas kernels: 0 us -> 24.5 us
  between operations: 15.8 us -> 1.01 us
  matrix products: 11.3 us -> 0 us
    psum x4 -> x0, blocking collectives: 327 us -> none  [the longest x1 121 us: local(): prediction = lax.psum(pred_part, 'fsdp')]
    unnamed x6 -> x0, waiting for transfers between devices: 313 us -> none
    all_gather x2 -> x0, waiting for transfers between devices: 247 us -> none  [the longest x1 124 us: local(): lax.all_gather(arrived.reshape(slot_total, feat_dev), 'fsdp', axis=1, til...]
    unnamed x39 -> x31, local copies, waits for them, and re-layouts: 43.6 us -> 2.84 us
    pallas_call x0 -> x10, Pallas kernels: none -> 24.5 us  [call(): pl.pallas_call(body, out_shape=out_shape, in_specs=[smem] * len(scalars)...]
    all_to_all x2 -> x5, starting transfers between devices: 61.7 us -> 44.8 us  [swap(): return lax.all_to_all(chunks, axis, split_axis=0, concat_axis=0, tiled=True)]
    all_to_all x2 -> x5, waiting for transfers between devices: 18.6 us -> 33 us  [swap(): return lax.all_to_all(chunks, axis, split_axis=0, concat_axis=0, tiled=True)]
    ppermute x0 -> x4, starting transfers between devices: none -> 13.3 us  [the longest x1 4 us: local(): w_z = lax.ppermute(w_in, 'zl', swap_pair)]
  transfers between devices with their start and end apart: 6 -> 9, of which waited for: 6 -> 4; matrix products, arithmetic and copies ran while one was open for 0% -> 2% of each run, Pallas kernels for 0% -> 7%
where the time goes in v3:
time: 156 us; the launch traced here: 155 us
  starting transfers between devices  58.1 us (37%)
  blocking collectives  33.3 us (21%)
  waiting for transfers between devices  33 us (21%)
  Pallas kernels  24.5 us (16%)
  local copies, waits for them, and re-layouts  5.21 us (3%)
    all_to_all x5, starting transfers between devices, swap(): return lax.all_to_all(chunks, axis, split_axis=0, concat_axis=0, tiled=True)  44.8 us
    all_to_all x2, blocking collectives, swap(): return lax.all_to_all(chunks, axis, split_axis=0, concat_axis=0, tiled=True)  33.3 us
    all_to_all x5, waiting for transfers between devices, swap(): return lax.all_to_all(chunks, axis, split_axis=0, concat_axis=0, tiled=True)  33 us
    pallas_call x10, Pallas kernels, call(): pl.pallas_call(body, out_shape=out_shape, in_specs=[smem] * len(scalars)...  24.5 us
    ppermute x1, starting transfers between devices, local(): w_z = lax.ppermute(w_in, 'zl', swap_pair)  4 us
    ppermute x1, starting transfers between devices, local(): weights.append(lax.ppermute(w_y[half:], 'zl', swap_pair))  4 us
  transfers between devices with their start and end apart: 9, of which 4 were waited for; matrix products, arithmetic and copies ran while one was open for 2% of the time, Pallas kernels for 7%

profile of v3, /device:TPU:1, one launch (start us, length us, event | category | flops | bytes accessed | tf_op | source)
XLA Modules:
  0.0 155.2 jit_solution(13386335825872158197)
XLA Ops:
  0.7 0.6 copy-done.12
  1.4 0.6 copy-done.6
  2.1 2.6 %routing.1 = (bf16[16,16,128]{2,1,0:T(8,128)(2,1)}, bf16[512,256]{1,0:T(8,128)(2,1)}, f32[32,128]{1,0:T(8,128)S(1)}, f32[2,32,128]{2,1,0:T(8,128)}) custom-call(s32[8]{0:T(128)S(1)} %concatenate.6.refs_0_, bf16[56,256]{1,0:T(8,128)(2,1)S(1)} %bitcast.27, s32[2,256]{1,0:T(2,128)S(1)} %bitcast.29, f32[2,256]{1,0:T(2,128)S(1)} %bitcast.30, ...), custom_call_target="tpu_custom_call" | custom-call | bytes 50944 | tf_op jit(solution)/shard_map/routing/pallas_call | solution.py:428
  4.8 11.1 %all-to-all-start = ((bf16[16,16,128]{2,1,0:T(8,128)(2,1)}), bf16[16,16,128]{2,1,0:T(8,128)(2,1)S(1)}, u32[]{:S(2)}, u32[]{:S(2)}) async-start(bf16[16,16,128]{2,1,0:T(8,128)(2,1)} %get-tuple-element.19), calls=%async_computation | async-start | bytes 131072 | tf_op jit(solution)/shard_map/dispatch/all_to_all | solution.py:441
  15.9 2.3 %collective-permute-start.1 = (bf16[224,1792]{1,0:T(8,128)(2,1)}, bf16[224,1792]{1,0:T(8,128)(2,1)S(1)}, u32[]{:S(2)}, u32[]{:S(2)}) collective-permute-start(bf16[224,1792]{1,0:T(8,128)(2,1)} %bitcast.32), channel_id=1, source_target_pairs={{0,128},{128,0},{1,129},{129,1},{2,130},{130,2},{3,131},{131,3},{4... | collective-permute-start | bytes 2408456 | tf_op jit(solution)/shard_map/weights/ppermute | solution.py:470
  18.2 4.0 %collective-permute-start = (bf16[224,1792]{1,0:T(8,128)(2,1)}, bf16[224,1792]{1,0:T(8,128)(2,1)S(1)}, u32[]{:S(2)}, u32[]{:S(2)}) collective-permute-start(bf16[224,1792]{1,0:T(8,128)(2,1)} %bitcast.33), channel_id=1, source_target_pairs={{0,16},{16,0},{1,17},{17,1},{2,18},{18,2},{3,19},{19,3},{4,20},{20... | collective-permute-start | bytes 2408456 | tf_op jit(solution)/shard_map/weights/ppermute | solution.py:469
  22.4 3.2 %all-to-all-done.refs_0_ = bf16[16,16,128]{2,1,0:T(8,128)(2,1)S(1)} async-done(((bf16[16,16,128]{2,1,0:T(8,128)(2,1)}), bf16[16,16,128]{2,1,0:T(8,128)(2,1)S(1)}, u32[]{:S(2)}, u32[]{:S(2)}) %all-to-all-start) | async-done | bytes 65568 | tf_op jit(solution)/shard_map/dispatch/all_to_all | solution.py:441
  25.6 1.0 dispatch.1
  26.6 10.9 %all-to-all-start.1 = ((bf16[32,72,128]{2,1,0:T(8,128)(2,1)}), bf16[32,72,128]{2,1,0:T(8,128)(2,1)S(1)}, u32[]{:S(2)}, u32[]{:S(2)}) async-start(bf16[32,72,128]{2,1,0:T(8,128)(2,1)} %dispatch.1), calls=%async_computation.1 | async-start | bytes 1179648 | tf_op jit(solution)/shard_map/dispatch/all_to_all | solution.py:441
  37.5 0.8 slice.13
  38.4 4.0 %collective-permute-start.3 = (bf16[112,1792]{1,0:T(8,128)(2,1)}, bf16[112,1792]{1,0:T(8,128)(2,1)S(1)}, u32[]{:S(2)}, u32[]{:S(2)}) collective-permute-start(bf16[112,1792]{1,0:T(8,128)(2,1)} %slice.13), channel_id=1, source_target_pairs={{0,16},{16,0},{1,17},{17,1},{2,18},{18,2},{3,19},{19,3},{4,20},{20... | collective-permute-start | bytes 1204232 | tf_op jit(solution)/shard_map/dispatch/ppermute | solution.py:490
  42.4 0.8 slice.12
  43.2 3.0 %collective-permute-start.2 = (bf16[112,1792]{1,0:T(8,128)(2,1)}, bf16[112,1792]{1,0:T(8,128)(2,1)S(1)}, u32[]{:S(2)}, u32[]{:S(2)}) collective-permute-start(bf16[112,1792]{1,0:T(8,128)(2,1)} %slice.12), channel_id=1, source_target_pairs={{0,128},{128,0},{1,129},{129,1},{2,130},{130,2},{3,131},{131,3},{4... | collective-permute-start | bytes 1204232 | tf_op jit(solution)/shard_map/dispatch/ppermute | solution.py:489
  46.4 0.3 copy.16.refs_1_
  46.7 13.1 %all-to-all-done.1.refs_0_ = bf16[32,72,128]{2,1,0:T(8,128)(2,1)S(1)} async-done(((bf16[32,72,128]{2,1,0:T(8,128)(2,1)}), bf16[32,72,128]{2,1,0:T(8,128)(2,1)S(1)}, u32[]{:S(2)}, u32[]{:S(2)}) %all-to-all-start.1) | async-done | bytes 589856 | tf_op jit(solution)/shard_map/dispatch/all_to_all | solution.py:441
  59.8 2.3 %projection.1 = (f32[4,16,224]{2,1,0:T(8,128)}, bf16[1792,128]{1,0:T(8,128)(2,1)}) custom-call(bf16[32,72,128]{2,1,0:T(8,128)(2,1)S(1)} %all-to-all-done.1.refs_0_, f32[1792,128]{1,0:T(8,128)S(1)} %copy.16.refs_1_, bf16[224,1792]{1,0:T(8,128)(2,1)} %bitcast.37), custom_call_target="tpu_custom_call" | custom-call | bytes 2310144 | tf_op jit(solution)/shard_map/projection/pallas_call | solution.py:428
  62.2 3.3 %all-to-all-start.2 = ((f32[4,16,224]{2,1,0:T(8,128)}), f32[4,16,224]{2,1,0:T(8,128)S(1)}, u32[]{:S(2)}, u32[]{:S(2)}) async-start(f32[4,16,224]{2,1,0:T(8,128)} %get-tuple-element.22), calls=%async_computation.2 | async-start | bytes 131072 | tf_op jit(solution)/shard_map/projection/all_to_all | solution.py:441
  65.6 0.7 copy-done.9
  66.4 4.7 %first_layer.1 = (bf16[4,128,224]{2,1,0:T(8,128)(2,1)}, f32[4,128,224]{2,1,0:T(8,128)}, bf16[128,1792]{1,0:T(8,128)(2,1)}) custom-call(bf16[32,72,128]{2,1,0:T(8,128)(2,1)S(1)} %all-to-all-done.1.refs_0_, f32[3,1792]{1,0:T(4,128)S(1)} %bitcast.24, bf16[224,1792]{1,0:T(8,128)(2,1)} %bitcast.34, bf16[224,1792]{1,0:T(8,128)(2,1)} %copy-done.8, ...), custom_call_target="tpu_custom_call" | custom-call | flops 411041792 | bytes 3822592 | tf_op jit(solution)/shard_map/first_layer/pallas_call | solution.py:428
  71.1 1.7 %predict.3 = f32[8,16,128]{2,1,0:T(8,128)S(1)} custom-call(s32[8]{0:T(128)S(1)} %concatenate.6.refs_0_, bf16[4,128,224]{2,1,0:T(8,128)(2,1)} %get-tuple-element.21.refs_1_, f32[4,16,224]{2,1,0:T(8,128)S(1)} %all-to-all-done.2.refs_2_.refs_6_), custom_call_target="tpu_custom_call" | custom-call | bytes 286720 | tf_op jit(solution)/shard_map/predict/pallas_call | solution.py:428
  72.8 15.2 %all_to_all.35.refs_0_ = f32[8,16,128]{2,1,0:T(8,128)S(1)} all-to-all(f32[8,16,128]{2,1,0:T(8,128)S(1)} %predict.3), channel_id=1, replica_groups=mesh['yh'=2,'yl'=2,'zh'=4,'zl'=2,'expert'=16] {'yh','zh'}, dimensions={0} | all-to-all | bytes 131072 | tf_op jit(solution)/shard_map/predict/all_to_all | solution.py:441
  88.0 1.2 predict.4
  89.2 13.6 %all-to-all-start.4 = ((bf16[16,16,128]{2,1,0:T(8,128)(2,1)}), bf16[16,16,128]{2,1,0:T(8,128)(2,1)S(1)}, u32[]{:S(2)}, u32[]{:S(2)}) async-start(bf16[16,16,128]{2,1,0:T(8,128)(2,1)} %get-tuple-element.23), calls=%async_computation.4 | async-start | bytes 131072 | tf_op jit(solution)/shard_map/predict/all_to_all | solution.py:441
  102.9 2.1 %predict.5 = (f32[16,128]{1,0:T(8,128)}, f32[72,128]{1,0:T(8,128)}) custom-call(bf16[32,72,128]{2,1,0:T(8,128)(2,1)S(1)} %all-to-all-done.1.refs_0_, bf16[128,1792]{1,0:T(8,128)(2,1)} %get-tuple-element.25.refs_1_.refs_10_, bf16[1792,128]{1,0:T(8,128)(2,1)} %get-tuple-element.26.refs_2_.refs_9_), custom_call_target="tpu_custom_call" | custom-call | bytes 1507328 | tf_op jit(solution)/shard_map/predict/pallas_call | solution.py:428
  105.0 7.6 %all-to-all-done.4.refs_1_ = bf16[16,16,128]{2,1,0:T(8,128)(2,1)S(1)} async-done(((bf16[16,16,128]{2,1,0:T(8,128)(2,1)}), bf16[16,16,128]{2,1,0:T(8,128)(2,1)S(1)}, u32[]{:S(2)}, u32[]{:S(2)}) %all-to-all-start.4) | async-done | bytes 65568 | tf_op jit(solution)/shard_map/predict/all_to_all | solution.py:441
  112.6 4.9 %backward.2 = bf16[32,64,128]{2,1,0:T(8,128)(2,1)S(1)} custom-call(s32[8]{0:T(128)S(1)} %concatenate.6.refs_0_, bf16[16,16,128]{2,1,0:T(8,128)(2,1)S(1)} %all-to-all-done.4.refs_1_, f32[16,128]{1,0:T(8,128)} %get-tuple-element.24.refs_2_, f32[16,128]{1,0:T(8,128)} %get-tuple-element.27.refs_3_, f32[72,128]{1,0:T(8,128)} %get-tuple-element.28.refs_4_, ...), custom_call_target="tpu_custom_call" | custom-call | flops 411041792 | bytes 4817920 | tf_op jit(solution)/shard_map/backward/pallas_call | solution.py:428
  117.5 18.1 %all_to_all.36.refs_0_ = bf16[32,64,128]{2,1,0:T(8,128)(2,1)S(1)} all-to-all(bf16[32,64,128]{2,1,0:T(8,128)(2,1)S(1)} %backward.2), channel_id=1, replica_groups=mesh['yh'=2,'yl'=2,'zh'=4,'zl'=2,'expert'=16] {'yh','yl','zh','zl'}, dimensions={0} | all-to-all | bytes 1048576 | tf_op jit(solution)/shard_map/backward/all_to_all | solution.py:441
  135.6 1.4 backward.3
  137.0 5.9 %all-to-all-start.6 = ((bf16[16,16,128]{2,1,0:T(8,128)(2,1)}), bf16[16,16,128]{2,1,0:T(8,128)(2,1)S(1)}, u32[]{:S(2)}, u32[]{:S(2)}) async-start(bf16[16,16,128]{2,1,0:T(8,128)(2,1)} %get-tuple-element.31), calls=%async_computation.6 | async-start | bytes 131072 | tf_op jit(solution)/shard_map/backward/all_to_all | solution.py:441
  143.0 0.6 copy-done.14
  143.6 9.1 %all-to-all-done.6.refs_2_ = bf16[16,16,128]{2,1,0:T(8,128)(2,1)S(1)} async-done(((bf16[16,16,128]{2,1,0:T(8,128)(2,1)}), bf16[16,16,128]{2,1,0:T(8,128)(2,1)S(1)}, u32[]{:S(2)}, u32[]{:S(2)}) %all-to-all-start.6) | async-done | bytes 65568 | tf_op jit(solution)/shard_map/backward/all_to_all | solution.py:441
  152.7 2.5 %finish.1 = (bf16[56,256]{1,0:T(8,128)(2,1)}, f32[1,1]{1,0:T(1,128)}) custom-call(s32[8]{0:T(128)S(1)} %concatenate.6.refs_0_, f32[6]{0:T(128)S(1)} %pad_maximum_fusion.refs_1_, bf16[16,16,128]{2,1,0:T(8,128)(2,1)S(1)} %all-to-all-done.6.refs_2_, bf16[512,256]{1,0:T(8,128)(2,1)} %get-tuple-element.32.refs_3_, f32[2,32,128]{2,1,0:T(8,128)} %get-tuple-element.33.refs_4_, ...), custom_call_target="tpu_custom_call" | custom-call | bytes 362240 | tf_op jit(solution)/shard_map/finish/pallas_call | solution.py:428
  (42 shorter events, 0.8 us)
Async XLA Ops:
  0.6 0.8 copy-start.3
  0.7 0.8 copy-start.4
  0.7 0.7 copy-start.12
  1.3 0.7 copy-start.6
  1.4 0.7 copy-start.2
  1.4 0.7 copy-start.5
  4.8 20.8 %all-to-all-start = ((bf16[16,16,128]{2,1,0:T(8,128)(2,1)}), bf16[16,16,128]{2,1,0:T(8,128)(2,1)S(1)}, u32[]{:S(2)}, u32[]{:S(2)}) async-start(bf16[16,16,128]{2,1,0:T(8,128)(2,1)} %get-tuple-element.19), calls=%async_computation | async-start | bytes 131072 | tf_op jit(solution)/shard_map/dispatch/all_to_all | solution.py:441
  15.9 21.6 %collective-permute-start.1 = (bf16[224,1792]{1,0:T(8,128)(2,1)}, bf16[224,1792]{1,0:T(8,128)(2,1)S(1)}, u32[]{:S(2)}, u32[]{:S(2)}) collective-permute-start(bf16[224,1792]{1,0:T(8,128)(2,1)} %bitcast.32), channel_id=1, source_target_pairs={{0,128},{128,0},{1,129},{129,1},{2,130},{130,2},{3,131},{131,3},{4... | collective-permute-start | bytes 2408456 | tf_op jit(solution)/shard_map/weights/ppermute | solution.py:470
  18.2 24.2 %collective-permute-start = (bf16[224,1792]{1,0:T(8,128)(2,1)}, bf16[224,1792]{1,0:T(8,128)(2,1)S(1)}, u32[]{:S(2)}, u32[]{:S(2)}) collective-permute-start(bf16[224,1792]{1,0:T(8,128)(2,1)} %bitcast.33), channel_id=1, source_target_pairs={{0,16},{16,0},{1,17},{17,1},{2,18},{18,2},{3,19},{19,3},{4,20},{20... | collective-permute-start | bytes 2408456 | tf_op jit(solution)/shard_map/weights/ppermute | solution.py:469
  26.6 33.3 %all-to-all-start.1 = ((bf16[32,72,128]{2,1,0:T(8,128)(2,1)}), bf16[32,72,128]{2,1,0:T(8,128)(2,1)S(1)}, u32[]{:S(2)}, u32[]{:S(2)}) async-start(bf16[32,72,128]{2,1,0:T(8,128)(2,1)} %dispatch.1), calls=%async_computation.1 | async-start | bytes 1179648 | tf_op jit(solution)/shard_map/dispatch/all_to_all | solution.py:441
  37.5 8.8 %copy-start.7 = (bf16[224,1792]{1,0:T(8,128)(2,1)}, bf16[224,1792]{1,0:T(8,128)(2,1)S(1)}, u32[]{:S(2)}) copy-start(bf16[224,1792]{1,0:T(8,128)(2,1)S(1)} %collective-permute-done.1.refs_4_.refs_13_) | copy-start | bytes 2408452
  38.4 7.9 %copy-start.11 = (f32[4,3,1792]{2,0,1:T(4,128)S(1)}, f32[4,3,1792]{2,0,1:T(4,128)}, u32[]{:S(2)}) copy-start(f32[4,3,1792]{2,0,1:T(4,128)} %param.12) | copy-start | bytes 258052
  38.4 27.2 %collective-permute-start.3 = (bf16[112,1792]{1,0:T(8,128)(2,1)}, bf16[112,1792]{1,0:T(8,128)(2,1)S(1)}, u32[]{:S(2)}, u32[]{:S(2)}) collective-permute-start(bf16[112,1792]{1,0:T(8,128)(2,1)} %slice.13), channel_id=1, source_target_pairs={{0,16},{16,0},{1,17},{17,1},{2,18},{18,2},{3,19},{19,3},{4,20},{20... | collective-permute-start | bytes 1204232 | tf_op jit(solution)/shard_map/dispatch/ppermute | solution.py:490
  42.4 4.0 %copy-start.8 = (bf16[224,1792]{1,0:T(8,128)(2,1)}, bf16[224,1792]{1,0:T(8,128)(2,1)S(1)}, u32[]{:S(2)}) copy-start(bf16[224,1792]{1,0:T(8,128)(2,1)S(1)} %collective-permute-done.refs_3_.refs_12_) | copy-start | bytes 2408452
  43.2 22.3 %collective-permute-start.2 = (bf16[112,1792]{1,0:T(8,128)(2,1)}, bf16[112,1792]{1,0:T(8,128)(2,1)S(1)}, u32[]{:S(2)}, u32[]{:S(2)}) collective-permute-start(bf16[112,1792]{1,0:T(8,128)(2,1)} %slice.12), channel_id=1, source_target_pairs={{0,128},{128,0},{1,129},{129,1},{2,130},{130,2},{3,131},{131,3},{4... | collective-permute-start | bytes 1204232 | tf_op jit(solution)/shard_map/dispatch/ppermute | solution.py:489
  62.2 9.0 %all-to-all-start.2 = ((f32[4,16,224]{2,1,0:T(8,128)}), f32[4,16,224]{2,1,0:T(8,128)S(1)}, u32[]{:S(2)}, u32[]{:S(2)}) async-start(f32[4,16,224]{2,1,0:T(8,128)} %get-tuple-element.22), calls=%async_computation.2 | async-start | bytes 131072 | tf_op jit(solution)/shard_map/projection/all_to_all | solution.py:441
  65.5 5.6 %copy-start.1 = (f32[1,3,1792]{2,1,0:T(4,128)}, f32[1,3,1792]{2,1,0:T(4,128)S(1)}, u32[]{:S(2)}) copy-start(f32[1,3,1792]{2,1,0:T(4,128)S(1)} %copy.19) | copy-start | bytes 64516
  65.5 0.8 copy-start.9
  65.6 0.9 copy-start.10
  71.1 1.7 %copy-start = (f32[4,16,224]{2,1,0:T(8,128)}, f32[4,16,224]{2,1,0:T(8,128)S(1)}, u32[]{:S(2)}) copy-start(f32[4,16,224]{2,1,0:T(8,128)S(1)} %all-to-all-done.2.refs_2_.refs_6_) | copy-start | bytes 172036
  89.2 23.3 %all-to-all-start.4 = ((bf16[16,16,128]{2,1,0:T(8,128)(2,1)}), bf16[16,16,128]{2,1,0:T(8,128)(2,1)S(1)}, u32[]{:S(2)}, u32[]{:S(2)}) async-start(bf16[16,16,128]{2,1,0:T(8,128)(2,1)} %get-tuple-element.23), calls=%async_computation.4 | async-start | bytes 131072 | tf_op jit(solution)/shard_map/predict/all_to_all | solution.py:441
  137.0 5.9 %copy-start.13 = (s32[2]{0:T(128)S(1)}, s32[2]{0:T(128)}, u32[]{:S(2)}) copy-start(s32[2]{0:T(128)} %param.21) | copy-start | bytes 28
  137.0 15.7 %all-to-all-start.6 = ((bf16[16,16,128]{2,1,0:T(8,128)(2,1)}), bf16[16,16,128]{2,1,0:T(8,128)(2,1)S(1)}, u32[]{:S(2)}, u32[]{:S(2)}) async-start(bf16[16,16,128]{2,1,0:T(8,128)(2,1)} %get-tuple-element.31), calls=%async_computation.6 | async-start | bytes 131072 | tf_op jit(solution)/shard_map/backward/all_to_all | solution.py:441
  142.9 0.7 copy-start.14

commit v4 on v3

--- a/solution.py
+++ b/solution.py
@@ -21,9 +21,9 @@
 HID = 224
 PACK = 64
 ROWS = 72
-FSDP = ("yh", "yl", "zh", "zl")
-QUAD = ("yl", "zl")
-SHARERS = ("yh", "zh")
+FSDP = ("y", "zh", "zl")
+RING = ("zh", "zl")
+SHARERS = ("y", "zh")
 
 
 norm_eps = 1e-06
@@ -156,7 +156,7 @@
         body = jnp.concatenate([tiles[0], tiles[1], tiles[2], tiles[3][:8]], axis=0)
         last = tiles[3][8:]
         for high in range(8):
-            f = (high // 4) * 16 + (q // 2) * 8 + (high % 4) * 2 + q % 2
+            f = 4 * high + q
             tail = jnp.where(row == 2, base_high[f : f + 1], last)
             tail = jnp.where(row == 3, base_low[f : f + 1], tail)
             parcel_ref[f] = jnp.concatenate([body, tail, head], axis=0).astype(bf16)
@@ -180,8 +180,9 @@
     proj = dot(w_out_ref[...], pair)
     proj = proj + pltpu.roll(proj, PACK, axis=1)
     proj = proj.T
-    for s in range(SAMPLES):
-        proj_ref[s] = proj[C_OUT * s : C_OUT * (s + 1)]
+    for z in range(8):
+        q = z % SAMPLES
+        proj_ref[z] = proj[C_OUT * q : C_OUT * (q + 1)].astype(bf16)
 
 
 def first_kernel(
@@ -204,26 +205,29 @@
         slope_ref[b] = half + 0.5 * pre * (1.0 - tanh * tanh) * (
             cubic * (1.0 + 3.0 * 0.044715 * square)
         )
+        slope_ref.start(b)
+
+
+def held_projections(proj_ref, z):
+    lane = iota((C_OUT, HID), 1)
+    after, before = proj_ref[(z + 2) % 8].astype(f32), proj_ref[(z + 6) % 8].astype(f32)
+    ends = jnp.where(lane < HID // 2, after, before).astype(bf16)
+    return [proj_ref[z], proj_ref[(z + 7) % 8], proj_ref[(z + 1) % 8], ends]
 
 
 def predict_kernel(place_ref, act_ref, proj_ref, part_ref):
-    quarter = place_ref[1]
     total = None
-    for b in range(4):
-        high, low = high_low(proj_ref[quarter ^ b])
-        pair = jnp.concatenate([high, low], axis=0).astype(bf16)
-        part = dot_nt(pair, act_ref[b])
+    for b, proj in enumerate(held_projections(proj_ref, place_ref[4])):
+        part = dot_nt(proj, act_ref[b])
         total = part if total is None else total + part
-    total = total[:C_OUT] + total[C_OUT:]
     for other in range(8):
         part_ref[other] = total
 
 
-def own_kernel(parts_ref, own_ref, shared_ref):
-    own = jnp.sum(parts_ref[...], axis=0)
-    own_ref[...] = own
+def own_kernel(parts_ref, shared_ref):
+    own = jnp.sum(parts_ref[...], axis=0).astype(bf16)
     for e in range(GROUPS):
-        shared_ref[e] = own.astype(bf16)
+        shared_ref[e] = own
 
 
 def base_kernel(gathered_ref, rows_ref, head_ref, base_ref, facts_ref):
@@ -236,7 +240,7 @@
 
 
 def backward_kernel(
-    place_ref, shared_ref, own_ref, base_ref, facts_ref, block_ref, proj_ref, slope_ref,
+    place_ref, shared_ref, base_ref, facts_ref, block_ref, proj_ref, slope_ref,
     mod_ref, head_ref, rows_ref, w0_ref, w1_ref, w2_ref, w3_ref, w4_ref, parcel_ref,
 ):
     shard, quarter, leader, sample = place_ref[0], place_ref[1], place_ref[2], place_ref[3]
@@ -250,7 +254,7 @@
     chosen = (iota((GROUPS * LANES, LANES), 0) == source).astype(f32).astype(bf16)
     everyone = jnp.concatenate([shared_ref[e] for e in range(GROUPS)], axis=1)
     partner = dot(everyone, chosen)
-    residue = base_ref[...] + own_w * own_ref[...] + other_w * partner - target
+    residue = base_ref[...] + own_w * shared_ref[place_ref[5]].astype(f32) + other_w * partner - target
     kept_err = jnp.sum(first * residue * residue, keepdims=True)
 
     lost_base = facts[PACK + 2 : PACK + 3] + facts[PACK + 3 : PACK + 4]
@@ -263,12 +267,12 @@
     for place, values in enumerate(high_low(lost) + high_low(err)):
         tail = jnp.where(row == place, values, tail)
 
-    upstream = (own_w * residue).T
+    upstream = jnp.concatenate(high_low((own_w * residue).T), axis=1).astype(bf16)
     weights = [w0_ref, w1_ref, w2_ref, (w3_ref, w4_ref)]
     total = None
-    for b, weight in enumerate(weights):
-        grad = slope_ref[b] * dot(upstream, proj_ref[quarter ^ b], precision=highest)
-        part = dot(grad.astype(bf16), whole(weight))
+    for b, proj in enumerate(held_projections(proj_ref, place_ref[4])):
+        grad = slope_ref[b] * dot(upstream, jnp.concatenate([proj, proj], axis=0))
+        part = dot(grad.astype(bf16), whole(weights[b]))
         total = part if total is None else total + part
     rows = rows_ref[...].astype(f32)
     rms = lax.rsqrt(jnp.sum(rows * rows, axis=1, keepdims=True) / D + norm_eps)
@@ -291,7 +295,7 @@
     for q in range(4):
         total = None
         for high in range(8):
-            f = (high // 4) * 16 + (q // 2) * 8 + (high % 4) * 2 + q % 2
+            f = 4 * high + q
             part = parcel_ref[f].astype(f32)
             lost_ref[0, f : f + 1] = part[FEAT : FEAT + 1]
             lost_ref[1, f : f + 1] = part[FEAT + 1 : FEAT + 2]
@@ -315,8 +319,8 @@
     place_ref, levels_ref, home_ref, pick_ref, lost_ref, head_ref,
     grad_ref, loss_ref,
 ):
-    sample = place_ref[3]
-    pairs = [place_ref[4 + i] for i in range(SAMPLES)]
+    sample = place_ref[3].astype(f32)
+    pairs = [levels_ref[SAMPLES + 2 + i] for i in range(SAMPLES)]
     columns = []
     for tile in range(4):
         tiles = lane_blocks([home_ref[4 * tile + b].astype(f32) for b in range(4)])
@@ -372,24 +376,35 @@
 
 
 class Stored:
-    def __init__(self, target, held, semaphore):
+    def __init__(self, target, held, semaphore, parts):
         self.held = held
-        self.copy = pltpu.make_async_copy(held, target, semaphore)
-        self.started = False
+        if parts == 1:
+            self.copies = [pltpu.make_async_copy(held, target, semaphore.at[0])]
+        else:
+            self.copies = [
+                pltpu.make_async_copy(held.at[i], target.at[i], semaphore.at[i])
+                for i in range(parts)
+            ]
+        self.started = [False] * parts
 
     def __setitem__(self, index, values):
         self.held[index] = values
 
-    def start(self):
-        if not self.started:
-            self.copy.start()
-            self.started = True
+    def start(self, part=0):
+        if not self.started[part]:
+            self.copies[part].start()
+            self.started[part] = True
+
+    def finish(self):
+        for part in range(len(self.copies)):
+            self.start(part)
 
     def wait(self):
-        self.copy.wait()
-
-
-def call(kernel, scalars, arrays, outs, fetch=(), store=(), flops=0):
+        for copy in self.copies:
+            copy.wait()
+
+
+def call(kernel, scalars, arrays, outs, fetch=(), store=(), parts={}, flops=0):
     vmem = pl.BlockSpec(memory_space=pltpu.VMEM)
     smem = pl.BlockSpec(memory_space=pltpu.SMEM)
     hbm = pl.BlockSpec(memory_space=pltpu.HBM)
@@ -404,8 +419,10 @@
     ]
     moved = [arrays[i] for i in fetch] + [out_shape[i] for i in store]
     scratch = [pltpu.VMEM(a.shape, a.dtype) for a in moved]
+    counts = [1] * len(fetch) + [parts.get(i, 1) for i in store]
+    starts = [sum(counts[:n]) for n in range(len(counts))]
     if moved:
-        scratch.append(pltpu.SemaphoreType.DMA((len(moved),)))
+        scratch.append(pltpu.SemaphoreType.DMA((sum(counts),)))
 
     def body(*refs):
         refs = list(refs)
@@ -417,11 +434,12 @@
             fetched.append(Fetched(refs[at_in + i], refs[at_held + n], refs[-1].at[n]))
             refs[at_in + i] = fetched[-1]
         for n, i in enumerate(store, len(fetch)):
-            stored.append(Stored(refs[at_out + i], refs[at_held + n], refs[-1].at[n]))
+            semaphores = refs[-1].at[pl.ds(starts[n], counts[n])]
+            stored.append(Stored(refs[at_out + i], refs[at_held + n], semaphores, counts[n]))
             refs[at_out + i] = stored[-1]
         kernel(*refs[:at_held])
         for item in stored:
-            item.start()
+            item.finish()
         for item in fetched + stored:
             item.wait()
 
@@ -455,19 +473,21 @@
     timesteps,
 ):
     shard = lax.axis_index(FSDP)
-    quarter = lax.axis_index(QUAD)
+    ring = lax.axis_index(RING)
+    quarter = lax.axis_index("zl")
     leader = (lax.axis_index(SHARERS) == 0).astype(i32)
     my_sample = lax.axis_index("expert") * SAMPLES // GROUPS
-    place = jnp.concatenate([jnp.stack([shard, quarter, leader, my_sample]).astype(i32), pair_ids])
+    place = jnp.stack([shard, quarter, leader, my_sample, ring, lax.axis_index("expert")]).astype(i32)
     fraction = timesteps.astype(f32) / 1000.0
     keep_level = jnp.cos((fraction + 0.008) / 1.008 * (math.pi / 2.0)) ** 2
-    levels = jnp.concatenate([ref_err, dpo_beta * keep_level])
+    levels = jnp.concatenate([ref_err, dpo_beta * keep_level, pair_ids.astype(f32)])
     w_in = w_first[0].T
 
     with jax.named_scope("weights"):
-        swap_pair = [(0, 1), (1, 0)]
-        w_z = lax.ppermute(w_in, "zl", swap_pair)
-        w_y = lax.ppermute(w_in, "yl", swap_pair)
+        up = [(z, (z + 1) % 8) for z in range(8)]
+        down = [(z, (z + 7) % 8) for z in range(8)]
+        w_before = lax.ppermute(w_in, RING, up)
+        w_after = lax.ppermute(w_in, RING, down)
 
     with jax.named_scope("routing"):
         sent, pick, base, block = call(
@@ -484,10 +504,15 @@
         )
     with jax.named_scope("dispatch"):
         arrived = swap(sent, "expert")
+        arrived, w_before, w_after = lax.optimization_barrier((arrived, w_before, w_after))
         half = HID // 2
-        weights = [w_in, w_z, w_y]
-        weights.append(lax.ppermute(w_z[:half], "yl", swap_pair))
-        weights.append(lax.ppermute(w_y[half:], "zl", swap_pair))
+        weights = [
+            w_in,
+            w_before,
+            w_after,
+            lax.ppermute(w_after[:half], RING, down),
+            lax.ppermute(w_before[half:], RING, up),
+        ]
         head_flat = jnp.pad(head.T.reshape(FEAT // 8, LANES), ((0, 1), (0, 0)))
         (parcel,) = call(
             parcel_kernel, [], [arrived, base, head_flat], [((SHARDS, ROWS, LANES), bf16)]
@@ -500,11 +525,11 @@
             head_kernel,
             [],
             [gathered, gate, w_second[0]],
-            [((SAMPLES, C_OUT, HID), f32), ((D, LANES), bf16)],
+            [((8, C_OUT, HID), bf16), ((D, LANES), bf16)],
             fetch=(2,),
             store=(0, 1),
         )
-        proj = swap(proj, QUAD)
+        proj = swap(proj, RING)
 
     with jax.named_scope("first_layer"):
         mod = lax.dynamic_index_in_dim(modulation, quarter, 0, keepdims=False)
@@ -513,20 +538,18 @@
             [],
             [gathered, mod] + weights,
             [((4, LANES, HID), bf16), ((4, LANES, HID), f32), ((LANES, D), bf16)],
-            fetch=(2, 3, 4, 5, 6),
-            store=(0, 1, 2),
+            fetch=(2, 3, 4),
+            store=(1, 2),
+            parts={1: 4},
             flops=8 * D * HID * LANES,
         )
 
     with jax.named_scope("predict"):
         (part,) = call(
-            predict_kernel, [place], [act, proj], [((8, C_OUT, LANES), f32)], fetch=(0,)
+            predict_kernel, [place], [act, proj], [((8, C_OUT, LANES), f32)]
         )
         parts = swap(part, SHARERS)
-        own, shared = call(
-            own_kernel, [], [parts], [((C_OUT, LANES), f32), ((GROUPS, C_OUT, LANES), bf16)],
-            store=(0,),
-        )
+        (shared,) = call(own_kernel, [], [parts], [((GROUPS, C_OUT, LANES), bf16)])
         base_rows, facts = call(
             base_kernel, [], [gathered, rows, head_all], [((C_OUT, LANES), f32), ((72, LANES), f32)],
             fetch=(1, 2),
@@ -538,10 +561,10 @@
         (parcel,) = call(
             backward_kernel,
             [place],
-            [shared, own, base_rows, facts, block, proj, slope, mod, head_all, rows]
+            [shared, base_rows, facts, block, proj, slope, mod, head_all, rows]
             + weights,
             [((SHARDS, PACK, LANES), bf16)],
-            fetch=tuple(range(1, 15)),
+            fetch=(1, 2, 3, 4, 5, 9, 10, 11, 12, 13, 6, 7, 8),
             flops=8 * D * HID * LANES,
         )
         parcel = swap(parcel, FSDP)
@@ -563,7 +586,7 @@
 
 
 def solution(mesh):
-    mesh = Mesh(mesh.devices.reshape(2, 2, 4, 2, 16), FSDP + ("expert",))
+    mesh = Mesh(mesh.devices.reshape(4, 2, 4, 16), FSDP + ("expert",))
     in_specs = (
         P("expert", FSDP),
         P(),

time: 156 us -> 151 us (0.968)
  starting transfers between devices: 58.1 us -> 52.9 us
  waiting for transfers between devices: 33 us -> 36.3 us
  Pallas kernels: 24.5 us -> 21.9 us
    all_to_all x5, starting transfers between devices: 44.8 us -> 33.2 us  [swap(): return lax.all_to_all(chunks, axis, split_axis=0, concat_axis=0, tiled=True)]
    ppermute x4, starting transfers between devices: 13.3 us -> 19.7 us  [the longest x1 11.5 us: local(): w_after = lax.ppermute(w_in, RING, down)]
    pallas_call x10, Pallas kernels: 24.5 us -> 21.9 us  [call(): pl.pallas_call(body, out_shape=out_shape, in_specs=[smem] * len(scalars)...]
    all_to_all x5, waiting for transfers between devices: 33 us -> 34.7 us  [swap(): return lax.all_to_all(chunks, axis, split_axis=0, concat_axis=0, tiled=True)]
  transfers between devices with their start and end apart: 9 -> 9, of which waited for: 4 -> 6; matrix products, arithmetic and copies ran while one was open for 2% -> 2% of each run, Pallas kernels for 7% -> 8%
where the time goes in v4:
time: 151 us; the launch traced here: 150 us
  starting transfers between devices  52.9 us (35%)
  waiting for transfers between devices  36.3 us (24%)
  blocking collectives  34 us (23%)
  Pallas kernels  21.9 us (15%)
  local copies, waits for them, and re-layouts  4.24 us (3%)
    all_to_all x5, waiting for transfers between devices, swap(): return lax.all_to_all(chunks, axis, split_axis=0, concat_axis=0, tiled=True)  34.7 us
    all_to_all x2, blocking collectives, swap(): return lax.all_to_all(chunks, axis, split_axis=0, concat_axis=0, tiled=True)  34 us
    all_to_all x5, starting transfers between devices, swap(): return lax.all_to_all(chunks, axis, split_axis=0, concat_axis=0, tiled=True)  33.2 us
    pallas_call x10, Pallas kernels, call(): pl.pallas_call(body, out_shape=out_shape, in_specs=[smem] * len(scalars)...  21.9 us
    ppermute x1, starting transfers between devices, local(): w_after = lax.ppermute(w_in, RING, down)  11.5 us
    ppermute x1, starting transfers between devices, local(): lax.ppermute(w_after[:half], RING, down)  4.34 us
  transfers between devices with their start and end apart: 9, of which 6 were waited for; matrix products, arithmetic and copies ran while one was open for 2% of the time, Pallas kernels for 8%

profile of v4, /device:TPU:1, one launch (start us, length us, event | category | flops | bytes accessed | tf_op | source)
XLA Modules:
  0.0 150.4 jit_solution(153406027692869532)
XLA Ops:
  0.6 11.5 %collective-permute-start.1 = (bf16[224,1792]{1,0:T(8,128)(2,1)}, bf16[224,1792]{1,0:T(8,128)(2,1)S(1)}, u32[]{:S(2)}, u32[]{:S(2)}) collective-permute-start(bf16[224,1792]{1,0:T(8,128)(2,1)} %bitcast.34), channel_id=1, source_target_pairs={{0,112},{16,0},{32,16},{48,32},{64,48},{80,64},{96,80},{112,96},{1... | collective-permute-start | bytes 2408456 | tf_op jit(solution)/shard_map/weights/ppermute | solution.py:490
  12.1 1.9 %collective-permute-start = (bf16[224,1792]{1,0:T(8,128)(2,1)}, bf16[224,1792]{1,0:T(8,128)(2,1)S(1)}, u32[]{:S(2)}, u32[]{:S(2)}) collective-permute-start(bf16[224,1792]{1,0:T(8,128)(2,1)} %bitcast.35), channel_id=1, source_target_pairs={{0,16},{16,32},{32,48},{48,64},{64,80},{80,96},{96,112},{112,0},{1... | collective-permute-start | bytes 2408456 | tf_op jit(solution)/shard_map/weights/ppermute | solution.py:489
  14.2 0.6 copy-done.5
  14.9 2.7 %routing.1 = (bf16[16,16,128]{2,1,0:T(8,128)(2,1)}, bf16[512,256]{1,0:T(8,128)(2,1)}, f32[32,128]{1,0:T(8,128)S(1)}, f32[2,32,128]{2,1,0:T(8,128)}) custom-call(s32[6]{0:T(128)S(1)} %stack.31.refs_0_, bf16[56,256]{1,0:T(8,128)(2,1)S(1)} %bitcast.29, s32[2,256]{1,0:T(2,128)S(1)} %bitcast.31, f32[2,256]{1,0:T(2,128)S(1)} %bitcast.32, f32[16,256]{1,0:T(8,128)S(1)} %bitcast.30, ...), custom_call_target="tpu_custom_call" | custom-call | bytes 50944 | tf_op jit(solution)/shard_map/routing/pallas_call | solution.py:446
  17.6 10.5 %all-to-all-start = ((bf16[16,16,128]{2,1,0:T(8,128)(2,1)}), bf16[16,16,128]{2,1,0:T(8,128)(2,1)S(1)}, u32[]{:S(2)}, u32[]{:S(2)}) async-start(bf16[16,16,128]{2,1,0:T(8,128)(2,1)} %get-tuple-element.20), calls=%async_computation | async-start | bytes 131072 | tf_op jit(solution)/shard_map/dispatch/all_to_all | solution.py:459
  28.3 9.5 %all-to-all-done.refs_0_ = bf16[16,16,128]{2,1,0:T(8,128)(2,1)S(1)} async-done(((bf16[16,16,128]{2,1,0:T(8,128)(2,1)}), bf16[16,16,128]{2,1,0:T(8,128)(2,1)S(1)}, u32[]{:S(2)}, u32[]{:S(2)}) %all-to-all-start) | async-done | bytes 65568 | tf_op jit(solution)/shard_map/dispatch/all_to_all | solution.py:459
  37.9 1.1 dispatch.1
  39.0 5.1 %all-to-all-start.1 = ((bf16[32,72,128]{2,1,0:T(8,128)(2,1)}), bf16[32,72,128]{2,1,0:T(8,128)(2,1)S(1)}, u32[]{:S(2)}, u32[]{:S(2)}) async-start(bf16[32,72,128]{2,1,0:T(8,128)(2,1)} %dispatch.1), calls=%async_computation.1 | async-start | bytes 1179648 | tf_op jit(solution)/shard_map/dispatch/all_to_all | solution.py:459
  44.1 0.8 slice.10
  44.9 0.8 slice.9
  45.7 4.3 %collective-permute-start.2 = (bf16[112,1792]{1,0:T(8,128)(2,1)}, bf16[112,1792]{1,0:T(8,128)(2,1)S(1)}, u32[]{:S(2)}, u32[]{:S(2)}) collective-permute-start(bf16[112,1792]{1,0:T(8,128)(2,1)} %slice.9), channel_id=1, source_target_pairs={{0,112},{16,0},{32,16},{48,32},{64,48},{80,64},{96,80},{112,96},{1... | collective-permute-start | bytes 1204232 | tf_op jit(solution)/shard_map/dispatch/ppermute | solution.py:513
  50.0 1.9 %collective-permute-start.3 = (bf16[112,1792]{1,0:T(8,128)(2,1)}, bf16[112,1792]{1,0:T(8,128)(2,1)S(1)}, u32[]{:S(2)}, u32[]{:S(2)}) collective-permute-start(bf16[112,1792]{1,0:T(8,128)(2,1)} %slice.10), channel_id=1, source_target_pairs={{0,16},{16,32},{32,48},{48,64},{64,80},{80,96},{96,112},{112,0},{1... | collective-permute-start | bytes 1204232 | tf_op jit(solution)/shard_map/dispatch/ppermute | solution.py:514
  52.4 7.8 %all-to-all-done.1.refs_0_ = bf16[32,72,128]{2,1,0:T(8,128)(2,1)S(1)} async-done(((bf16[32,72,128]{2,1,0:T(8,128)(2,1)}), bf16[32,72,128]{2,1,0:T(8,128)(2,1)S(1)}, u32[]{:S(2)}, u32[]{:S(2)}) %all-to-all-start.1) | async-done | bytes 589856 | tf_op jit(solution)/shard_map/dispatch/all_to_all | solution.py:459
  60.2 2.4 %projection.1 = (bf16[8,16,224]{2,1,0:T(8,128)(2,1)}, bf16[1792,128]{1,0:T(8,128)(2,1)}) custom-call(bf16[32,72,128]{2,1,0:T(8,128)(2,1)S(1)} %all-to-all-done.1.refs_0_, f32[1792,128]{1,0:T(8,128)S(1)} %copy.16.refs_1_, bf16[224,1792]{1,0:T(8,128)(2,1)} %bitcast.39), custom_call_target="tpu_custom_call" | custom-call | bytes 2310144 | tf_op jit(solution)/shard_map/projection/pallas_call | solution.py:446
  62.6 5.3 %all-to-all-start.2 = ((bf16[8,16,224]{2,1,0:T(8,128)(2,1)}), bf16[8,16,224]{2,1,0:T(8,128)(2,1)S(1)}, u32[]{:S(2)}, u32[]{:S(2)}) async-start(bf16[8,16,224]{2,1,0:T(8,128)(2,1)} %get-tuple-element.26), calls=%async_computation.2 | async-start | bytes 131072 | tf_op jit(solution)/shard_map/projection/all_to_all | solution.py:459
  68.0 1.6 %collective-permute-done.3.refs_6_.refs_14_ = bf16[112,1792]{1,0:T(8,128)(2,1)S(1)} collective-permute-done((bf16[112,1792]{1,0:T(8,128)(2,1)}, bf16[112,1792]{1,0:T(8,128)(2,1)S(1)}, u32[]{:S(2)}, u32[]{:S(2)}) %collective-permute-start.3) | collective-permute-done | bytes 401440 | tf_op jit(solution)/shard_map/dispatch/ppermute | solution.py:514
  69.5 4.3 %first_layer.1 = (bf16[4,128,224]{2,1,0:T(8,128)(2,1)S(1)}, f32[4,128,224]{2,1,0:T(8,128)}, bf16[128,1792]{1,0:T(8,128)(2,1)}) custom-call(bf16[32,72,128]{2,1,0:T(8,128)(2,1)S(1)} %all-to-all-done.1.refs_0_, f32[3,1792]{1,0:T(4,128)S(1)} %bitcast.26, bf16[224,1792]{1,0:T(8,128)(2,1)} %bitcast.36, bf16[224,1792]{1,0:T(8,128)(2,1)} %copy-done.10, ...), custom_call_target="tpu_custom_call" | custom-call | flops 411041792 | bytes 3822592 | tf_op jit(solution)/shard_map/first_layer/pallas_call | solution.py:446
  73.8 1.4 all-to-all-done.2.refs_2_.refs_5_
  75.2 0.7 predict.3
  75.9 15.7 %all_to_all.35.refs_0_ = f32[8,16,128]{2,1,0:T(8,128)S(1)} all-to-all(f32[8,16,128]{2,1,0:T(8,128)S(1)} %predict.3), channel_id=1, replica_groups=mesh['y'=4,'zh'=2,'zl'=4,'expert'=16] {'y','zh'}, dimensions={0} | all-to-all | bytes 131072 | tf_op jit(solution)/shard_map/predict/all_to_all | solution.py:459
  91.7 0.6 predict.4
  92.3 6.8 %all-to-all-start.4 = ((bf16[16,16,128]{2,1,0:T(8,128)(2,1)}), bf16[16,16,128]{2,1,0:T(8,128)(2,1)S(1)}, u32[]{:S(2)}, u32[]{:S(2)}) async-start(bf16[16,16,128]{2,1,0:T(8,128)(2,1)} %predict.4), calls=%async_computation.4 | async-start | bytes 131072 | tf_op jit(solution)/shard_map/predict/all_to_all | solution.py:459
  99.1 2.1 %predict.5 = (f32[16,128]{1,0:T(8,128)}, f32[72,128]{1,0:T(8,128)}) custom-call(bf16[32,72,128]{2,1,0:T(8,128)(2,1)S(1)} %all-to-all-done.1.refs_0_, bf16[128,1792]{1,0:T(8,128)(2,1)} %get-tuple-element.27.refs_1_.refs_9_, bf16[1792,128]{1,0:T(8,128)(2,1)} %get-tuple-element.28.refs_2_.refs_8_), custom_call_target="tpu_custom_call" | custom-call | bytes 1507328 | tf_op jit(solution)/shard_map/predict/pallas_call | solution.py:446
  101.2 7.6 %all-to-all-done.4.refs_1_ = bf16[16,16,128]{2,1,0:T(8,128)(2,1)S(1)} async-done(((bf16[16,16,128]{2,1,0:T(8,128)(2,1)}), bf16[16,16,128]{2,1,0:T(8,128)(2,1)S(1)}, u32[]{:S(2)}, u32[]{:S(2)}) %all-to-all-start.4) | async-done | bytes 65568 | tf_op jit(solution)/shard_map/predict/all_to_all | solution.py:459
  108.8 4.1 %backward.2 = bf16[32,64,128]{2,1,0:T(8,128)(2,1)S(1)} custom-call(s32[6]{0:T(128)S(1)} %stack.31.refs_0_, bf16[16,16,128]{2,1,0:T(8,128)(2,1)S(1)} %all-to-all-done.4.refs_1_, f32[16,128]{1,0:T(8,128)} %get-tuple-element.29.refs_2_, f32[72,128]{1,0:T(8,128)} %get-tuple-element.30.refs_3_, f32[2,32,128]{2,1,0:T(8,128)} %get-tuple-element.31.refs_4_, ...), custom_call_target="tpu_custom_call" | custom-call | flops 411041792 | bytes 4809728 | tf_op jit(solution)/shard_map/backward/pallas_call | solution.py:446
  112.9 18.2 %all_to_all.36.refs_0_ = bf16[32,64,128]{2,1,0:T(8,128)(2,1)S(1)} all-to-all(bf16[32,64,128]{2,1,0:T(8,128)(2,1)S(1)} %backward.2), channel_id=1, replica_groups=mesh['y'=4,'zh'=2,'zl'=4,'expert'=16] {'y','zh','zl'}, dimensions={0} | all-to-all | bytes 1048576 | tf_op jit(solution)/shard_map/backward/all_to_all | solution.py:459
  131.2 1.4 backward.3
  132.6 5.4 %all-to-all-start.6 = ((bf16[16,16,128]{2,1,0:T(8,128)(2,1)}), bf16[16,16,128]{2,1,0:T(8,128)(2,1)S(1)}, u32[]{:S(2)}, u32[]{:S(2)}) async-start(bf16[16,16,128]{2,1,0:T(8,128)(2,1)} %get-tuple-element.33), calls=%async_computation.6 | async-start | bytes 131072 | tf_op jit(solution)/shard_map/backward/all_to_all | solution.py:459
  138.1 0.6 copy-done.14
  138.7 0.7 copy-done.12
  139.4 8.4 %all-to-all-done.6.refs_2_ = bf16[16,16,128]{2,1,0:T(8,128)(2,1)S(1)} async-done(((bf16[16,16,128]{2,1,0:T(8,128)(2,1)}), bf16[16,16,128]{2,1,0:T(8,128)(2,1)S(1)}, u32[]{:S(2)}, u32[]{:S(2)}) %all-to-all-start.6) | async-done | bytes 65568 | tf_op jit(solution)/shard_map/backward/all_to_all | solution.py:459
  147.8 2.5 %finish.1 = (bf16[56,256]{1,0:T(8,128)(2,1)}, f32[1,1]{1,0:T(1,128)}) custom-call(s32[6]{0:T(128)S(1)} %stack.31.refs_0_, f32[10]{0:T(128)S(1)} %pad_maximum_fusion.refs_1_, bf16[16,16,128]{2,1,0:T(8,128)(2,1)S(1)} %all-to-all-done.6.refs_2_, bf16[512,256]{1,0:T(8,128)(2,1)} %get-tuple-element.34.refs_3_, f32[2,32,128]{2,1,0:T(8,128)} %get-tuple-element.35.refs_4_, ...), custom_call_target="tpu_custom_call" | custom-call | bytes 362240 | tf_op jit(solution)/shard_map/finish/pallas_call | solution.py:446
  (43 shorter events, 1.0 us)
Async XLA Ops:
  0.6 37.2 %collective-permute-start.1 = (bf16[224,1792]{1,0:T(8,128)(2,1)}, bf16[224,1792]{1,0:T(8,128)(2,1)S(1)}, u32[]{:S(2)}, u32[]{:S(2)}) collective-permute-start(bf16[224,1792]{1,0:T(8,128)(2,1)} %bitcast.34), channel_id=1, source_target_pairs={{0,112},{16,0},{32,16},{48,32},{64,48},{80,64},{96,80},{112,96},{1... | collective-permute-start | bytes 2408456 | tf_op jit(solution)/shard_map/weights/ppermute | solution.py:490
  12.1 25.7 %collective-permute-start = (bf16[224,1792]{1,0:T(8,128)(2,1)}, bf16[224,1792]{1,0:T(8,128)(2,1)S(1)}, u32[]{:S(2)}, u32[]{:S(2)}) collective-permute-start(bf16[224,1792]{1,0:T(8,128)(2,1)} %bitcast.35), channel_id=1, source_target_pairs={{0,16},{16,32},{32,48},{48,64},{64,80},{80,96},{96,112},{112,0},{1... | collective-permute-start | bytes 2408456 | tf_op jit(solution)/shard_map/weights/ppermute | solution.py:489
  14.1 0.7 copy-start.5
  14.1 0.7 copy-start.6
  14.1 0.7 copy-start.8
  14.2 0.7 copy-start.4
  14.2 0.7 copy-start.7
  17.6 20.3 %all-to-all-start = ((bf16[16,16,128]{2,1,0:T(8,128)(2,1)}), bf16[16,16,128]{2,1,0:T(8,128)(2,1)S(1)}, u32[]{:S(2)}, u32[]{:S(2)}) async-start(bf16[16,16,128]{2,1,0:T(8,128)(2,1)} %get-tuple-element.20), calls=%async_computation | async-start | bytes 131072 | tf_op jit(solution)/shard_map/dispatch/all_to_all | solution.py:459
  37.9 7.1 %copy-start.9 = (bf16[224,1792]{1,0:T(8,128)(2,1)}, bf16[224,1792]{1,0:T(8,128)(2,1)S(1)}, u32[]{:S(2)}) copy-start(bf16[224,1792]{1,0:T(8,128)(2,1)S(1)} %collective-permute-done.1.refs_4_.refs_12_) | copy-start | bytes 2408452
  37.9 6.3 %copy-start.10 = (bf16[224,1792]{1,0:T(8,128)(2,1)}, bf16[224,1792]{1,0:T(8,128)(2,1)S(1)}, u32[]{:S(2)}) copy-start(bf16[224,1792]{1,0:T(8,128)(2,1)S(1)} %collective-permute-done.refs_3_.refs_11_) | copy-start | bytes 2408452
  39.0 21.2 %all-to-all-start.1 = ((bf16[32,72,128]{2,1,0:T(8,128)(2,1)}), bf16[32,72,128]{2,1,0:T(8,128)(2,1)S(1)}, u32[]{:S(2)}, u32[]{:S(2)}) async-start(bf16[32,72,128]{2,1,0:T(8,128)(2,1)} %dispatch.1), calls=%async_computation.1 | async-start | bytes 1179648 | tf_op jit(solution)/shard_map/dispatch/all_to_all | solution.py:459
  44.9 7.0 %copy-start.11 = (f32[4,3,1792]{2,0,1:T(4,128)S(1)}, f32[4,3,1792]{2,0,1:T(4,128)}, u32[]{:S(2)}) copy-start(f32[4,3,1792]{2,0,1:T(4,128)} %param.12) | copy-start | bytes 258052
  45.7 22.3 %collective-permute-start.2 = (bf16[112,1792]{1,0:T(8,128)(2,1)}, bf16[112,1792]{1,0:T(8,128)(2,1)S(1)}, u32[]{:S(2)}, u32[]{:S(2)}) collective-permute-start(bf16[112,1792]{1,0:T(8,128)(2,1)} %slice.9), channel_id=1, source_target_pairs={{0,112},{16,0},{32,16},{48,32},{64,48},{80,64},{96,80},{112,96},{1... | collective-permute-start | bytes 1204232 | tf_op jit(solution)/shard_map/dispatch/ppermute | solution.py:513
  50.0 19.5 %collective-permute-start.3 = (bf16[112,1792]{1,0:T(8,128)(2,1)}, bf16[112,1792]{1,0:T(8,128)(2,1)S(1)}, u32[]{:S(2)}, u32[]{:S(2)}) collective-permute-start(bf16[112,1792]{1,0:T(8,128)(2,1)} %slice.10), channel_id=1, source_target_pairs={{0,16},{16,32},{32,48},{48,64},{64,80},{80,96},{96,112},{112,0},{1... | collective-permute-start | bytes 1204232 | tf_op jit(solution)/shard_map/dispatch/ppermute | solution.py:514
  62.6 12.6 %all-to-all-start.2 = ((bf16[8,16,224]{2,1,0:T(8,128)(2,1)}), bf16[8,16,224]{2,1,0:T(8,128)(2,1)S(1)}, u32[]{:S(2)}, u32[]{:S(2)}) async-start(bf16[8,16,224]{2,1,0:T(8,128)(2,1)} %get-tuple-element.26), calls=%async_computation.2 | async-start | bytes 131072 | tf_op jit(solution)/shard_map/projection/all_to_all | solution.py:459
  67.9 5.9 %copy-start.3 = (f32[1,3,1792]{2,1,0:T(4,128)}, f32[1,3,1792]{2,1,0:T(4,128)S(1)}, u32[]{:S(2)}) copy-start(f32[1,3,1792]{2,1,0:T(4,128)S(1)} %copy.19) | copy-start | bytes 64516
  67.9 5.9 %copy-start = (bf16[112,1792]{1,0:T(8,128)(2,1)}, bf16[112,1792]{1,0:T(8,128)(2,1)S(1)}, u32[]{:S(2)}) copy-start(bf16[112,1792]{1,0:T(8,128)(2,1)S(1)} %collective-permute-done.2.refs_5_.refs_13_) | copy-start | bytes 1204228
  69.5 4.3 %copy-start.1 = (bf16[112,1792]{1,0:T(8,128)(2,1)}, bf16[112,1792]{1,0:T(8,128)(2,1)S(1)}, u32[]{:S(2)}) copy-start(bf16[112,1792]{1,0:T(8,128)(2,1)S(1)} %collective-permute-done.3.refs_6_.refs_14_) | copy-start | bytes 1204228
  75.2 0.7 copy-start.2
  92.3 16.5 %all-to-all-start.4 = ((bf16[16,16,128]{2,1,0:T(8,128)(2,1)}), bf16[16,16,128]{2,1,0:T(8,128)(2,1)S(1)}, u32[]{:S(2)}, u32[]{:S(2)}) async-start(bf16[16,16,128]{2,1,0:T(8,128)(2,1)} %predict.4), calls=%async_computation.4 | async-start | bytes 131072 | tf_op jit(solution)/shard_map/predict/all_to_all | solution.py:459
  132.6 5.5 %copy-start.13 = (s32[2]{0:T(128)S(1)}, s32[2]{0:T(128)}, u32[]{:S(2)}) copy-start(s32[2]{0:T(128)} %param.21) | copy-start | bytes 28
  132.6 15.2 %all-to-all-start.6 = ((bf16[16,16,128]{2,1,0:T(8,128)(2,1)}), bf16[16,16,128]{2,1,0:T(8,128)(2,1)S(1)}, u32[]{:S(2)}, u32[]{:S(2)}) async-start(bf16[16,16,128]{2,1,0:T(8,128)(2,1)} %get-tuple-element.33), calls=%async_computation.6 | async-start | bytes 131072 | tf_op jit(solution)/shard_map/backward/all_to_all | solution.py:459
  138.1 0.7 copy-start.14
  138.7 0.7 copy-start.12

commit v5 on v4

--- a/solution.py
+++ b/solution.py
@@ -186,13 +186,14 @@
 
 
 def first_kernel(
-    gathered_ref, mod_ref, w0_ref, w1_ref, w2_ref, w3_ref, w4_ref, act_ref, slope_ref, rows_ref
+    place_ref, gathered_ref, mod_ref, w0_ref, w1_ref, w2_ref, w3_ref, w4_ref, act_ref, slope_ref, rows_ref
 ):
     rows = jnp.concatenate([gathered_ref[f, :FEAT].astype(f32) for f in range(SHARDS)], axis=0).T
     rows_ref[...] = rows.astype(bf16)
     rows_ref.start()
     rms = lax.rsqrt(jnp.sum(rows * rows, axis=1, keepdims=True) / D + norm_eps)
-    normed = (rows * rms) * (1.0 + mod_ref[1:2, :]) + mod_ref[0:1, :]
+    mine = pl.ds(place_ref[1], 1)
+    normed = (rows * rms) * (1.0 + mod_ref[1, mine, :]) + mod_ref[0, mine, :]
     normed = normed.astype(bf16)
     weights = [w0_ref, w1_ref, w2_ref, (w3_ref, w4_ref)]
     for b, weight in enumerate(weights):
@@ -276,7 +277,7 @@
         total = part if total is None else total + part
     rows = rows_ref[...].astype(f32)
     rms = lax.rsqrt(jnp.sum(rows * rows, axis=1, keepdims=True) / D + norm_eps)
-    total = total * (rms * (1.0 + mod_ref[1:2, :]))
+    total = total * (rms * (1.0 + mod_ref[1, pl.ds(quarter, 1), :]))
     inner = jnp.sum(total * rows, axis=1, keepdims=True) * (rms * rms / D)
     high, low = high_low(first * residue * 0.125)
     direct = jnp.concatenate([high, low, jnp.zeros((LANES - 2 * C_OUT, LANES), f32)], axis=0)
@@ -288,7 +289,7 @@
         ).astype(bf16)
 
 
-def mid_kernel(parcel_ref, home_ref, lost_ref):
+def mid_kernel(parcel_ref, home_ref):
     lane = iota((1, LANES), 1)
     row = iota((8, LANES), 0)
     sums, tails = [], []
@@ -297,8 +298,6 @@
         for high in range(8):
             f = 4 * high + q
             part = parcel_ref[f].astype(f32)
-            lost_ref[0, f : f + 1] = part[FEAT : FEAT + 1]
-            lost_ref[1, f : f + 1] = part[FEAT + 1 : FEAT + 2]
             total = part if total is None else total + part
         sums.append(total[:FEAT])
         tails.append(total[FEAT:])
@@ -315,8 +314,20 @@
             home_ref[4 * q + b] = tiles[b].astype(bf16)
 
 
+def direct_kernel(parcel_ref, head_ref, direct_ref):
+    tails = [parcel_ref[f, FEAT:].astype(f32) for f in range(SHARDS)]
+    lane = iota((SHARDS, LANES), 1) // C_OUT
+    head_tile = jnp.concatenate([head_ref[...]] * 8, axis=0).astype(f32).T.astype(bf16)
+    direct = 0.0
+    for part in range(2):
+        rows = jnp.concatenate([tail[part : part + 1] for tail in tails], axis=0)
+        lost = [jnp.where(lane == j, rows, 0.0) for j in range(8)]
+        direct = direct + dot_nt(head_tile, jnp.concatenate(lost, axis=0).astype(bf16))
+    direct_ref[...] = direct
+
+
 def end_kernel(
-    place_ref, levels_ref, home_ref, pick_ref, lost_ref, head_ref,
+    place_ref, levels_ref, home_ref, pick_ref, direct_ref,
     grad_ref, loss_ref,
 ):
     sample = place_ref[3].astype(f32)
@@ -349,14 +360,8 @@
         coef = coef + jnp.where(winner == sample, rate, 0.0)
         coef = coef - jnp.where(loser == sample, rate, 0.0)
     loss_ref[...] = loss[0:1, 0:1] * 0.5
-    lane = iota((SHARDS, LANES), 1) // C_OUT
-    head_tile = jnp.concatenate([head_ref[...]] * 8, axis=0).astype(f32).T.astype(bf16)
-    direct = 0.0
-    for part in range(2):
-        lost = [jnp.where(lane == j, lost_ref[part], 0.0) for j in range(8)]
-        direct = direct + dot_nt(head_tile, jnp.concatenate(lost, axis=0).astype(bf16))
     coef = coef[0:1, 0:1] * (TOK * GROUPS * C_OUT * 2.0 / (TOK * GROUPS // SAMPLES * C_OUT))
-    grad_ref[...] = (coef * (direct + back[:FEAT])).astype(bf16)
+    grad_ref[...] = (coef * (direct_ref[...] + back[:FEAT])).astype(bf16)
 
 
 class Fetched:
@@ -482,6 +487,7 @@
     keep_level = jnp.cos((fraction + 0.008) / 1.008 * (math.pi / 2.0)) ** 2
     levels = jnp.concatenate([ref_err, dpo_beta * keep_level, pair_ids.astype(f32)])
     w_in = w_first[0].T
+    mod = modulation.transpose(1, 0, 2)
 
     with jax.named_scope("weights"):
         up = [(z, (z + 1) % 8) for z in range(8)]
@@ -520,25 +526,23 @@
         gathered = swap(parcel, FSDP)
 
     with jax.named_scope("projection"):
-        gate = jnp.tile(jnp.repeat(modulation[:, 2].T, C_OUT, axis=1), (1, 2))
+        gate = jnp.tile(jnp.repeat(mod[2].T, C_OUT, axis=1), (1, 2))
         proj, head_all = call(
             head_kernel,
             [],
             [gathered, gate, w_second[0]],
             [((8, C_OUT, HID), bf16), ((D, LANES), bf16)],
-            fetch=(2,),
             store=(0, 1),
         )
         proj = swap(proj, RING)
 
     with jax.named_scope("first_layer"):
-        mod = lax.dynamic_index_in_dim(modulation, quarter, 0, keepdims=False)
         act, slope, rows = call(
             first_kernel,
-            [],
+            [place],
             [gathered, mod] + weights,
             [((4, LANES, HID), bf16), ((4, LANES, HID), f32), ((LANES, D), bf16)],
-            fetch=(2, 3, 4),
+            fetch=(1, 2, 3, 4),
             store=(1, 2),
             parts={1: 4},
             flops=8 * D * HID * LANES,
@@ -568,19 +572,16 @@
             flops=8 * D * HID * LANES,
         )
         parcel = swap(parcel, FSDP)
-        home, lost = call(
-            mid_kernel, [], [parcel], [((GROUPS, 16, LANES), bf16), ((2, SHARDS, LANES), f32)],
-            store=(1,),
-        )
+        (home,) = call(mid_kernel, [], [parcel], [((GROUPS, 16, LANES), bf16)])
+        (direct,) = call(direct_kernel, [], [parcel, head], [((FEAT, TOK), f32)])
         home = swap(home, "expert")
 
     with jax.named_scope("finish"):
         grad_tokens, loss = call(
             end_kernel,
             [place, levels],
-            [home, pick, lost, head],
+            [home, pick, direct],
             [((FEAT, TOK), bf16), ((1, 1), f32)],
-            fetch=(1, 2),
         )
     return (grad_tokens.T, loss.reshape(()))
 

time: 151 us -> 149 us (0.987)
  waiting for transfers between devices: 36.3 us -> 33.4 us
  local copies, waits for them, and re-layouts: 4.24 us -> 6.41 us
  Pallas kernels: 21.9 us -> 20 us
    all_to_all x5, waiting for transfers between devices: 34.7 us -> 31.2 us  [swap(): return lax.all_to_all(chunks, axis, split_axis=0, concat_axis=0, tiled=True)]
    another operation x2, local copies, waits for them, and re-layouts: 0.35 us -> 2.53 us  [local(): gate = jnp.tile(jnp.repeat(mod[2].T, C_OUT, axis=1), (1, 2))]
    pallas_call x10 -> x11, Pallas kernels: 21.9 us -> 20 us  [call(): pl.pallas_call(body, out_shape=out_shape, in_specs=[smem] * len(scalars)...]
  transfers between devices with their start and end apart: 9 -> 9, of which waited for: 6 -> 7; matrix products, arithmetic and copies ran while one was open for 2% -> 3% of each run, Pallas kernels for 8% -> 8%
where the time goes in v5:
time: 149 us; the launch traced here: 148 us
  starting transfers between devices  52.9 us (36%)
  blocking collectives  34.4 us (23%)
  waiting for transfers between devices  33.4 us (22%)
  Pallas kernels  20 us (13%)
  local copies, waits for them, and re-layouts  6.41 us (4%)
    all_to_all x2, blocking collectives, swap(): return lax.all_to_all(chunks, axis, split_axis=0, concat_axis=0, tiled=True)  34.4 us
    all_to_all x5, starting transfers between devices, swap(): return lax.all_to_all(chunks, axis, split_axis=0, concat_axis=0, tiled=True)  33.2 us
    all_to_all x5, waiting for transfers between devices, swap(): return lax.all_to_all(chunks, axis, split_axis=0, concat_axis=0, tiled=True)  31.2 us
    pallas_call x11, Pallas kernels, call(): pl.pallas_call(body, out_shape=out_shape, in_specs=[smem] * len(scalars)...  20 us
    ppermute x1, starting transfers between devices, local(): w_after = lax.ppermute(w_in, RING, down)  11.5 us
    ppermute x1, starting transfers between devices, local(): lax.ppermute(w_after[:half], RING, down)  4.34 us
  transfers between devices with their start and end apart: 9, of which 7 were waited for; matrix products, arithmetic and copies ran while one was open for 3% of the time, Pallas kernels for 8%

profile of v5, /device:TPU:1, one launch (start us, length us, event | category | flops | bytes accessed | tf_op | source)
XLA Modules:
  0.0 148.2 jit_solution(18053038585151715929)
XLA Ops:
  0.6 11.5 %collective-permute-start.1 = (bf16[224,1792]{1,0:T(8,128)(2,1)}, bf16[224,1792]{1,0:T(8,128)(2,1)S(1)}, u32[]{:S(2)}, u32[]{:S(2)}) collective-permute-start(bf16[224,1792]{1,0:T(8,128)(2,1)} %bitcast.31), channel_id=1, source_target_pairs={{0,112},{16,0},{32,16},{48,32},{64,48},{80,64},{96,80},{112,96},{1... | collective-permute-start | bytes 2408456 | tf_op jit(solution)/shard_map/weights/ppermute | solution.py:496
  12.1 1.9 %collective-permute-start = (bf16[224,1792]{1,0:T(8,128)(2,1)}, bf16[224,1792]{1,0:T(8,128)(2,1)S(1)}, u32[]{:S(2)}, u32[]{:S(2)}) collective-permute-start(bf16[224,1792]{1,0:T(8,128)(2,1)} %bitcast.32), channel_id=1, source_target_pairs={{0,16},{16,32},{32,48},{48,64},{64,80},{80,96},{96,112},{112,0},{1... | collective-permute-start | bytes 2408456 | tf_op jit(solution)/shard_map/weights/ppermute | solution.py:495
  14.2 0.6 copy-done.6
  14.9 2.6 %routing.1 = (bf16[16,16,128]{2,1,0:T(8,128)(2,1)}, bf16[512,256]{1,0:T(8,128)(2,1)}, f32[32,128]{1,0:T(8,128)S(1)}, f32[2,32,128]{2,1,0:T(8,128)}) custom-call(s32[6]{0:T(128)S(1)} %stack.31.refs_0_, bf16[56,256]{1,0:T(8,128)(2,1)S(1)} %bitcast.26, s32[2,256]{1,0:T(2,128)S(1)} %bitcast.28, f32[2,256]{1,0:T(2,128)S(1)} %bitcast.29, f32[16,256]{1,0:T(8,128)S(1)} %bitcast.27, ...), custom_call_target="tpu_custom_call" | custom-call | bytes 50944 | tf_op jit(solution)/shard_map/routing/pallas_call | solution.py:451
  17.6 10.5 %all-to-all-start = ((bf16[16,16,128]{2,1,0:T(8,128)(2,1)}), bf16[16,16,128]{2,1,0:T(8,128)(2,1)S(1)}, u32[]{:S(2)}, u32[]{:S(2)}) async-start(bf16[16,16,128]{2,1,0:T(8,128)(2,1)} %get-tuple-element.18), calls=%async_computation | async-start | bytes 131072 | tf_op jit(solution)/shard_map/dispatch/all_to_all | solution.py:464
  28.3 9.5 %all-to-all-done.refs_0_ = bf16[16,16,128]{2,1,0:T(8,128)(2,1)S(1)} async-done(((bf16[16,16,128]{2,1,0:T(8,128)(2,1)}), bf16[16,16,128]{2,1,0:T(8,128)(2,1)S(1)}, u32[]{:S(2)}, u32[]{:S(2)}) %all-to-all-start) | async-done | bytes 65568 | tf_op jit(solution)/shard_map/dispatch/all_to_all | solution.py:464
  37.9 1.1 dispatch.1
  39.0 5.1 %all-to-all-start.1 = ((bf16[32,72,128]{2,1,0:T(8,128)(2,1)}), bf16[32,72,128]{2,1,0:T(8,128)(2,1)S(1)}, u32[]{:S(2)}, u32[]{:S(2)}) async-start(bf16[32,72,128]{2,1,0:T(8,128)(2,1)} %dispatch.1), calls=%async_computation.1 | async-start | bytes 1179648 | tf_op jit(solution)/shard_map/dispatch/all_to_all | solution.py:464
  44.1 0.8 slice.9
  44.9 4.3 %collective-permute-start.2 = (bf16[112,1792]{1,0:T(8,128)(2,1)}, bf16[112,1792]{1,0:T(8,128)(2,1)S(1)}, u32[]{:S(2)}, u32[]{:S(2)}) collective-permute-start(bf16[112,1792]{1,0:T(8,128)(2,1)} %slice.9), channel_id=1, source_target_pairs={{0,112},{16,0},{32,16},{48,32},{64,48},{80,64},{96,80},{112,96},{1... | collective-permute-start | bytes 1204232 | tf_op jit(solution)/shard_map/dispatch/ppermute | solution.py:519
  49.3 1.9 %collective-permute-start.3 = (bf16[112,1792]{1,0:T(8,128)(2,1)S(1)}, bf16[112,1792]{1,0:T(8,128)(2,1)S(1)}, u32[]{:S(2)}, u32[]{:S(2)}) collective-permute-start(bf16[112,1792]{1,0:T(8,128)(2,1)S(1)} %slice.10), channel_id=1, source_target_pairs={{0,16},{16,32},{32,48},{48,64},{64,80},{80,96},{96,112},{112,0},{1... | collective-permute-start | bytes 1204232 | tf_op jit(solution)/shard_map/dispatch/ppermute | solution.py:520
  51.2 0.8 slice_bitcast_fusion
  52.0 1.0 tile.11
  53.0 1.5 %copy.16.refs_1_ = f32[1792,128]{1,0:T(8,128)S(1)} copy(f32[1792,128]{0,1:T(8,128)} %bitcast.30) | data formatting | bytes 1835008 | tf_op jit(solution)/shard_map/projection/tile | solution.py:529
  54.5 5.6 %all-to-all-done.1.refs_1_.refs_0_ = bf16[32,72,128]{2,1,0:T(8,128)(2,1)S(1)} async-done(((bf16[32,72,128]{2,1,0:T(8,128)(2,1)}), bf16[32,72,128]{2,1,0:T(8,128)(2,1)S(1)}, u32[]{:S(2)}, u32[]{:S(2)}) %all-to-all-start.1) | async-done | bytes 589856 | tf_op jit(solution)/shard_map/dispatch/all_to_all | solution.py:464
  60.2 1.4 projection.1
  61.6 5.3 %all-to-all-start.2 = ((bf16[8,16,224]{2,1,0:T(8,128)(2,1)}), bf16[8,16,224]{2,1,0:T(8,128)(2,1)S(1)}, u32[]{:S(2)}, u32[]{:S(2)}) async-start(bf16[8,16,224]{2,1,0:T(8,128)(2,1)} %get-tuple-element.24), calls=%async_computation.2 | async-start | bytes 131072 | tf_op jit(solution)/shard_map/projection/all_to_all | solution.py:464
  67.3 1.8 %collective-permute-done.3.refs_7_.refs_14_ = bf16[112,1792]{1,0:T(8,128)(2,1)S(1)} collective-permute-done((bf16[112,1792]{1,0:T(8,128)(2,1)S(1)}, bf16[112,1792]{1,0:T(8,128)(2,1)S(1)}, u32[]{:S(2)}, u32[]{:S(2)}) %collective-permute-start.3) | collective-permute-done | bytes 401440 | tf_op jit(solution)/shard_map/dispatch/ppermute | solution.py:520
  69.1 4.9 %first_layer.1 = (bf16[4,128,224]{2,1,0:T(8,128)(2,1)S(1)}, f32[4,128,224]{2,1,0:T(8,128)}, bf16[128,1792]{1,0:T(8,128)(2,1)}) custom-call(s32[6]{0:T(128)S(1)} %stack.31.refs_0_, bf16[32,72,128]{2,1,0:T(8,128)(2,1)S(1)} %all-to-all-done.1.refs_1_.refs_0_, f32[3,4,1792]{2,1,0:T(4,128)} %bitcast.37, bf16[224,1792]{1,0:T(8,128)(2,1)} %bitcast.33, ...), custom_call_target="tpu_custom_call" | custom-call | flops 411041792 | bytes 3887104 | tf_op jit(solution)/shard_map/first_layer/pallas_call | solution.py:451
  74.2 0.7 predict.3
  74.9 16.1 %all_to_all.35.refs_0_ = f32[8,16,128]{2,1,0:T(8,128)S(1)} all-to-all(f32[8,16,128]{2,1,0:T(8,128)S(1)} %predict.3), channel_id=1, replica_groups=mesh['y'=4,'zh'=2,'zl'=4,'expert'=16] {'y','zh'}, dimensions={0} | all-to-all | bytes 131072 | tf_op jit(solution)/shard_map/predict/all_to_all | solution.py:464
  91.0 0.6 predict.4
  91.7 6.8 %all-to-all-start.4 = ((bf16[16,16,128]{2,1,0:T(8,128)(2,1)}), bf16[16,16,128]{2,1,0:T(8,128)(2,1)S(1)}, u32[]{:S(2)}, u32[]{:S(2)}) async-start(bf16[16,16,128]{2,1,0:T(8,128)(2,1)} %predict.4), calls=%async_computation.4 | async-start | bytes 131072 | tf_op jit(solution)/shard_map/predict/all_to_all | solution.py:464
  98.5 2.1 %predict.5 = (f32[16,128]{1,0:T(8,128)}, f32[72,128]{1,0:T(8,128)}) custom-call(bf16[32,72,128]{2,1,0:T(8,128)(2,1)S(1)} %all-to-all-done.1.refs_1_.refs_0_, bf16[128,1792]{1,0:T(8,128)(2,1)} %get-tuple-element.25.refs_1_.refs_9_, bf16[1792,128]{1,0:T(8,128)(2,1)} %get-tuple-element.26.refs_2_.refs_8_), custom_call_target="tpu_custom_call" | custom-call | bytes 1507328 | tf_op jit(solution)/shard_map/predict/pallas_call | solution.py:451
  100.6 7.6 %all-to-all-done.4.refs_1_ = bf16[16,16,128]{2,1,0:T(8,128)(2,1)S(1)} async-done(((bf16[16,16,128]{2,1,0:T(8,128)(2,1)}), bf16[16,16,128]{2,1,0:T(8,128)(2,1)S(1)}, u32[]{:S(2)}, u32[]{:S(2)}) %all-to-all-start.4) | async-done | bytes 65568 | tf_op jit(solution)/shard_map/predict/all_to_all | solution.py:464
  108.2 4.1 %backward.3 = bf16[32,64,128]{2,1,0:T(8,128)(2,1)S(1)} custom-call(s32[6]{0:T(128)S(1)} %stack.31.refs_0_, bf16[16,16,128]{2,1,0:T(8,128)(2,1)S(1)} %all-to-all-done.4.refs_1_, f32[16,128]{1,0:T(8,128)} %get-tuple-element.27.refs_2_, f32[72,128]{1,0:T(8,128)} %get-tuple-element.28.refs_3_, f32[2,32,128]{2,1,0:T(8,128)} %get-tuple-element.29.refs_4_, ...), custom_call_target="tpu_custom_call" | custom-call | flops 411041792 | bytes 4874240 | tf_op jit(solution)/shard_map/backward/pallas_call | solution.py:451
  112.3 18.3 %all_to_all.36.refs_0_ = bf16[32,64,128]{2,1,0:T(8,128)(2,1)S(1)} all-to-all(bf16[32,64,128]{2,1,0:T(8,128)(2,1)S(1)} %backward.3), channel_id=1, replica_groups=mesh['y'=4,'zh'=2,'zl'=4,'expert'=16] {'y','zh','zl'}, dimensions={0} | all-to-all | bytes 1048576 | tf_op jit(solution)/shard_map/backward/all_to_all | solution.py:464
  130.6 0.9 backward.4
  131.5 5.5 %all-to-all-start.6 = ((bf16[16,16,128]{2,1,0:T(8,128)(2,1)}), bf16[16,16,128]{2,1,0:T(8,128)(2,1)S(1)}, u32[]{:S(2)}, u32[]{:S(2)}) async-start(bf16[16,16,128]{2,1,0:T(8,128)(2,1)} %backward.4), calls=%async_computation.6 | async-start | bytes 131072 | tf_op jit(solution)/shard_map/backward/all_to_all | solution.py:464
  137.6 0.7 copy-done.12
  138.6 8.2 %all-to-all-done.6.refs_2_ = bf16[16,16,128]{2,1,0:T(8,128)(2,1)S(1)} async-done(((bf16[16,16,128]{2,1,0:T(8,128)(2,1)}), bf16[16,16,128]{2,1,0:T(8,128)(2,1)S(1)}, u32[]{:S(2)}, u32[]{:S(2)}) %all-to-all-start.6) | async-done | bytes 65568 | tf_op jit(solution)/shard_map/backward/all_to_all | solution.py:464
  146.8 1.4 finish.1
  (42 shorter events, 2.0 us)
Async XLA Ops:
  0.6 37.2 %collective-permute-start.1 = (bf16[224,1792]{1,0:T(8,128)(2,1)}, bf16[224,1792]{1,0:T(8,128)(2,1)S(1)}, u32[]{:S(2)}, u32[]{:S(2)}) collective-permute-start(bf16[224,1792]{1,0:T(8,128)(2,1)} %bitcast.31), channel_id=1, source_target_pairs={{0,112},{16,0},{32,16},{48,32},{64,48},{80,64},{96,80},{112,96},{1... | collective-permute-start | bytes 2408456 | tf_op jit(solution)/shard_map/weights/ppermute | solution.py:496
  12.1 25.7 %collective-permute-start = (bf16[224,1792]{1,0:T(8,128)(2,1)}, bf16[224,1792]{1,0:T(8,128)(2,1)S(1)}, u32[]{:S(2)}, u32[]{:S(2)}) collective-permute-start(bf16[224,1792]{1,0:T(8,128)(2,1)} %bitcast.32), channel_id=1, source_target_pairs={{0,16},{16,32},{32,48},{48,64},{64,80},{80,96},{96,112},{112,0},{1... | collective-permute-start | bytes 2408456 | tf_op jit(solution)/shard_map/weights/ppermute | solution.py:495
  14.1 0.7 copy-start.6
  14.1 0.7 copy-start.7
  14.1 0.7 copy-start.9
  14.2 0.7 copy-start.5
  14.2 0.7 copy-start.8
  17.6 20.3 %all-to-all-start = ((bf16[16,16,128]{2,1,0:T(8,128)(2,1)}), bf16[16,16,128]{2,1,0:T(8,128)(2,1)S(1)}, u32[]{:S(2)}, u32[]{:S(2)}) async-start(bf16[16,16,128]{2,1,0:T(8,128)(2,1)} %get-tuple-element.18), calls=%async_computation | async-start | bytes 131072 | tf_op jit(solution)/shard_map/dispatch/all_to_all | solution.py:464
  37.8 6.3 %copy-start.10 = (bf16[224,1792]{1,0:T(8,128)(2,1)}, bf16[224,1792]{1,0:T(8,128)(2,1)S(1)}, u32[]{:S(2)}) copy-start(bf16[224,1792]{1,0:T(8,128)(2,1)S(1)} %collective-permute-done.1.refs_5_.refs_12_) | copy-start | bytes 2408452
  37.9 6.2 %copy-start.11 = (bf16[224,1792]{1,0:T(8,128)(2,1)}, bf16[224,1792]{1,0:T(8,128)(2,1)S(1)}, u32[]{:S(2)}) copy-start(bf16[224,1792]{1,0:T(8,128)(2,1)S(1)} %collective-permute-done.refs_4_.refs_11_) | copy-start | bytes 2408452
  39.0 21.2 %all-to-all-start.1 = ((bf16[32,72,128]{2,1,0:T(8,128)(2,1)}), bf16[32,72,128]{2,1,0:T(8,128)(2,1)S(1)}, u32[]{:S(2)}, u32[]{:S(2)}) async-start(bf16[32,72,128]{2,1,0:T(8,128)(2,1)} %dispatch.1), calls=%async_computation.1 | async-start | bytes 1179648 | tf_op jit(solution)/shard_map/dispatch/all_to_all | solution.py:464
  44.9 22.4 %collective-permute-start.2 = (bf16[112,1792]{1,0:T(8,128)(2,1)}, bf16[112,1792]{1,0:T(8,128)(2,1)S(1)}, u32[]{:S(2)}, u32[]{:S(2)}) collective-permute-start(bf16[112,1792]{1,0:T(8,128)(2,1)} %slice.9), channel_id=1, source_target_pairs={{0,112},{16,0},{32,16},{48,32},{64,48},{80,64},{96,80},{112,96},{1... | collective-permute-start | bytes 1204232 | tf_op jit(solution)/shard_map/dispatch/ppermute | solution.py:519
  49.3 19.8 %collective-permute-start.3 = (bf16[112,1792]{1,0:T(8,128)(2,1)S(1)}, bf16[112,1792]{1,0:T(8,128)(2,1)S(1)}, u32[]{:S(2)}, u32[]{:S(2)}) collective-permute-start(bf16[112,1792]{1,0:T(8,128)(2,1)S(1)} %slice.10), channel_id=1, source_target_pairs={{0,16},{16,32},{32,48},{48,64},{64,80},{80,96},{96,112},{112,0},{1... | collective-permute-start | bytes 1204232 | tf_op jit(solution)/shard_map/dispatch/ppermute | solution.py:520
  53.0 7.2 %copy-start.2 = (bf16[1,224,1792]{2,1,0:T(8,128)(2,1)S(1)}, bf16[1,224,1792]{2,1,0:T(8,128)(2,1)}, u32[]{:S(2)}) copy-start(bf16[1,224,1792]{2,1,0:T(8,128)(2,1)} %param.16) | copy-start | bytes 2408452
  61.6 12.6 %all-to-all-start.2 = ((bf16[8,16,224]{2,1,0:T(8,128)(2,1)}), bf16[8,16,224]{2,1,0:T(8,128)(2,1)S(1)}, u32[]{:S(2)}, u32[]{:S(2)}) async-start(bf16[8,16,224]{2,1,0:T(8,128)(2,1)} %get-tuple-element.24), calls=%async_computation.2 | async-start | bytes 131072 | tf_op jit(solution)/shard_map/projection/all_to_all | solution.py:464
  67.3 6.7 %copy-start = (bf16[112,1792]{1,0:T(8,128)(2,1)}, bf16[112,1792]{1,0:T(8,128)(2,1)S(1)}, u32[]{:S(2)}) copy-start(bf16[112,1792]{1,0:T(8,128)(2,1)S(1)} %collective-permute-done.2.refs_6_.refs_13_) | copy-start | bytes 1204228
  69.1 4.9 %copy-start.1 = (bf16[112,1792]{1,0:T(8,128)(2,1)}, bf16[112,1792]{1,0:T(8,128)(2,1)S(1)}, u32[]{:S(2)}) copy-start(bf16[112,1792]{1,0:T(8,128)(2,1)S(1)} %collective-permute-done.3.refs_7_.refs_14_) | copy-start | bytes 1204228
  74.2 0.7 copy-start.3
  91.7 16.5 %all-to-all-start.4 = ((bf16[16,16,128]{2,1,0:T(8,128)(2,1)}), bf16[16,16,128]{2,1,0:T(8,128)(2,1)S(1)}, u32[]{:S(2)}, u32[]{:S(2)}) async-start(bf16[16,16,128]{2,1,0:T(8,128)(2,1)} %predict.4), calls=%async_computation.4 | async-start | bytes 131072 | tf_op jit(solution)/shard_map/predict/all_to_all | solution.py:464
  131.5 5.5 %copy-start.13 = (s32[2]{0:T(128)S(1)}, s32[2]{0:T(128)}, u32[]{:S(2)}) copy-start(s32[2]{0:T(128)} %param.21) | copy-start | bytes 28
  131.5 15.3 %all-to-all-start.6 = ((bf16[16,16,128]{2,1,0:T(8,128)(2,1)}), bf16[16,16,128]{2,1,0:T(8,128)(2,1)S(1)}, u32[]{:S(2)}, u32[]{:S(2)}) async-start(bf16[16,16,128]{2,1,0:T(8,128)(2,1)} %backward.4), calls=%async_computation.6 | async-start | bytes 131072 | tf_op jit(solution)/shard_map/backward/all_to_all | solution.py:464
  137.0 0.7 copy-start.14
  137.6 0.7 copy-start.12
  138.4 8.4 %copy-start.4 = (bf16[512,256]{1,0:T(8,128)(2,1)S(1)}, bf16[512,256]{1,0:T(8,128)(2,1)}, u32[]{:S(2)}) copy-start(bf16[512,256]{1,0:T(8,128)(2,1)} %get-tuple-element.31.refs_3_) | copy-start | bytes 786436

commit v6 on v5

--- a/solution.py
+++ b/solution.py
@@ -20,7 +20,6 @@
 TOK = 256
 HID = 224
 PACK = 64
-ROWS = 72
 FSDP = ("y", "zh", "zl")
 RING = ("zh", "zl")
 SHARERS = ("y", "zh")
@@ -71,38 +70,45 @@
     return out
 
 
-def routing_kernel(
-    place_ref, tokens_ref, routes_ref, weights_ref, targets_ref, head_ref,
-    sent_ref, pick_ref, base_ref, facts_ref,
-):
+def routing_kernel(place_ref, tokens_ref, routes_ref, weights_ref, targets_ref, sent_ref, pick_ref):
     shard = place_ref[0]
-    tokens = tokens_ref[...]
     expert = iota((GROUPS, TOK), 0)
     hits = [(routes_ref[k : k + 1, :] == expert).astype(f32) for k in range(TOPK)]
     below = (iota((TOK, TOK), 0) < iota((TOK, TOK), 1)).astype(bf16)
-    earlier = dot((hits[0] + hits[1]).astype(bf16), below)
+    named = hits[0] + hits[1]
+    earlier = dot(named.astype(bf16), below)
     slots = [jnp.sum(earlier * hit, axis=0, keepdims=True) for hit in hits]
     kept = [(slot < CAP).astype(f32) for slot in slots]
+    lost = (1.0 - kept[0]) * (1.0 - kept[1])
+    rank = dot(jnp.broadcast_to(lost, (8, TOK)).astype(bf16), below)[0:1]
+    full = jnp.minimum(jnp.sum(named, axis=1, keepdims=True), float(CAP))
+    empty = jnp.broadcast_to(CAP - full, (GROUPS, LANES))
+    order = (iota((GROUPS, GROUPS), 1) < iota((GROUPS, GROUPS), 0)).astype(bf16)
+    start = dot(order, empty.astype(bf16))[:, 0:1]
+    inside = (rank >= start) & (rank < start + CAP - full)
+    spare = jnp.where(inside, expert.astype(f32) * CAP + full + rank - start, 0.0)
+    spare = jnp.sum(spare, axis=0, keepdims=True)
     lane = iota((GROUPS * CAP, TOK), 0)
     places = []
     for k in range(TOPK):
-        dest = jnp.where(
-            kept[k] > 0.5, routes_ref[k : k + 1, :] * CAP + slots[k].astype(i32), -1
-        )
-        places.append((lane == dest).astype(f32))
+        dest = routes_ref[k : k + 1, :].astype(f32) * CAP + slots[k]
+        dest = jnp.where(kept[k] > 0.5, dest, -1.0)
+        if k == 0:
+            dest = jnp.where(lost > 0.5, spare, dest)
+        places.append((lane == dest.astype(i32)).astype(f32))
     pick_ref[...] = (places[0] + places[1]).astype(bf16)
     pick_ref.start()
 
-    target_high, target_low = high_low(targets_ref[...])
     row = iota((PACK, LANES), 0)
-    column = iota((PACK, LANES), 1)
-    pick_fact = (row >= FEAT) & (row < FEAT + 2) & (column == 2 * shard + row - FEAT)
-    pick_fact = pick_fact.astype(bf16)
-    body = jnp.concatenate([tokens.astype(f32), jnp.zeros((PACK - FEAT, TOK), f32)], axis=0)
+    pick_fact = ((row == FEAT) & (iota((PACK, LANES), 1) == shard)).astype(bf16)
+    body = jnp.concatenate(
+        [tokens_ref[...].astype(f32), jnp.zeros((PACK - FEAT, TOK), f32)], axis=0
+    )
+    line = iota((8, TOK), 0)
     packed = None
     for k in range(TOPK):
         other = 1 - k
-        own = high_low(weights_ref[k : k + 1, :])
+        own = high_low(weights_ref[k : k + 1, :] * kept[k])
         partner = high_low(weights_ref[other : other + 1, :] * kept[other])
         first = jnp.ones((1, TOK), f32) if k == 0 else 1.0 - kept[0]
         facts = [
@@ -111,12 +117,11 @@
             slots[other] * kept[other],
             first,
         ]
-        line = iota((8, TOK), 0)
         table = jnp.zeros((8, TOK), f32)
         for place, fact in enumerate(facts):
             table = jnp.where(line == place, fact, table)
         table = jnp.concatenate(
-            [target_high, target_low, table, jnp.zeros((LANES - 40, TOK), f32)], axis=0
+            [targets_ref[...], table, jnp.zeros((LANES - C_OUT - 8, TOK), f32)], axis=0
         )
         features = body + dot(pick_fact, table.astype(bf16))
         part = dot_nt(features.astype(bf16), places[k].astype(bf16))
@@ -128,46 +133,25 @@
         for b, piece in enumerate(lane_blocks(pieces)):
             sent_ref[4 * tile + b] = piece.astype(bf16)
 
-    base = dot(head_ref[...], tokens)
-    lost = (1.0 - kept[0]) * (1.0 - kept[1])
-    lost = jnp.broadcast_to(lost, (C_OUT, TOK))
-    stack = jnp.concatenate([base, targets_ref[...], lost], axis=0).T
-    stack = jnp.concatenate([stack, jnp.zeros((TOK, LANES - 3 * C_OUT), f32)], axis=1)
-    group = iota((SHARDS, LANES), 1) // C_OUT
-    for place in range(3):
-        total = jnp.zeros((SHARDS, LANES), f32)
-        for j in range(8):
-            piece = stack[SHARDS * j : SHARDS * (j + 1)]
-            shift = (C_OUT * (j - place)) % LANES
-            piece = pltpu.roll(piece, shift, axis=1) if shift else piece
-            total = jnp.where(group == j, piece, total)
-        if place == 0:
-            base_ref[...] = total
-        else:
-            facts_ref[place - 1] = total
-
-
-def parcel_kernel(arrived_ref, base_ref, head_ref, parcel_ref):
-    base_high, base_low = high_low(base_ref[...])
+
+def parcel_kernel(arrived_ref, head_ref, parcel_ref):
     row = iota((8, LANES), 0)
     head = head_ref[...].astype(f32)
     for q in range(4):
         tiles = lane_blocks([arrived_ref[4 * q + b].astype(f32) for b in range(4)])
-        body = jnp.concatenate([tiles[0], tiles[1], tiles[2], tiles[3][:8]], axis=0)
-        last = tiles[3][8:]
+        tail = jnp.where(row == 0, tiles[3][8:], head)
+        body = jnp.concatenate([tiles[0], tiles[1], tiles[2], tiles[3][:8], tail], axis=0)
+        body = body.astype(bf16)
         for high in range(8):
-            f = 4 * high + q
-            tail = jnp.where(row == 2, base_high[f : f + 1], last)
-            tail = jnp.where(row == 3, base_low[f : f + 1], tail)
-            parcel_ref[f] = jnp.concatenate([body, tail, head], axis=0).astype(bf16)
+            parcel_ref[4 * high + q] = body
 
 
 def head_kernel(gathered_ref, gate_ref, w_out_ref, proj_ref, head_ref):
     pieces = []
     for f in range(SHARDS):
-        rows = gathered_ref[f, PACK:ROWS].astype(f32)
+        rows = gathered_ref[f, FEAT:PACK].astype(f32)
         for i in range(FEAT // 8):
-            pieces.append(jnp.broadcast_to(rows[i : i + 1], (8, LANES)))
+            pieces.append(jnp.broadcast_to(rows[i + 1 : i + 2], (8, LANES)))
     spread = jnp.concatenate(pieces, axis=0)
     lane = iota((D, LANES), 1)
     spread = jnp.where(lane // C_OUT == iota((D, LANES), 0) % 8, spread, 0.0).astype(bf16)
@@ -234,38 +218,32 @@
 def base_kernel(gathered_ref, rows_ref, head_ref, base_ref, facts_ref):
     base = dot(rows_ref[...], head_ref[...]).T
     base_ref[...] = base[:C_OUT]
-    tails = [gathered_ref[f, FEAT:PACK].astype(f32) for f in range(SHARDS)]
-    facts = jnp.concatenate([tail[:2] for tail in tails], axis=0)
-    facts_ref[:PACK] = facts
-    facts_ref[PACK:] = functools.reduce(jnp.add, tails)
+    tails = [gathered_ref[f, FEAT:PACK].astype(f32)[:1] for f in range(SHARDS)]
+    facts_ref[...] = jnp.concatenate(tails, axis=0)
 
 
 def backward_kernel(
-    place_ref, shared_ref, base_ref, facts_ref, block_ref, proj_ref, slope_ref,
+    place_ref, shared_ref, base_ref, facts_ref, proj_ref, slope_ref,
     mod_ref, head_ref, rows_ref, w0_ref, w1_ref, w2_ref, w3_ref, w4_ref, parcel_ref,
 ):
-    shard, quarter, leader, sample = place_ref[0], place_ref[1], place_ref[2], place_ref[3]
+    quarter, leader = place_ref[1], place_ref[2]
     facts = facts_ref[...]
-    target = facts[:C_OUT] + facts[C_OUT : 2 * C_OUT]
-    own_w = facts[32:33] + facts[33:34]
-    other_w = facts[34:35] + facts[35:36]
-    first = facts[38:39]
+    target = facts[:C_OUT]
+    own_w = facts[16:17] + facts[17:18]
+    other_w = facts[18:19] + facts[19:20]
+    first = facts[22:23]
     lane = iota((1, LANES), 1)
-    source = facts[36:37].astype(i32) * LANES + facts[37:38].astype(i32) + lane // CAP * CAP
+    source = facts[20:21].astype(i32) * LANES + facts[21:22].astype(i32) + lane // CAP * CAP
     chosen = (iota((GROUPS * LANES, LANES), 0) == source).astype(f32).astype(bf16)
     everyone = jnp.concatenate([shared_ref[e] for e in range(GROUPS)], axis=1)
     partner = dot(everyone, chosen)
     residue = base_ref[...] + own_w * shared_ref[place_ref[5]].astype(f32) + other_w * partner - target
     kept_err = jnp.sum(first * residue * residue, keepdims=True)
 
-    lost_base = facts[PACK + 2 : PACK + 3] + facts[PACK + 3 : PACK + 4]
-    lost = (lost_base - block_ref[0, pl.ds(shard, 1), :]) * block_ref[1, pl.ds(shard, 1), :]
-    lost_err = jnp.sum(lost * lost, keepdims=True)
     err = jnp.where((lane == quarter) & (leader == 1), kept_err, 0.0)
-    err = err + jnp.where(lane == sample, lost_err, 0.0)
     row = iota((8, LANES), 0)
     tail = jnp.zeros((8, LANES), f32)
-    for place, values in enumerate(high_low(lost) + high_low(err)):
+    for place, values in enumerate(high_low(err)):
         tail = jnp.where(row == place, values, tail)
 
     upstream = jnp.concatenate(high_low((own_w * residue).T), axis=1).astype(bf16)
@@ -302,7 +280,7 @@
         sums.append(total[:FEAT])
         tails.append(total[FEAT:])
     tail = tails[0] + tails[1] + tails[2] + tails[3]
-    err = jnp.where(lane < SAMPLES, tail[2:3] + tail[3:4], 0.0)
+    err = jnp.where(lane < SAMPLES, tail[0:1] + tail[1:2], 0.0)
     err = err + pltpu.roll(err, CAP, axis=1)
     err = err + pltpu.roll(err, 2 * CAP, axis=1)
     high, low = high_low(err)
@@ -314,20 +292,8 @@
             home_ref[4 * q + b] = tiles[b].astype(bf16)
 
 
-def direct_kernel(parcel_ref, head_ref, direct_ref):
-    tails = [parcel_ref[f, FEAT:].astype(f32) for f in range(SHARDS)]
-    lane = iota((SHARDS, LANES), 1) // C_OUT
-    head_tile = jnp.concatenate([head_ref[...]] * 8, axis=0).astype(f32).T.astype(bf16)
-    direct = 0.0
-    for part in range(2):
-        rows = jnp.concatenate([tail[part : part + 1] for tail in tails], axis=0)
-        lost = [jnp.where(lane == j, rows, 0.0) for j in range(8)]
-        direct = direct + dot_nt(head_tile, jnp.concatenate(lost, axis=0).astype(bf16))
-    direct_ref[...] = direct
-
-
 def end_kernel(
-    place_ref, levels_ref, home_ref, pick_ref, direct_ref,
+    place_ref, levels_ref, home_ref, pick_ref,
     grad_ref, loss_ref,
 ):
     sample = place_ref[3].astype(f32)
@@ -361,7 +327,7 @@
         coef = coef - jnp.where(loser == sample, rate, 0.0)
     loss_ref[...] = loss[0:1, 0:1] * 0.5
     coef = coef[0:1, 0:1] * (TOK * GROUPS * C_OUT * 2.0 / (TOK * GROUPS // SAMPLES * C_OUT))
-    grad_ref[...] = (coef * (direct_ref[...] + back[:FEAT])).astype(bf16)
+    grad_ref[...] = (coef * back[:FEAT]).astype(bf16)
 
 
 class Fetched:
@@ -496,17 +462,12 @@
         w_after = lax.ppermute(w_in, RING, down)
 
     with jax.named_scope("routing"):
-        sent, pick, base, block = call(
+        sent, pick = call(
             routing_kernel,
             [place],
-            [tokens.T, routes.T, route_weights.T, targets.T, head],
-            [
-                ((GROUPS, 16, LANES), bf16),
-                ((GROUPS * CAP, TOK), bf16),
-                ((SHARDS, LANES), f32),
-                ((2, SHARDS, LANES), f32),
-            ],
-            store=(1, 3),
+            [tokens.T, routes.T, route_weights.T, targets.T],
+            [((GROUPS, 16, LANES), bf16), ((GROUPS * CAP, TOK), bf16)],
+            store=(1,),
         )
     with jax.named_scope("dispatch"):
         arrived = swap(sent, "expert")
@@ -519,10 +480,8 @@
             lax.ppermute(w_after[:half], RING, down),
             lax.ppermute(w_before[half:], RING, up),
         ]
-        head_flat = jnp.pad(head.T.reshape(FEAT // 8, LANES), ((0, 1), (0, 0)))
-        (parcel,) = call(
-            parcel_kernel, [], [arrived, base, head_flat], [((SHARDS, ROWS, LANES), bf16)]
-        )
+        head_flat = jnp.pad(head.T.reshape(FEAT // 8, LANES), ((1, 0), (0, 0)))
+        (parcel,) = call(parcel_kernel, [], [arrived, head_flat], [((SHARDS, PACK, LANES), bf16)])
         gathered = swap(parcel, FSDP)
 
     with jax.named_scope("projection"):
@@ -555,7 +514,7 @@
         parts = swap(part, SHARERS)
         (shared,) = call(own_kernel, [], [parts], [((GROUPS, C_OUT, LANES), bf16)])
         base_rows, facts = call(
-            base_kernel, [], [gathered, rows, head_all], [((C_OUT, LANES), f32), ((72, LANES), f32)],
+            base_kernel, [], [gathered, rows, head_all], [((C_OUT, LANES), f32), ((SHARDS, LANES), f32)],
             fetch=(1, 2),
             store=(0, 1),
         )
@@ -565,22 +524,21 @@
         (parcel,) = call(
             backward_kernel,
             [place],
-            [shared, base_rows, facts, block, proj, slope, mod, head_all, rows]
+            [shared, base_rows, facts, proj, slope, mod, head_all, rows]
             + weights,
             [((SHARDS, PACK, LANES), bf16)],
-            fetch=(1, 2, 3, 4, 5, 9, 10, 11, 12, 13, 6, 7, 8),
+            fetch=(1, 2, 3, 4, 8, 9, 10, 11, 12, 5, 6, 7),
             flops=8 * D * HID * LANES,
         )
         parcel = swap(parcel, FSDP)
         (home,) = call(mid_kernel, [], [parcel], [((GROUPS, 16, LANES), bf16)])
-        (direct,) = call(direct_kernel, [], [parcel, head], [((FEAT, TOK), f32)])
         home = swap(home, "expert")
 
     with jax.named_scope("finish"):
         grad_tokens, loss = call(
             end_kernel,
             [place, levels],
-            [home, pick, direct],
+            [home, pick],
             [((FEAT, TOK), bf16), ((1, 1), f32)],
         )
     return (grad_tokens.T, loss.reshape(()))

time: 149 us -> 148 us (level)
    pallas_call x11 -> x10, Pallas kernels: 20 us -> 19.4 us  [call(): pl.pallas_call(body, out_shape=out_shape, in_specs=[smem] * len(scalars)...]
  transfers between devices with their start and end apart: 9 -> 9, of which waited for: 7 -> 6; matrix products, arithmetic and copies ran while one was open for 3% -> 3% of each run, Pallas kernels for 8% -> 7%
where the time goes in v6:
time: 148 us; the launch traced here: 147 us
  starting transfers between devices  53 us (36%)
  blocking collectives  34.3 us (23%)
  waiting for transfers between devices  32.6 us (22%)
  Pallas kernels  19.4 us (13%)
  local copies, waits for them, and re-layouts  6.41 us (4%)
    all_to_all x2, blocking collectives, swap(): return lax.all_to_all(chunks, axis, split_axis=0, concat_axis=0, tiled=True)  34.3 us
    all_to_all x5, starting transfers between devices, swap(): return lax.all_to_all(chunks, axis, split_axis=0, concat_axis=0, tiled=True)  33.3 us
    all_to_all x5, waiting for transfers between devices, swap(): return lax.all_to_all(chunks, axis, split_axis=0, concat_axis=0, tiled=True)  30 us
    pallas_call x10, Pallas kernels, call(): pl.pallas_call(body, out_shape=out_shape, in_specs=[smem] * len(scalars)...  19.4 us
    ppermute x1, starting transfers between devices, local(): w_after = lax.ppermute(w_in, RING, down)  11.5 us
    ppermute x1, starting transfers between devices, local(): lax.ppermute(w_after[:half], RING, down)  4.34 us
  transfers between devices with their start and end apart: 9, of which 6 were waited for; matrix products, arithmetic and copies ran while one was open for 3% of the time, Pallas kernels for 7%

profile of v6, /device:TPU:1, one launch (start us, length us, event | category | flops | bytes accessed | tf_op | source)
XLA Modules:
  0.0 146.7 jit_solution(15274154560800891316)
XLA Ops:
  0.6 11.5 %collective-permute-start.1 = (bf16[224,1792]{1,0:T(8,128)(2,1)}, bf16[224,1792]{1,0:T(8,128)(2,1)S(1)}, u32[]{:S(2)}, u32[]{:S(2)}) collective-permute-start(bf16[224,1792]{1,0:T(8,128)(2,1)} %bitcast.30), channel_id=1, source_target_pairs={{0,112},{16,0},{32,16},{48,32},{64,48},{80,64},{96,80},{112,96},{1... | collective-permute-start | bytes 2408456 | tf_op jit(solution)/shard_map/weights/ppermute | solution.py:462
  12.1 1.9 %collective-permute-start = (bf16[224,1792]{1,0:T(8,128)(2,1)}, bf16[224,1792]{1,0:T(8,128)(2,1)S(1)}, u32[]{:S(2)}, u32[]{:S(2)}) collective-permute-start(bf16[224,1792]{1,0:T(8,128)(2,1)} %bitcast.31), channel_id=1, source_target_pairs={{0,16},{16,32},{32,48},{48,64},{64,80},{80,96},{96,112},{112,0},{1... | collective-permute-start | bytes 2408456 | tf_op jit(solution)/shard_map/weights/ppermute | solution.py:461
  14.9 2.3 %routing.1 = (bf16[16,16,128]{2,1,0:T(8,128)(2,1)}, bf16[512,256]{1,0:T(8,128)(2,1)}) custom-call(s32[6]{0:T(128)S(1)} %stack.31.refs_0_, bf16[56,256]{1,0:T(8,128)(2,1)S(1)} %bitcast.25, s32[2,256]{1,0:T(2,128)S(1)} %bitcast.27, f32[2,256]{1,0:T(2,128)S(1)} %bitcast.28, f32[16,256]{1,0:T(8,128)S(1)} %bitcast.26), custom_call_target="tpu_custom_call" | custom-call | bytes 49152 | tf_op jit(solution)/shard_map/routing/pallas_call | solution.py:417
  17.2 10.5 %all-to-all-start = ((bf16[16,16,128]{2,1,0:T(8,128)(2,1)}), bf16[16,16,128]{2,1,0:T(8,128)(2,1)S(1)}, u32[]{:S(2)}, u32[]{:S(2)}) async-start(bf16[16,16,128]{2,1,0:T(8,128)(2,1)} %get-tuple-element.16), calls=%async_computation | async-start | bytes 131072 | tf_op jit(solution)/shard_map/dispatch/all_to_all | solution.py:430
  27.9 9.5 %all-to-all-done.refs_0_ = bf16[16,16,128]{2,1,0:T(8,128)(2,1)S(1)} async-done(((bf16[16,16,128]{2,1,0:T(8,128)(2,1)}), bf16[16,16,128]{2,1,0:T(8,128)(2,1)S(1)}, u32[]{:S(2)}, u32[]{:S(2)}) %all-to-all-start) | async-done | bytes 65568 | tf_op jit(solution)/shard_map/dispatch/all_to_all | solution.py:430
  37.5 1.1 dispatch.1
  38.5 5.1 %all-to-all-start.1 = ((bf16[32,64,128]{2,1,0:T(8,128)(2,1)}), bf16[32,64,128]{2,1,0:T(8,128)(2,1)S(1)}, u32[]{:S(2)}, u32[]{:S(2)}) async-start(bf16[32,64,128]{2,1,0:T(8,128)(2,1)} %dispatch.1), calls=%async_computation.1 | async-start | bytes 1048576 | tf_op jit(solution)/shard_map/dispatch/all_to_all | solution.py:430
  43.7 0.8 slice.9
  44.5 4.3 %collective-permute-start.2 = (bf16[112,1792]{1,0:T(8,128)(2,1)}, bf16[112,1792]{1,0:T(8,128)(2,1)S(1)}, u32[]{:S(2)}, u32[]{:S(2)}) collective-permute-start(bf16[112,1792]{1,0:T(8,128)(2,1)} %slice.9), channel_id=1, source_target_pairs={{0,112},{16,0},{32,16},{48,32},{64,48},{80,64},{96,80},{112,96},{1... | collective-permute-start | bytes 1204232 | tf_op jit(solution)/shard_map/dispatch/ppermute | solution.py:480
  48.8 1.9 %collective-permute-start.3 = (bf16[112,1792]{1,0:T(8,128)(2,1)S(1)}, bf16[112,1792]{1,0:T(8,128)(2,1)S(1)}, u32[]{:S(2)}, u32[]{:S(2)}) collective-permute-start(bf16[112,1792]{1,0:T(8,128)(2,1)S(1)} %slice.10), channel_id=1, source_target_pairs={{0,16},{16,32},{32,48},{48,64},{64,80},{80,96},{96,112},{112,0},{1... | collective-permute-start | bytes 1204232 | tf_op jit(solution)/shard_map/dispatch/ppermute | solution.py:481
  50.8 0.8 slice_bitcast_fusion
  51.6 1.0 tile.11
  52.6 1.5 %copy.16.refs_1_ = f32[1792,128]{1,0:T(8,128)S(1)} copy(f32[1792,128]{0,1:T(8,128)} %bitcast.29) | data formatting | bytes 1835008 | tf_op jit(solution)/shard_map/projection/tile | solution.py:488
  54.1 4.5 %all-to-all-done.1.refs_1_.refs_0_ = bf16[32,64,128]{2,1,0:T(8,128)(2,1)S(1)} async-done(((bf16[32,64,128]{2,1,0:T(8,128)(2,1)}), bf16[32,64,128]{2,1,0:T(8,128)(2,1)S(1)}, u32[]{:S(2)}, u32[]{:S(2)}) %all-to-all-start.1) | async-done | bytes 524320 | tf_op jit(solution)/shard_map/dispatch/all_to_all | solution.py:430
  58.6 1.4 projection.1
  60.0 5.0 %all-to-all-start.2 = ((bf16[8,16,224]{2,1,0:T(8,128)(2,1)}), bf16[8,16,224]{2,1,0:T(8,128)(2,1)S(1)}, u32[]{:S(2)}, u32[]{:S(2)}) async-start(bf16[8,16,224]{2,1,0:T(8,128)(2,1)} %get-tuple-element.21), calls=%async_computation.2 | async-start | bytes 131072 | tf_op jit(solution)/shard_map/projection/all_to_all | solution.py:430
  65.0 0.7 collective-permute-done.2.refs_6_.refs_12_
  65.7 1.9 %collective-permute-done.3.refs_7_.refs_13_ = bf16[112,1792]{1,0:T(8,128)(2,1)S(1)} collective-permute-done((bf16[112,1792]{1,0:T(8,128)(2,1)S(1)}, bf16[112,1792]{1,0:T(8,128)(2,1)S(1)}, u32[]{:S(2)}, u32[]{:S(2)}) %collective-permute-start.3) | collective-permute-done | bytes 401440 | tf_op jit(solution)/shard_map/dispatch/ppermute | solution.py:481
  67.6 4.9 %first_layer.1 = (bf16[4,128,224]{2,1,0:T(8,128)(2,1)S(1)}, f32[4,128,224]{2,1,0:T(8,128)}, bf16[128,1792]{1,0:T(8,128)(2,1)}) custom-call(s32[6]{0:T(128)S(1)} %stack.31.refs_0_, bf16[32,64,128]{2,1,0:T(8,128)(2,1)S(1)} %all-to-all-done.1.refs_1_.refs_0_, f32[3,4,1792]{2,1,0:T(4,128)} %bitcast.36, bf16[224,1792]{1,0:T(8,128)(2,1)} %bitcast.32, ...), custom_call_target="tpu_custom_call" | custom-call | flops 411041792 | bytes 3821568 | tf_op jit(solution)/shard_map/first_layer/pallas_call | solution.py:417
  72.6 0.7 predict.3
  73.3 16.0 %all_to_all.35.refs_0_ = f32[8,16,128]{2,1,0:T(8,128)S(1)} all-to-all(f32[8,16,128]{2,1,0:T(8,128)S(1)} %predict.3), channel_id=1, replica_groups=mesh['y'=4,'zh'=2,'zl'=4,'expert'=16] {'y','zh'}, dimensions={0} | all-to-all | bytes 131072 | tf_op jit(solution)/shard_map/predict/all_to_all | solution.py:430
  89.3 0.6 predict.4
  89.9 7.2 %all-to-all-start.4 = ((bf16[16,16,128]{2,1,0:T(8,128)(2,1)}), bf16[16,16,128]{2,1,0:T(8,128)(2,1)S(1)}, u32[]{:S(2)}, u32[]{:S(2)}) async-start(bf16[16,16,128]{2,1,0:T(8,128)(2,1)} %predict.4), calls=%async_computation.4 | async-start | bytes 131072 | tf_op jit(solution)/shard_map/predict/all_to_all | solution.py:430
  97.1 2.1 %predict.5 = (f32[16,128]{1,0:T(8,128)}, f32[32,128]{1,0:T(8,128)}) custom-call(bf16[32,64,128]{2,1,0:T(8,128)(2,1)S(1)} %all-to-all-done.1.refs_1_.refs_0_, bf16[128,1792]{1,0:T(8,128)(2,1)} %get-tuple-element.22.refs_1_.refs_8_, bf16[1792,128]{1,0:T(8,128)(2,1)} %get-tuple-element.23.refs_2_.refs_7_), custom_call_target="tpu_custom_call" | custom-call | bytes 1441792 | tf_op jit(solution)/shard_map/predict/pallas_call | solution.py:417
  99.2 7.6 %all-to-all-done.4.refs_1_ = bf16[16,16,128]{2,1,0:T(8,128)(2,1)S(1)} async-done(((bf16[16,16,128]{2,1,0:T(8,128)(2,1)}), bf16[16,16,128]{2,1,0:T(8,128)(2,1)S(1)}, u32[]{:S(2)}, u32[]{:S(2)}) %all-to-all-start.4) | async-done | bytes 65568 | tf_op jit(solution)/shard_map/predict/all_to_all | solution.py:430
  106.8 4.1 %backward.2 = bf16[32,64,128]{2,1,0:T(8,128)(2,1)S(1)} custom-call(s32[6]{0:T(128)S(1)} %stack.31.refs_0_, bf16[16,16,128]{2,1,0:T(8,128)(2,1)S(1)} %all-to-all-done.4.refs_1_, f32[16,128]{1,0:T(8,128)} %get-tuple-element.24.refs_2_, f32[32,128]{1,0:T(8,128)} %get-tuple-element.25.refs_3_, bf16[8,16,224]{2,1,0:T(8,128)(2,1)} %copy-done.3, ...), custom_call_target="tpu_custom_call" | custom-call | flops 411041792 | bytes 4820992 | tf_op jit(solution)/shard_map/backward/pallas_call | solution.py:417
  110.9 18.3 %all_to_all.36.refs_0_ = bf16[32,64,128]{2,1,0:T(8,128)(2,1)S(1)} all-to-all(bf16[32,64,128]{2,1,0:T(8,128)(2,1)S(1)} %backward.2), channel_id=1, replica_groups=mesh['y'=4,'zh'=2,'zl'=4,'expert'=16] {'y','zh','zl'}, dimensions={0} | all-to-all | bytes 1048576 | tf_op jit(solution)/shard_map/backward/all_to_all | solution.py:430
  129.2 0.9 backward.3
  130.0 5.5 %all-to-all-start.6 = ((bf16[16,16,128]{2,1,0:T(8,128)(2,1)}), bf16[16,16,128]{2,1,0:T(8,128)(2,1)S(1)}, u32[]{:S(2)}, u32[]{:S(2)}) async-start(bf16[16,16,128]{2,1,0:T(8,128)(2,1)} %backward.3), calls=%async_computation.6 | async-start | bytes 131072 | tf_op jit(solution)/shard_map/backward/all_to_all | solution.py:430
  136.2 0.7 copy-done.12
  136.9 8.4 %all-to-all-done.6.refs_2_ = bf16[16,16,128]{2,1,0:T(8,128)(2,1)S(1)} async-done(((bf16[16,16,128]{2,1,0:T(8,128)(2,1)}), bf16[16,16,128]{2,1,0:T(8,128)(2,1)S(1)}, u32[]{:S(2)}, u32[]{:S(2)}) %all-to-all-start.6) | async-done | bytes 65568 | tf_op jit(solution)/shard_map/backward/all_to_all | solution.py:430
  145.3 1.4 finish.1
  (41 shorter events, 1.8 us)
Async XLA Ops:
  0.6 36.8 %collective-permute-start.1 = (bf16[224,1792]{1,0:T(8,128)(2,1)}, bf16[224,1792]{1,0:T(8,128)(2,1)S(1)}, u32[]{:S(2)}, u32[]{:S(2)}) collective-permute-start(bf16[224,1792]{1,0:T(8,128)(2,1)} %bitcast.30), channel_id=1, source_target_pairs={{0,112},{16,0},{32,16},{48,32},{64,48},{80,64},{96,80},{112,96},{1... | collective-permute-start | bytes 2408456 | tf_op jit(solution)/shard_map/weights/ppermute | solution.py:462
  12.1 25.3 %collective-permute-start = (bf16[224,1792]{1,0:T(8,128)(2,1)}, bf16[224,1792]{1,0:T(8,128)(2,1)S(1)}, u32[]{:S(2)}, u32[]{:S(2)}) collective-permute-start(bf16[224,1792]{1,0:T(8,128)(2,1)} %bitcast.31), channel_id=1, source_target_pairs={{0,16},{16,32},{32,48},{48,64},{64,80},{80,96},{96,112},{112,0},{1... | collective-permute-start | bytes 2408456 | tf_op jit(solution)/shard_map/weights/ppermute | solution.py:461
  14.1 0.7 copy-start.5
  14.1 0.7 copy-start.6
  14.2 0.7 copy-start.8
  14.2 0.7 copy-start.7
  17.2 10.6 %copy-start.11 = (bf16[16,56]{1,0:T(8,128)(2,1)S(1)}, bf16[16,56]{1,0:T(8,128)(2,1)}, u32[]{:S(2)}) copy-start(bf16[16,56]{1,0:T(8,128)(2,1)} %param.17) | copy-start | bytes 5380
  17.2 20.3 %all-to-all-start = ((bf16[16,16,128]{2,1,0:T(8,128)(2,1)}), bf16[16,16,128]{2,1,0:T(8,128)(2,1)S(1)}, u32[]{:S(2)}, u32[]{:S(2)}) async-start(bf16[16,16,128]{2,1,0:T(8,128)(2,1)} %get-tuple-element.16), calls=%async_computation | async-start | bytes 131072 | tf_op jit(solution)/shard_map/dispatch/all_to_all | solution.py:430
  37.5 6.2 %copy-start.9 = (bf16[224,1792]{1,0:T(8,128)(2,1)}, bf16[224,1792]{1,0:T(8,128)(2,1)S(1)}, u32[]{:S(2)}) copy-start(bf16[224,1792]{1,0:T(8,128)(2,1)S(1)} %collective-permute-done.1.refs_5_.refs_11_) | copy-start | bytes 2408452
  37.5 6.2 %copy-start.10 = (bf16[224,1792]{1,0:T(8,128)(2,1)}, bf16[224,1792]{1,0:T(8,128)(2,1)S(1)}, u32[]{:S(2)}) copy-start(bf16[224,1792]{1,0:T(8,128)(2,1)S(1)} %collective-permute-done.refs_4_.refs_10_) | copy-start | bytes 2408452
  38.5 20.1 %all-to-all-start.1 = ((bf16[32,64,128]{2,1,0:T(8,128)(2,1)}), bf16[32,64,128]{2,1,0:T(8,128)(2,1)S(1)}, u32[]{:S(2)}, u32[]{:S(2)}) async-start(bf16[32,64,128]{2,1,0:T(8,128)(2,1)} %dispatch.1), calls=%async_computation.1 | async-start | bytes 1048576 | tf_op jit(solution)/shard_map/dispatch/all_to_all | solution.py:430
  44.5 21.2 %collective-permute-start.2 = (bf16[112,1792]{1,0:T(8,128)(2,1)}, bf16[112,1792]{1,0:T(8,128)(2,1)S(1)}, u32[]{:S(2)}, u32[]{:S(2)}) collective-permute-start(bf16[112,1792]{1,0:T(8,128)(2,1)} %slice.9), channel_id=1, source_target_pairs={{0,112},{16,0},{32,16},{48,32},{64,48},{80,64},{96,80},{112,96},{1... | collective-permute-start | bytes 1204232 | tf_op jit(solution)/shard_map/dispatch/ppermute | solution.py:480
  48.8 18.8 %collective-permute-start.3 = (bf16[112,1792]{1,0:T(8,128)(2,1)S(1)}, bf16[112,1792]{1,0:T(8,128)(2,1)S(1)}, u32[]{:S(2)}, u32[]{:S(2)}) collective-permute-start(bf16[112,1792]{1,0:T(8,128)(2,1)S(1)} %slice.10), channel_id=1, source_target_pairs={{0,16},{16,32},{32,48},{48,64},{64,80},{80,96},{96,112},{112,0},{1... | collective-permute-start | bytes 1204232 | tf_op jit(solution)/shard_map/dispatch/ppermute | solution.py:481
  52.6 6.0 %copy-start.2 = (bf16[1,224,1792]{2,1,0:T(8,128)(2,1)S(1)}, bf16[1,224,1792]{2,1,0:T(8,128)(2,1)}, u32[]{:S(2)}) copy-start(bf16[1,224,1792]{2,1,0:T(8,128)(2,1)} %param.16) | copy-start | bytes 2408452
  60.0 12.5 %all-to-all-start.2 = ((bf16[8,16,224]{2,1,0:T(8,128)(2,1)}), bf16[8,16,224]{2,1,0:T(8,128)(2,1)S(1)}, u32[]{:S(2)}, u32[]{:S(2)}) async-start(bf16[8,16,224]{2,1,0:T(8,128)(2,1)} %get-tuple-element.21), calls=%async_computation.2 | async-start | bytes 131072 | tf_op jit(solution)/shard_map/projection/all_to_all | solution.py:430
  65.7 6.8 %copy-start = (bf16[112,1792]{1,0:T(8,128)(2,1)}, bf16[112,1792]{1,0:T(8,128)(2,1)S(1)}, u32[]{:S(2)}) copy-start(bf16[112,1792]{1,0:T(8,128)(2,1)S(1)} %collective-permute-done.2.refs_6_.refs_12_) | copy-start | bytes 1204228
  67.6 4.9 %copy-start.1 = (bf16[112,1792]{1,0:T(8,128)(2,1)}, bf16[112,1792]{1,0:T(8,128)(2,1)S(1)}, u32[]{:S(2)}) copy-start(bf16[112,1792]{1,0:T(8,128)(2,1)S(1)} %collective-permute-done.3.refs_7_.refs_13_) | copy-start | bytes 1204228
  72.6 0.7 copy-start.3
  89.9 16.9 %all-to-all-start.4 = ((bf16[16,16,128]{2,1,0:T(8,128)(2,1)}), bf16[16,16,128]{2,1,0:T(8,128)(2,1)S(1)}, u32[]{:S(2)}, u32[]{:S(2)}) async-start(bf16[16,16,128]{2,1,0:T(8,128)(2,1)} %predict.4), calls=%async_computation.4 | async-start | bytes 131072 | tf_op jit(solution)/shard_map/predict/all_to_all | solution.py:430
  129.2 16.1 %copy-start.4 = (bf16[512,256]{1,0:T(8,128)(2,1)S(1)}, bf16[512,256]{1,0:T(8,128)(2,1)}, u32[]{:S(2)}) copy-start(bf16[512,256]{1,0:T(8,128)(2,1)} %get-tuple-element.27.refs_3_) | copy-start | bytes 786436
  130.0 5.5 %copy-start.13 = (s32[2]{0:T(128)S(1)}, s32[2]{0:T(128)}, u32[]{:S(2)}) copy-start(s32[2]{0:T(128)} %param.21) | copy-start | bytes 28
  130.0 15.3 %all-to-all-start.6 = ((bf16[16,16,128]{2,1,0:T(8,128)(2,1)}), bf16[16,16,128]{2,1,0:T(8,128)(2,1)S(1)}, u32[]{:S(2)}, u32[]{:S(2)}) async-start(bf16[16,16,128]{2,1,0:T(8,128)(2,1)} %backward.3), calls=%async_computation.6 | async-start | bytes 131072 | tf_op jit(solution)/shard_map/backward/all_to_all | solution.py:430
  135.5 0.7 copy-start.14
  136.2 0.7 copy-start.12

commit v7 on v6

--- a/solution.py
+++ b/solution.py
@@ -170,7 +170,8 @@
 
 
 def first_kernel(
-    place_ref, gathered_ref, mod_ref, w0_ref, w1_ref, w2_ref, w3_ref, w4_ref, act_ref, slope_ref, rows_ref
+    place_ref, gathered_ref, mod_ref, w0_ref, w1_ref, w2_ref, w3_ref, w4_ref, head_ref,
+    act_ref, slope_ref, rows_ref, base_ref, facts_ref,
 ):
     rows = jnp.concatenate([gathered_ref[f, :FEAT].astype(f32) for f in range(SHARDS)], axis=0).T
     rows_ref[...] = rows.astype(bf16)
@@ -191,6 +192,9 @@
             cubic * (1.0 + 3.0 * 0.044715 * square)
         )
         slope_ref.start(b)
+    base_ref[...] = dot(rows.astype(bf16), head_ref[...]).T[:C_OUT]
+    tails = [gathered_ref[f, FEAT:PACK].astype(f32)[:1] for f in range(SHARDS)]
+    facts_ref[...] = jnp.concatenate(tails, axis=0)
 
 
 def held_projections(proj_ref, z):
@@ -213,13 +217,6 @@
     own = jnp.sum(parts_ref[...], axis=0).astype(bf16)
     for e in range(GROUPS):
         shared_ref[e] = own
-
-
-def base_kernel(gathered_ref, rows_ref, head_ref, base_ref, facts_ref):
-    base = dot(rows_ref[...], head_ref[...]).T
-    base_ref[...] = base[:C_OUT]
-    tails = [gathered_ref[f, FEAT:PACK].astype(f32)[:1] for f in range(SHARDS)]
-    facts_ref[...] = jnp.concatenate(tails, axis=0)
 
 
 def backward_kernel(
@@ -470,6 +467,8 @@
             store=(1,),
         )
     with jax.named_scope("dispatch"):
+        head_flat = jnp.pad(head.T.reshape(FEAT // 8, LANES), ((1, 0), (0, 0)))
+        sent, head_flat = lax.optimization_barrier((sent, head_flat))
         arrived = swap(sent, "expert")
         arrived, w_before, w_after = lax.optimization_barrier((arrived, w_before, w_after))
         half = HID // 2
@@ -480,9 +479,8 @@
             lax.ppermute(w_after[:half], RING, down),
             lax.ppermute(w_before[half:], RING, up),
         ]
-        head_flat = jnp.pad(head.T.reshape(FEAT // 8, LANES), ((1, 0), (0, 0)))
         (parcel,) = call(parcel_kernel, [], [arrived, head_flat], [((SHARDS, PACK, LANES), bf16)])
-        gathered = swap(parcel, FSDP)
+        gathered, levels = lax.optimization_barrier((swap(parcel, FSDP), levels))
 
     with jax.named_scope("projection"):
         gate = jnp.tile(jnp.repeat(mod[2].T, C_OUT, axis=1), (1, 2))
@@ -496,13 +494,13 @@
         proj = swap(proj, RING)
 
     with jax.named_scope("first_layer"):
-        act, slope, rows = call(
+        act, slope, rows, base_rows, facts = call(
             first_kernel,
             [place],
-            [gathered, mod] + weights,
-            [((4, LANES, HID), bf16), ((4, LANES, HID), f32), ((LANES, D), bf16)],
-            fetch=(1, 2, 3, 4),
-            store=(1, 2),
+            [gathered, mod] + weights + [head_all],
+            [((4, LANES, HID), bf16), ((4, LANES, HID), f32), ((LANES, D), bf16), ((C_OUT, LANES), f32), ((SHARDS, LANES), f32)],
+            fetch=(1, 2, 3, 4, 7),
+            store=(1, 2, 3, 4),
             parts={1: 4},
             flops=8 * D * HID * LANES,
         )
@@ -513,11 +511,6 @@
         )
         parts = swap(part, SHARERS)
         (shared,) = call(own_kernel, [], [parts], [((GROUPS, C_OUT, LANES), bf16)])
-        base_rows, facts = call(
-            base_kernel, [], [gathered, rows, head_all], [((C_OUT, LANES), f32), ((SHARDS, LANES), f32)],
-            fetch=(1, 2),
-            store=(0, 1),
-        )
         shared = swap(shared, "expert")
 
     with jax.named_scope("backward"):

time: 148 us -> 145 us (0.980)
  blocking collectives: 34.3 us -> 85.2 us
  waiting for transfers between devices: 32.6 us -> 6.43 us
  starting transfers between devices: 53 us -> 29.8 us
  Pallas kernels: 19.4 us -> 15.5 us
    all_to_all x2 -> x5, blocking collectives: 34.3 us -> 85.2 us  [swap(): return lax.all_to_all(chunks, axis, split_axis=0, concat_axis=0, tiled=True)]
    all_to_all x5 -> x2, waiting for transfers between devices: 30 us -> 3.73 us  [swap(): return lax.all_to_all(chunks, axis, split_axis=0, concat_axis=0, tiled=True)]
    all_to_all x5 -> x2, starting transfers between devices: 33.3 us -> 10.1 us  [swap(): return lax.all_to_all(chunks, axis, split_axis=0, concat_axis=0, tiled=True)]
    pallas_call x10 -> x9, Pallas kernels: 19.4 us -> 15.5 us  [call(): pl.pallas_call(body, out_shape=out_shape, in_specs=[smem] * len(scalars)...]
  transfers between devices with their start and end apart: 9 -> 6, of which waited for: 6 -> 3; matrix products, arithmetic and copies ran while one was open for 3% -> 3% of each run, Pallas kernels for 7% -> 6%
where the time goes in v7:
time: 145 us; the launch traced here: 144 us
  blocking collectives  85.2 us (59%)
  starting transfers between devices  29.8 us (21%)
  Pallas kernels  15.5 us (11%)
  local copies, waits for them, and re-layouts  6.43 us (4%)
  waiting for transfers between devices  6.43 us (4%)
    all_to_all x5, blocking collectives, swap(): return lax.all_to_all(chunks, axis, split_axis=0, concat_axis=0, tiled=True)  85.2 us
    pallas_call x9, Pallas kernels, call(): pl.pallas_call(body, out_shape=out_shape, in_specs=[smem] * len(scalars)...  15.5 us
    ppermute x1, starting transfers between devices, local(): w_after = lax.ppermute(w_in, RING, down)  11.5 us
    all_to_all x2, starting transfers between devices, swap(): return lax.all_to_all(chunks, axis, split_axis=0, concat_axis=0, tiled=True)  10.1 us
    ppermute x1, starting transfers between devices, local(): lax.ppermute(w_after[:half], RING, down)  4.34 us
    all_to_all x2, waiting for transfers between devices, swap(): return lax.all_to_all(chunks, axis, split_axis=0, concat_axis=0, tiled=True)  3.73 us
  transfers between devices with their start and end apart: 6, of which 3 were waited for; matrix products, arithmetic and copies ran while one was open for 3% of the time, Pallas kernels for 6%

profile of v7, /device:TPU:1, one launch (start us, length us, event | category | flops | bytes accessed | tf_op | source)
XLA Modules:
  0.0 144.3 jit_solution(4631725328157311170)
XLA Ops:
  0.6 11.5 %collective-permute-start.1 = (bf16[224,1792]{1,0:T(8,128)(2,1)}, bf16[224,1792]{1,0:T(8,128)(2,1)S(1)}, u32[]{:S(2)}, u32[]{:S(2)}) collective-permute-start(bf16[224,1792]{1,0:T(8,128)(2,1)} %bitcast.30), channel_id=1, source_target_pairs={{0,112},{16,0},{32,16},{48,32},{64,48},{80,64},{96,80},{112,96},{1... | collective-permute-start | bytes 2408456 | tf_op jit(solution)/shard_map/weights/ppermute | solution.py:459
  12.1 1.9 %collective-permute-start = (bf16[224,1792]{1,0:T(8,128)(2,1)}, bf16[224,1792]{1,0:T(8,128)(2,1)S(1)}, u32[]{:S(2)}, u32[]{:S(2)}) collective-permute-start(bf16[224,1792]{1,0:T(8,128)(2,1)} %bitcast.31), channel_id=1, source_target_pairs={{0,16},{16,32},{32,48},{48,64},{64,80},{80,96},{96,112},{112,0},{1... | collective-permute-start | bytes 2408456 | tf_op jit(solution)/shard_map/weights/ppermute | solution.py:458
  14.1 0.7 copy-done.11
  14.8 0.1 copy.15
  14.9 0.1 reshape.15
  15.0 0.1 stack.31.refs_0_
  15.1 0.5 copy-done.5
  15.8 1.7 %routing.1 = (bf16[16,16,128]{2,1,0:T(8,128)(2,1)S(1)}, bf16[512,256]{1,0:T(8,128)(2,1)}) custom-call(s32[6]{0:T(128)S(1)} %stack.31.refs_0_, bf16[56,256]{1,0:T(8,128)(2,1)S(1)} %bitcast.25, s32[2,256]{1,0:T(2,128)S(1)} %bitcast.27, f32[2,256]{1,0:T(2,128)S(1)} %bitcast.28, f32[16,256]{1,0:T(8,128)S(1)} %bitcast.26), custom_call_target="tpu_custom_call" | custom-call | bytes 49152 | tf_op jit(solution)/shard_map/routing/pallas_call | solution.py:414
  17.4 20.1 %all_to_all.35.refs_0_ = bf16[16,16,128]{2,1,0:T(8,128)(2,1)S(1)} all-to-all(bf16[16,16,128]{2,1,0:T(8,128)(2,1)S(1)} %get-tuple-element.21), channel_id=1, replica_groups=mesh['y'=4,'zh'=2,'zl'=4,'expert'=16] {'expert'}, dimensions={0} | all-to-all | bytes 131072 | tf_op jit(solution)/shard_map/dispatch/all_to_all | solution.py:427
  37.5 1.0 dispatch.1
  38.5 5.1 %all-to-all-start.1 = ((bf16[32,64,128]{2,1,0:T(8,128)(2,1)}), bf16[32,64,128]{2,1,0:T(8,128)(2,1)S(1)}, u32[]{:S(2)}, u32[]{:S(2)}) async-start(bf16[32,64,128]{2,1,0:T(8,128)(2,1)} %dispatch.1), calls=%async_computation.1 | async-start | bytes 1048576 | tf_op jit(solution)/shard_map/dispatch/all_to_all | solution.py:427
  43.7 0.8 slice.9
  44.5 4.3 %collective-permute-start.2 = (bf16[112,1792]{1,0:T(8,128)(2,1)}, bf16[112,1792]{1,0:T(8,128)(2,1)S(1)}, u32[]{:S(2)}, u32[]{:S(2)}) collective-permute-start(bf16[112,1792]{1,0:T(8,128)(2,1)} %slice.9), channel_id=1, source_target_pairs={{0,112},{16,0},{32,16},{48,32},{64,48},{80,64},{96,80},{112,96},{1... | collective-permute-start | bytes 1204232 | tf_op jit(solution)/shard_map/dispatch/ppermute | solution.py:479
  48.9 1.9 %collective-permute-start.3 = (bf16[112,1792]{1,0:T(8,128)(2,1)S(1)}, bf16[112,1792]{1,0:T(8,128)(2,1)S(1)}, u32[]{:S(2)}, u32[]{:S(2)}) collective-permute-start(bf16[112,1792]{1,0:T(8,128)(2,1)S(1)} %slice.10), channel_id=1, source_target_pairs={{0,16},{16,32},{32,48},{48,64},{64,80},{80,96},{96,112},{112,0},{1... | collective-permute-start | bytes 1204232 | tf_op jit(solution)/shard_map/dispatch/ppermute | solution.py:480
  50.8 0.8 slice_bitcast_fusion
  51.6 1.0 tile.11
  52.6 1.5 %copy.16.refs_1_ = f32[1792,128]{1,0:T(8,128)S(1)} copy(f32[1792,128]{0,1:T(8,128)} %bitcast.29) | data formatting | bytes 1835008 | tf_op jit(solution)/shard_map/projection/tile | solution.py:486
  54.2 0.6 copy-done.12
  54.9 3.7 %all-to-all-done.1.refs_0_.refs_1_ = bf16[32,64,128]{2,1,0:T(8,128)(2,1)S(1)} async-done(((bf16[32,64,128]{2,1,0:T(8,128)(2,1)}), bf16[32,64,128]{2,1,0:T(8,128)(2,1)S(1)}, u32[]{:S(2)}, u32[]{:S(2)}) %all-to-all-start.1) | async-done | bytes 524320 | tf_op jit(solution)/shard_map/dispatch/all_to_all | solution.py:427
  58.6 1.4 projection.1
  60.0 5.0 %all-to-all-start.2 = ((bf16[8,16,224]{2,1,0:T(8,128)(2,1)}), bf16[8,16,224]{2,1,0:T(8,128)(2,1)S(1)}, u32[]{:S(2)}, u32[]{:S(2)}) async-start(bf16[8,16,224]{2,1,0:T(8,128)(2,1)} %get-tuple-element.30), calls=%async_computation.2 | async-start | bytes 131072 | tf_op jit(solution)/shard_map/projection/all_to_all | solution.py:427
  65.0 0.7 collective-permute-done.2.refs_6_.refs_12_
  65.7 2.0 %collective-permute-done.3.refs_7_.refs_13_ = bf16[112,1792]{1,0:T(8,128)(2,1)S(1)} collective-permute-done((bf16[112,1792]{1,0:T(8,128)(2,1)S(1)}, bf16[112,1792]{1,0:T(8,128)(2,1)S(1)}, u32[]{:S(2)}, u32[]{:S(2)}) %collective-permute-start.3) | collective-permute-done | bytes 401440 | tf_op jit(solution)/shard_map/dispatch/ppermute | solution.py:480
  67.7 5.0 %first_layer.1 = (bf16[4,128,224]{2,1,0:T(8,128)(2,1)S(1)}, f32[4,128,224]{2,1,0:T(8,128)}, bf16[128,1792]{1,0:T(8,128)(2,1)}, f32[16,128]{1,0:T(8,128)}, f32[32,128]{1,0:T(8,128)}) custom-call(s32[6]{0:T(128)S(1)} %stack.31.refs_0_, bf16[32,64,128]{2,1,0:T(8,128)(2,1)S(1)} %all-to-all-done.1.refs_0_.refs_1_, f32[3,4,1792]{2,1,0:T(4,128)} %bitcast.36, ...), custom_call_target="tpu_custom_call" | custom-call | flops 411041792 | bytes 4280320 | tf_op jit(solution)/shard_map/first_layer/pallas_call | solution.py:414
  72.8 0.7 predict.2
  73.5 15.9 %all_to_all.36.refs_0_ = f32[8,16,128]{2,1,0:T(8,128)S(1)} all-to-all(f32[8,16,128]{2,1,0:T(8,128)S(1)} %predict.2), channel_id=1, replica_groups=mesh['y'=4,'zh'=2,'zl'=4,'expert'=16] {'y','zh'}, dimensions={0} | all-to-all | bytes 131072 | tf_op jit(solution)/shard_map/predict/all_to_all | solution.py:427
  89.4 16.7 %all_to_all.37.refs_1_ = bf16[16,16,128]{2,1,0:T(8,128)(2,1)S(1)} all-to-all(bf16[16,16,128]{2,1,0:T(8,128)(2,1)S(1)} %predict.3), channel_id=1, replica_groups=mesh['y'=4,'zh'=2,'zl'=4,'expert'=16] {'expert'}, dimensions={0} | all-to-all | bytes 131072 | tf_op jit(solution)/shard_map/predict/all_to_all | solution.py:427
  106.0 4.0 %backward.2 = bf16[32,64,128]{2,1,0:T(8,128)(2,1)S(1)} custom-call(s32[6]{0:T(128)S(1)} %stack.31.refs_0_, bf16[16,16,128]{2,1,0:T(8,128)(2,1)S(1)} %all_to_all.37.refs_1_, f32[16,128]{1,0:T(8,128)} %get-tuple-element.31.refs_2_, f32[32,128]{1,0:T(8,128)} %get-tuple-element.32.refs_3_, bf16[8,16,224]{2,1,0:T(8,128)(2,1)} %copy-done.3, ...), custom_call_target="tpu_custom_call" | custom-call | flops 411041792 | bytes 4820992 | tf_op jit(solution)/shard_map/backward/pallas_call | solution.py:414
  110.1 18.3 %all_to_all.38.refs_0_ = bf16[32,64,128]{2,1,0:T(8,128)(2,1)S(1)} all-to-all(bf16[32,64,128]{2,1,0:T(8,128)(2,1)S(1)} %backward.2), channel_id=1, replica_groups=mesh['y'=4,'zh'=2,'zl'=4,'expert'=16] {'y','zh','zl'}, dimensions={0} | all-to-all | bytes 1048576 | tf_op jit(solution)/shard_map/backward/all_to_all | solution.py:427
  128.4 0.2 backward.3
  128.7 14.2 %all_to_all.39.refs_2_ = bf16[16,16,128]{2,1,0:T(8,128)(2,1)S(1)} all-to-all(bf16[16,16,128]{2,1,0:T(8,128)(2,1)S(1)} %backward.3), channel_id=1, replica_groups=mesh['y'=4,'zh'=2,'zl'=4,'expert'=16] {'expert'}, dimensions={0} | all-to-all | bytes 131072 | tf_op jit(solution)/shard_map/backward/all_to_all | solution.py:427
  142.9 1.4 finish.1
  (37 shorter events, 0.4 us)
Async XLA Ops:
  0.6 36.9 %collective-permute-start.1 = (bf16[224,1792]{1,0:T(8,128)(2,1)}, bf16[224,1792]{1,0:T(8,128)(2,1)S(1)}, u32[]{:S(2)}, u32[]{:S(2)}) collective-permute-start(bf16[224,1792]{1,0:T(8,128)(2,1)} %bitcast.30), channel_id=1, source_target_pairs={{0,112},{16,0},{32,16},{48,32},{64,48},{80,64},{96,80},{112,96},{1... | collective-permute-start | bytes 2408456 | tf_op jit(solution)/shard_map/weights/ppermute | solution.py:459
  12.1 25.4 %collective-permute-start = (bf16[224,1792]{1,0:T(8,128)(2,1)}, bf16[224,1792]{1,0:T(8,128)(2,1)S(1)}, u32[]{:S(2)}, u32[]{:S(2)}) collective-permute-start(bf16[224,1792]{1,0:T(8,128)(2,1)} %bitcast.31), channel_id=1, source_target_pairs={{0,16},{16,32},{32,48},{48,64},{64,80},{80,96},{96,112},{112,0},{1... | collective-permute-start | bytes 2408456 | tf_op jit(solution)/shard_map/weights/ppermute | solution.py:458
  14.1 0.7 copy-start.11
  14.9 0.8 copy-start.5
  15.0 0.7 copy-start.6
  15.1 0.7 copy-start.8
  15.1 0.7 copy-start.7
  37.5 6.2 %copy-start.9 = (bf16[224,1792]{1,0:T(8,128)(2,1)}, bf16[224,1792]{1,0:T(8,128)(2,1)S(1)}, u32[]{:S(2)}) copy-start(bf16[224,1792]{1,0:T(8,128)(2,1)S(1)} %collective-permute-done.1.refs_5_.refs_11_) | copy-start | bytes 2408452
  37.5 6.2 %copy-start.10 = (bf16[224,1792]{1,0:T(8,128)(2,1)}, bf16[224,1792]{1,0:T(8,128)(2,1)S(1)}, u32[]{:S(2)}) copy-start(bf16[224,1792]{1,0:T(8,128)(2,1)S(1)} %collective-permute-done.refs_4_.refs_10_) | copy-start | bytes 2408452
  38.5 20.1 %all-to-all-start.1 = ((bf16[32,64,128]{2,1,0:T(8,128)(2,1)}), bf16[32,64,128]{2,1,0:T(8,128)(2,1)S(1)}, u32[]{:S(2)}, u32[]{:S(2)}) async-start(bf16[32,64,128]{2,1,0:T(8,128)(2,1)} %dispatch.1), calls=%async_computation.1 | async-start | bytes 1048576 | tf_op jit(solution)/shard_map/dispatch/all_to_all | solution.py:427
  44.5 21.2 %collective-permute-start.2 = (bf16[112,1792]{1,0:T(8,128)(2,1)}, bf16[112,1792]{1,0:T(8,128)(2,1)S(1)}, u32[]{:S(2)}, u32[]{:S(2)}) collective-permute-start(bf16[112,1792]{1,0:T(8,128)(2,1)} %slice.9), channel_id=1, source_target_pairs={{0,112},{16,0},{32,16},{48,32},{64,48},{80,64},{96,80},{112,96},{1... | collective-permute-start | bytes 1204232 | tf_op jit(solution)/shard_map/dispatch/ppermute | solution.py:479
  48.9 18.9 %collective-permute-start.3 = (bf16[112,1792]{1,0:T(8,128)(2,1)S(1)}, bf16[112,1792]{1,0:T(8,128)(2,1)S(1)}, u32[]{:S(2)}, u32[]{:S(2)}) collective-permute-start(bf16[112,1792]{1,0:T(8,128)(2,1)S(1)} %slice.10), channel_id=1, source_target_pairs={{0,16},{16,32},{32,48},{48,64},{64,80},{80,96},{96,112},{112,0},{1... | collective-permute-start | bytes 1204232 | tf_op jit(solution)/shard_map/dispatch/ppermute | solution.py:480
  50.8 0.8 copy-start.13
  52.6 1.6 %copy-start.14 = (s32[2]{0:T(128)S(1)}, s32[2]{0:T(128)}, u32[]{:S(2)}) copy-start(s32[2]{0:T(128)} %param.21) | copy-start | bytes 28
  52.6 6.0 %copy-start.2 = (bf16[1,224,1792]{2,1,0:T(8,128)(2,1)S(1)}, bf16[1,224,1792]{2,1,0:T(8,128)(2,1)}, u32[]{:S(2)}) copy-start(bf16[1,224,1792]{2,1,0:T(8,128)(2,1)} %param.16) | copy-start | bytes 2408452
  54.1 0.7 copy-start.12
  60.0 12.7 %all-to-all-start.2 = ((bf16[8,16,224]{2,1,0:T(8,128)(2,1)}), bf16[8,16,224]{2,1,0:T(8,128)(2,1)S(1)}, u32[]{:S(2)}, u32[]{:S(2)}) async-start(bf16[8,16,224]{2,1,0:T(8,128)(2,1)} %get-tuple-element.30), calls=%async_computation.2 | async-start | bytes 131072 | tf_op jit(solution)/shard_map/projection/all_to_all | solution.py:427
  65.7 7.0 %copy-start = (bf16[112,1792]{1,0:T(8,128)(2,1)}, bf16[112,1792]{1,0:T(8,128)(2,1)S(1)}, u32[]{:S(2)}) copy-start(bf16[112,1792]{1,0:T(8,128)(2,1)S(1)} %collective-permute-done.2.refs_6_.refs_12_) | copy-start | bytes 1204228
  67.7 5.0 %copy-start.1 = (bf16[112,1792]{1,0:T(8,128)(2,1)}, bf16[112,1792]{1,0:T(8,128)(2,1)S(1)}, u32[]{:S(2)}) copy-start(bf16[112,1792]{1,0:T(8,128)(2,1)S(1)} %collective-permute-done.3.refs_7_.refs_13_) | copy-start | bytes 1204228
  72.7 0.7 copy-start.3
  128.4 14.5 %copy-start.4 = (bf16[512,256]{1,0:T(8,128)(2,1)S(1)}, bf16[512,256]{1,0:T(8,128)(2,1)}, u32[]{:S(2)}) copy-start(bf16[512,256]{1,0:T(8,128)(2,1)} %get-tuple-element.35.refs_3_) | copy-start | bytes 786436

commit v8 on v7

--- a/solution.py
+++ b/solution.py
@@ -136,7 +136,11 @@
 
 def parcel_kernel(arrived_ref, head_ref, parcel_ref):
     row = iota((8, LANES), 0)
-    head = head_ref[...].astype(f32)
+    spread = jnp.concatenate([head_ref[...].astype(f32)] * 8, axis=0).T
+    own = iota((FEAT, LANES), 1) // C_OUT == iota((FEAT, LANES), 0) % 8
+    spread = jnp.where(own, spread, 0.0).astype(bf16)
+    fold = iota((8, FEAT), 1) // 8 + 1 == iota((8, FEAT), 0)
+    head = dot(fold.astype(bf16), spread)
     for q in range(4):
         tiles = lane_blocks([arrived_ref[4 * q + b].astype(f32) for b in range(4)])
         tail = jnp.where(row == 0, tiles[3][8:], head)
@@ -467,10 +471,9 @@
             store=(1,),
         )
     with jax.named_scope("dispatch"):
-        head_flat = jnp.pad(head.T.reshape(FEAT // 8, LANES), ((1, 0), (0, 0)))
-        sent, head_flat = lax.optimization_barrier((sent, head_flat))
         arrived = swap(sent, "expert")
-        arrived, w_before, w_after = lax.optimization_barrier((arrived, w_before, w_after))
+        (parcel,) = call(parcel_kernel, [], [arrived, head], [((SHARDS, PACK, LANES), bf16)])
+        parcel, w_before, w_after = lax.optimization_barrier((parcel, w_before, w_after))
         half = HID // 2
         weights = [
             w_in,
@@ -479,7 +482,6 @@
             lax.ppermute(w_after[:half], RING, down),
             lax.ppermute(w_before[half:], RING, up),
         ]
-        (parcel,) = call(parcel_kernel, [], [arrived, head_flat], [((SHARDS, PACK, LANES), bf16)])
         gathered, levels = lax.optimization_barrier((swap(parcel, FSDP), levels))
 
     with jax.named_scope("projection"):

time: 145 us -> 144 us (level)
  no operation moved by 1% of the time
where the time goes in v8:
time: 144 us; the launch traced here: 143 us
  blocking collectives  85 us (59%)
  starting transfers between devices  29.8 us (21%)
  Pallas kernels  15.4 us (11%)
  waiting for transfers between devices  6.4 us (4%)
  local copies, waits for them, and re-layouts  5.59 us (4%)
    all_to_all x5, blocking collectives, swap(): return lax.all_to_all(chunks, axis, split_axis=0, concat_axis=0, tiled=True)  85 us
    pallas_call x9, Pallas kernels, call(): pl.pallas_call(body, out_shape=out_shape, in_specs=[smem] * len(scalars)...  15.4 us
    ppermute x1, starting transfers between devices, local(): w_after = lax.ppermute(w_in, RING, down)  11.5 us
    all_to_all x2, starting transfers between devices, swap(): return lax.all_to_all(chunks, axis, split_axis=0, concat_axis=0, tiled=True)  10.2 us
    ppermute x1, starting transfers between devices, local(): lax.ppermute(w_after[:half], RING, down)  4.34 us
    all_to_all x2, waiting for transfers between devices, swap(): return lax.all_to_all(chunks, axis, split_axis=0, concat_axis=0, tiled=True)  3.71 us
  transfers between devices with their start and end apart: 6, of which 3 were waited for; matrix products, arithmetic and copies ran while one was open for 3% of the time, Pallas kernels for 6%

profile of v8, /device:TPU:1, one launch (start us, length us, event | category | flops | bytes accessed | tf_op | source)
XLA Modules:
  0.0 143.3 jit_solution(11736182544521303396)
XLA Ops:
  0.6 11.5 %collective-permute-start.1 = (bf16[224,1792]{1,0:T(8,128)(2,1)}, bf16[224,1792]{1,0:T(8,128)(2,1)S(1)}, u32[]{:S(2)}, u32[]{:S(2)}) collective-permute-start(bf16[224,1792]{1,0:T(8,128)(2,1)} %bitcast.29), channel_id=1, source_target_pairs={{0,112},{16,0},{32,16},{48,32},{64,48},{80,64},{96,80},{112,96},{1... | collective-permute-start | bytes 2408456 | tf_op jit(solution)/shard_map/weights/ppermute | solution.py:463
  12.1 1.9 %collective-permute-start = (bf16[224,1792]{1,0:T(8,128)(2,1)}, bf16[224,1792]{1,0:T(8,128)(2,1)S(1)}, u32[]{:S(2)}, u32[]{:S(2)}) collective-permute-start(bf16[224,1792]{1,0:T(8,128)(2,1)} %bitcast.30), channel_id=1, source_target_pairs={{0,16},{16,32},{32,48},{48,64},{64,80},{80,96},{96,112},{112,0},{1... | collective-permute-start | bytes 2408456 | tf_op jit(solution)/shard_map/weights/ppermute | solution.py:462
  14.1 0.1 stack.31.refs_0_
  14.2 0.6 copy-done.5
  14.8 0.1 copy-done.9
  14.9 0.0 copy-done.8
  14.9 1.7 %routing.1 = (bf16[16,16,128]{2,1,0:T(8,128)(2,1)S(1)}, bf16[512,256]{1,0:T(8,128)(2,1)}) custom-call(s32[6]{0:T(128)S(1)} %stack.31.refs_0_, bf16[56,256]{1,0:T(8,128)(2,1)S(1)} %bitcast.24, s32[2,256]{1,0:T(2,128)S(1)} %bitcast.26, f32[2,256]{1,0:T(2,128)S(1)} %bitcast.27, f32[16,256]{1,0:T(8,128)S(1)} %bitcast.25), custom_call_target="tpu_custom_call" | custom-call | bytes 49152 | tf_op jit(solution)/shard_map/routing/pallas_call | solution.py:418
  16.6 20.1 %all_to_all.35.refs_0_ = bf16[16,16,128]{2,1,0:T(8,128)(2,1)S(1)} all-to-all(bf16[16,16,128]{2,1,0:T(8,128)(2,1)S(1)} %get-tuple-element.18), channel_id=1, replica_groups=mesh['y'=4,'zh'=2,'zl'=4,'expert'=16] {'expert'}, dimensions={0} | all-to-all | bytes 131072 | tf_op jit(solution)/shard_map/dispatch/all_to_all | solution.py:431
  36.6 1.0 dispatch.1
  37.7 5.1 %all-to-all-start.1 = ((bf16[32,64,128]{2,1,0:T(8,128)(2,1)}), bf16[32,64,128]{2,1,0:T(8,128)(2,1)S(1)}, u32[]{:S(2)}, u32[]{:S(2)}) async-start(bf16[32,64,128]{2,1,0:T(8,128)(2,1)} %dispatch.1), calls=%async_computation.1 | async-start | bytes 1048576 | tf_op jit(solution)/shard_map/dispatch/all_to_all | solution.py:431
  42.9 0.8 slice.9
  43.7 4.3 %collective-permute-start.2 = (bf16[112,1792]{1,0:T(8,128)(2,1)}, bf16[112,1792]{1,0:T(8,128)(2,1)S(1)}, u32[]{:S(2)}, u32[]{:S(2)}) collective-permute-start(bf16[112,1792]{1,0:T(8,128)(2,1)} %slice.9), channel_id=1, source_target_pairs={{0,112},{16,0},{32,16},{48,32},{64,48},{80,64},{96,80},{112,96},{1... | collective-permute-start | bytes 1204232 | tf_op jit(solution)/shard_map/dispatch/ppermute | solution.py:482
  48.0 1.9 %collective-permute-start.3 = (bf16[112,1792]{1,0:T(8,128)(2,1)S(1)}, bf16[112,1792]{1,0:T(8,128)(2,1)S(1)}, u32[]{:S(2)}, u32[]{:S(2)}) collective-permute-start(bf16[112,1792]{1,0:T(8,128)(2,1)S(1)} %slice.10), channel_id=1, source_target_pairs={{0,16},{16,32},{32,48},{48,64},{64,80},{80,96},{96,112},{112,0},{1... | collective-permute-start | bytes 1204232 | tf_op jit(solution)/shard_map/dispatch/ppermute | solution.py:483
  50.0 0.8 slice_bitcast_fusion
  50.8 1.0 tile.11
  51.8 1.5 %copy.14.refs_1_ = f32[1792,128]{1,0:T(8,128)S(1)} copy(f32[1792,128]{0,1:T(8,128)} %bitcast.28) | data formatting | bytes 1835008 | tf_op jit(solution)/shard_map/projection/tile | solution.py:488
  53.4 0.6 copy-done.12
  54.0 0.1 pad_maximum_fusion.refs_1_
  54.1 3.7 %all-to-all-done.1.refs_0_.refs_1_ = bf16[32,64,128]{2,1,0:T(8,128)(2,1)S(1)} async-done(((bf16[32,64,128]{2,1,0:T(8,128)(2,1)}), bf16[32,64,128]{2,1,0:T(8,128)(2,1)S(1)}, u32[]{:S(2)}, u32[]{:S(2)}) %all-to-all-start.1) | async-done | bytes 524320 | tf_op jit(solution)/shard_map/dispatch/all_to_all | solution.py:431
  57.8 1.4 projection.1
  59.2 5.0 %all-to-all-start.2 = ((bf16[8,16,224]{2,1,0:T(8,128)(2,1)}), bf16[8,16,224]{2,1,0:T(8,128)(2,1)S(1)}, u32[]{:S(2)}, u32[]{:S(2)}) async-start(bf16[8,16,224]{2,1,0:T(8,128)(2,1)} %get-tuple-element.26), calls=%async_computation.2 | async-start | bytes 131072 | tf_op jit(solution)/shard_map/projection/all_to_all | solution.py:431
  64.2 0.7 collective-permute-done.2.refs_6_.refs_12_
  64.9 2.0 %collective-permute-done.3.refs_7_.refs_13_ = bf16[112,1792]{1,0:T(8,128)(2,1)S(1)} collective-permute-done((bf16[112,1792]{1,0:T(8,128)(2,1)S(1)}, bf16[112,1792]{1,0:T(8,128)(2,1)S(1)}, u32[]{:S(2)}, u32[]{:S(2)}) %collective-permute-start.3) | collective-permute-done | bytes 401440 | tf_op jit(solution)/shard_map/dispatch/ppermute | solution.py:483
  66.9 5.0 %first_layer.1 = (bf16[4,128,224]{2,1,0:T(8,128)(2,1)S(1)}, f32[4,128,224]{2,1,0:T(8,128)}, bf16[128,1792]{1,0:T(8,128)(2,1)}, f32[16,128]{1,0:T(8,128)}, f32[32,128]{1,0:T(8,128)}) custom-call(s32[6]{0:T(128)S(1)} %stack.31.refs_0_, bf16[32,64,128]{2,1,0:T(8,128)(2,1)S(1)} %all-to-all-done.1.refs_0_.refs_1_, f32[3,4,1792]{2,1,0:T(4,128)} %bitcast.35, ...), custom_call_target="tpu_custom_call" | custom-call | flops 411041792 | bytes 4280320 | tf_op jit(solution)/shard_map/first_layer/pallas_call | solution.py:418
  71.9 0.7 predict.2
  72.6 15.9 %all_to_all.36.refs_0_ = f32[8,16,128]{2,1,0:T(8,128)S(1)} all-to-all(f32[8,16,128]{2,1,0:T(8,128)S(1)} %predict.2), channel_id=1, replica_groups=mesh['y'=4,'zh'=2,'zl'=4,'expert'=16] {'y','zh'}, dimensions={0} | all-to-all | bytes 131072 | tf_op jit(solution)/shard_map/predict/all_to_all | solution.py:431
  88.5 16.5 %all_to_all.37.refs_1_ = bf16[16,16,128]{2,1,0:T(8,128)(2,1)S(1)} all-to-all(bf16[16,16,128]{2,1,0:T(8,128)(2,1)S(1)} %predict.3), channel_id=1, replica_groups=mesh['y'=4,'zh'=2,'zl'=4,'expert'=16] {'expert'}, dimensions={0} | all-to-all | bytes 131072 | tf_op jit(solution)/shard_map/predict/all_to_all | solution.py:431
  105.0 4.0 %backward.2 = bf16[32,64,128]{2,1,0:T(8,128)(2,1)S(1)} custom-call(s32[6]{0:T(128)S(1)} %stack.31.refs_0_, bf16[16,16,128]{2,1,0:T(8,128)(2,1)S(1)} %all_to_all.37.refs_1_, f32[16,128]{1,0:T(8,128)} %get-tuple-element.27.refs_2_, f32[32,128]{1,0:T(8,128)} %get-tuple-element.28.refs_3_, bf16[8,16,224]{2,1,0:T(8,128)(2,1)} %copy-done.3, ...), custom_call_target="tpu_custom_call" | custom-call | flops 411041792 | bytes 4820992 | tf_op jit(solution)/shard_map/backward/pallas_call | solution.py:418
  109.1 18.3 %all_to_all.38.refs_0_ = bf16[32,64,128]{2,1,0:T(8,128)(2,1)S(1)} all-to-all(bf16[32,64,128]{2,1,0:T(8,128)(2,1)S(1)} %backward.2), channel_id=1, replica_groups=mesh['y'=4,'zh'=2,'zl'=4,'expert'=16] {'y','zh','zl'}, dimensions={0} | all-to-all | bytes 1048576 | tf_op jit(solution)/shard_map/backward/all_to_all | solution.py:431
  127.4 0.2 backward.3
  127.6 14.2 %all_to_all.39.refs_2_ = bf16[16,16,128]{2,1,0:T(8,128)(2,1)S(1)} all-to-all(bf16[16,16,128]{2,1,0:T(8,128)(2,1)S(1)} %backward.3), channel_id=1, replica_groups=mesh['y'=4,'zh'=2,'zl'=4,'expert'=16] {'expert'}, dimensions={0} | all-to-all | bytes 131072 | tf_op jit(solution)/shard_map/backward/all_to_all | solution.py:431
  141.9 1.4 finish.1
  (34 shorter events, 0.2 us)
Async XLA Ops:
  0.6 37.0 %collective-permute-start.1 = (bf16[224,1792]{1,0:T(8,128)(2,1)}, bf16[224,1792]{1,0:T(8,128)(2,1)S(1)}, u32[]{:S(2)}, u32[]{:S(2)}) collective-permute-start(bf16[224,1792]{1,0:T(8,128)(2,1)} %bitcast.29), channel_id=1, source_target_pairs={{0,112},{16,0},{32,16},{48,32},{64,48},{80,64},{96,80},{112,96},{1... | collective-permute-start | bytes 2408456 | tf_op jit(solution)/shard_map/weights/ppermute | solution.py:463
  12.1 25.5 %collective-permute-start = (bf16[224,1792]{1,0:T(8,128)(2,1)}, bf16[224,1792]{1,0:T(8,128)(2,1)S(1)}, u32[]{:S(2)}, u32[]{:S(2)}) collective-permute-start(bf16[224,1792]{1,0:T(8,128)(2,1)} %bitcast.30), channel_id=1, source_target_pairs={{0,16},{16,32},{32,48},{48,64},{64,80},{80,96},{96,112},{112,0},{1... | collective-permute-start | bytes 2408456 | tf_op jit(solution)/shard_map/weights/ppermute | solution.py:462
  14.1 0.7 copy-start.5
  14.1 0.7 copy-start.6
  14.2 0.7 copy-start.9
  14.2 0.7 copy-start.8
  16.6 20.1 %copy-start.7 = (bf16[16,56]{1,0:T(8,128)(2,1)S(1)}, bf16[16,56]{1,0:T(8,128)(2,1)}, u32[]{:S(2)}) copy-start(bf16[16,56]{1,0:T(8,128)(2,1)} %refs_1_.1) | copy-start | bytes 5380
  37.7 5.2 %copy-start.10 = (bf16[224,1792]{1,0:T(8,128)(2,1)}, bf16[224,1792]{1,0:T(8,128)(2,1)S(1)}, u32[]{:S(2)}) copy-start(bf16[224,1792]{1,0:T(8,128)(2,1)S(1)} %collective-permute-done.1.refs_5_.refs_11_) | copy-start | bytes 2408452
  37.7 5.2 %copy-start.11 = (bf16[224,1792]{1,0:T(8,128)(2,1)}, bf16[224,1792]{1,0:T(8,128)(2,1)S(1)}, u32[]{:S(2)}) copy-start(bf16[224,1792]{1,0:T(8,128)(2,1)S(1)} %collective-permute-done.refs_4_.refs_10_) | copy-start | bytes 2408452
  37.7 20.1 %all-to-all-start.1 = ((bf16[32,64,128]{2,1,0:T(8,128)(2,1)}), bf16[32,64,128]{2,1,0:T(8,128)(2,1)S(1)}, u32[]{:S(2)}, u32[]{:S(2)}) async-start(bf16[32,64,128]{2,1,0:T(8,128)(2,1)} %dispatch.1), calls=%async_computation.1 | async-start | bytes 1048576 | tf_op jit(solution)/shard_map/dispatch/all_to_all | solution.py:431
  43.7 21.2 %collective-permute-start.2 = (bf16[112,1792]{1,0:T(8,128)(2,1)}, bf16[112,1792]{1,0:T(8,128)(2,1)S(1)}, u32[]{:S(2)}, u32[]{:S(2)}) collective-permute-start(bf16[112,1792]{1,0:T(8,128)(2,1)} %slice.9), channel_id=1, source_target_pairs={{0,112},{16,0},{32,16},{48,32},{64,48},{80,64},{96,80},{112,96},{1... | collective-permute-start | bytes 1204232 | tf_op jit(solution)/shard_map/dispatch/ppermute | solution.py:482
  48.0 18.9 %collective-permute-start.3 = (bf16[112,1792]{1,0:T(8,128)(2,1)S(1)}, bf16[112,1792]{1,0:T(8,128)(2,1)S(1)}, u32[]{:S(2)}, u32[]{:S(2)}) collective-permute-start(bf16[112,1792]{1,0:T(8,128)(2,1)S(1)} %slice.10), channel_id=1, source_target_pairs={{0,16},{16,32},{32,48},{48,64},{64,80},{80,96},{96,112},{112,0},{1... | collective-permute-start | bytes 1204232 | tf_op jit(solution)/shard_map/dispatch/ppermute | solution.py:483
  49.9 0.8 copy-start.13
  51.8 1.6 %copy-start.14 = (s32[2]{0:T(128)S(1)}, s32[2]{0:T(128)}, u32[]{:S(2)}) copy-start(s32[2]{0:T(128)} %param.21) | copy-start | bytes 28
  51.8 6.0 %copy-start.2 = (bf16[1,224,1792]{2,1,0:T(8,128)(2,1)S(1)}, bf16[1,224,1792]{2,1,0:T(8,128)(2,1)}, u32[]{:S(2)}) copy-start(bf16[1,224,1792]{2,1,0:T(8,128)(2,1)} %param.16) | copy-start | bytes 2408452
  53.3 0.7 copy-start.12
  59.2 12.7 %all-to-all-start.2 = ((bf16[8,16,224]{2,1,0:T(8,128)(2,1)}), bf16[8,16,224]{2,1,0:T(8,128)(2,1)S(1)}, u32[]{:S(2)}, u32[]{:S(2)}) async-start(bf16[8,16,224]{2,1,0:T(8,128)(2,1)} %get-tuple-element.26), calls=%async_computation.2 | async-start | bytes 131072 | tf_op jit(solution)/shard_map/projection/all_to_all | solution.py:431
  64.9 7.0 %copy-start = (bf16[112,1792]{1,0:T(8,128)(2,1)}, bf16[112,1792]{1,0:T(8,128)(2,1)S(1)}, u32[]{:S(2)}) copy-start(bf16[112,1792]{1,0:T(8,128)(2,1)S(1)} %collective-permute-done.2.refs_6_.refs_12_) | copy-start | bytes 1204228
  66.9 5.0 %copy-start.1 = (bf16[112,1792]{1,0:T(8,128)(2,1)}, bf16[112,1792]{1,0:T(8,128)(2,1)S(1)}, u32[]{:S(2)}) copy-start(bf16[112,1792]{1,0:T(8,128)(2,1)S(1)} %collective-permute-done.3.refs_7_.refs_13_) | copy-start | bytes 1204228
  71.9 0.7 copy-start.3
  127.4 14.5 %copy-start.4 = (bf16[512,256]{1,0:T(8,128)(2,1)S(1)}, bf16[512,256]{1,0:T(8,128)(2,1)}, u32[]{:S(2)}) copy-start(bf16[512,256]{1,0:T(8,128)(2,1)} %get-tuple-element.31.refs_3_) | copy-start | bytes 786436
